TPU v7x, 512 devices: a whole 4x8x8 slice. The times are simulated.
512 devices in a mesh: dp: 64 (over x, y, core), mp: 8 (over z).
Axes of the slice: x: 4, y: 8, z: 8, core: 2. Of those that a mesh axis runs over, the one named last changes fastest.
Arguments:
- activations: bfloat16 [32768, 4096], P('dp', 'mp'), may hold values from -30 to 30
- cotangent: bfloat16 [32768, 1024], P('dp', 'mp'), may hold values from -0.125 to 0.125
- block_start: int32 [8, 80], replicated, may hold values from 0 to 127, as said below
- block_owner: int32 [8, 80], replicated, may hold values from 0 to 63, as said below
- first_moment: float32 [8, 64, 4, 4096], P('mp', 'dp'), may hold values from -6 to 6
- block_second: float32 [8, 64, 2], P('mp', 'dp'), may hold values from 0.25 to 4
- master_rows: float32 [8, 64, 4, 4096], P('mp', 'dp'), may hold values from -6 to 6
Outputs:
- new_weight: bfloat16 [1024, 4096], P('mp')
- moment_new: float32 [8, 64, 4, 4096], P('mp', 'dp')
- second_new: float32 [8, 64, 2], P('mp', 'dp')
- master_new: float32 [8, 64, 4, 4096], P('mp', 'dp')
Inputs may be any that keep to these rules, and one draw needn't show every extreme that they name: `block_start`: for each head, the first neuron of each of its 80 blocks, increasing from 0; every block holds one or more of the head's 128 neurons. `block_owner`: for each head, a quarter of the ranks own 4 neurons in two blocks, a quarter own 2 neurons in one block, the rest own 1 neuron in one block.
All inputs are finite; a program needn't handle non-finite values.
Results may differ from a plain program's by a relative error of at most 0.001.
Values may be sent and summed in bfloat16 or wider, within the bound.
No kernel may reach another device: no remote copies, remote signals or barrier semaphores. Data moves between devices by JAX's collectives and lax.ppermute only.
A program may use at most 64 MiB of HBM per device.

v0:
```python
from functools import partial

import jax
import jax.numpy as jnp
from jax import lax
from jax.sharding import PartitionSpec as P

HD = 128


beta_one = 0.9
beta_two = 0.95
learn_rate = 0.05
decay_rate = 0.1
epsilon = 1e-08
fix_one = 1.0 - 0.9**10
fix_two = 1.0 - 0.95**10


def block_tables(starts, owners, owner_count, capacity):
    neuron_ids = jnp.arange(HD, dtype=jnp.int32)
    count_blocks = starts.shape[0]
    block_ids = jnp.sum((starts[None, :] <= neuron_ids[:, None]).astype(jnp.int32), axis=1) - 1
    onehot = block_ids[:, None] == jnp.arange(count_blocks, dtype=jnp.int32)[None, :]
    row_owner = jnp.sum(jnp.where(onehot, owners[None, :], 0), axis=1)
    earlier = (row_owner[:, None] == row_owner[None, :]) & (
        neuron_ids[None, :] < neuron_ids[:, None]
    )
    row_slot = jnp.sum(earlier.astype(jnp.int32), axis=1)
    before_blocks = (owners[:, None] == owners[None, :]) & (starts[None, :] < starts[:, None])
    block_rank = jnp.sum(before_blocks.astype(jnp.int32), axis=1)
    row_rank = jnp.sum(jnp.where(onehot, block_rank[None, :], 0), axis=1)
    target = row_owner * capacity + row_slot
    picker = jnp.arange(owner_count * capacity, dtype=jnp.int32)[:, None] == target[None, :]
    filled = jnp.any(picker, axis=1)
    slot_rank = jnp.sum(jnp.where(picker, row_rank[None, :], 0), axis=1)
    assign = filled[:, None] & (slot_rank[:, None] == jnp.arange(2, dtype=jnp.int32)[None, :])
    assign = jnp.transpose(assign.reshape(owner_count, capacity, 2), (0, 2, 1))
    return (
        picker.astype(jnp.float32),
        assign.astype(jnp.float32),
        filled.reshape(owner_count, capacity),
    )


def adam_rows(grad_slots, moment, second, master, assign, filled):
    width = grad_slots.shape[-1]
    row_squares = jnp.sum(grad_slots * grad_slots, axis=-1)
    block_sums = jnp.einsum(
        "...qc,...c->...q", assign, row_squares, precision=lax.Precision.HIGHEST
    )
    block_counts = jnp.sum(assign, axis=-1) * width
    block_used = block_counts > 0.0
    block_mean = block_sums / jnp.maximum(block_counts, 1.0)
    second_new = jnp.where(block_used, beta_two * second + (1.0 - beta_two) * block_mean, 0.0)
    slot_second = jnp.einsum(
        "...qc,...q->...c", assign, second_new, precision=lax.Precision.HIGHEST
    )
    slot_second = jnp.where(filled, slot_second, 1.0)
    moment_new = jnp.where(
        filled[..., None], beta_one * moment + (1.0 - beta_one) * grad_slots, 0.0
    )
    update = moment_new / fix_one / (jnp.sqrt(slot_second / fix_two)[..., None] + epsilon)
    master_new = jnp.where(
        filled[..., None], master - learn_rate * (update + decay_rate * master), 0.0
    )
    return (moment_new, second_new, master_new)


def slot_rows(picker):
    neuron_ids = jnp.arange(picker.shape[1], dtype=jnp.int32)
    chosen = picker > 0.5
    index = jnp.sum(jnp.where(chosen, neuron_ids[None, :], 0), axis=1)
    return (index, jnp.any(chosen, axis=1))


def take_rows(matrix, pickers):
    index, full = jax.vmap(slot_rows)(pickers)
    rows = jnp.take_along_axis(matrix, index[:, :, None], axis=1)
    rows = jnp.where(full[:, :, None], rows, 0.0)
    return jnp.transpose(rows, (1, 0, 2))


def body(activations, cotangent, block_start, block_owner, first_moment, block_second, master_rows):
    owner_count = lax.axis_size("dp")
    capacity = first_moment.shape[2]
    width = first_moment.shape[3]
    head_here = lax.axis_index("mp")
    owner_here = lax.axis_index("dp")
    make = partial(block_tables, owner_count=owner_count, capacity=capacity)
    pickers, assigns, filleds = jax.vmap(make)(block_start, block_owner)
    picker_here = lax.dynamic_index_in_dim(pickers, head_here, 0, keepdims=False)
    used_inputs = lax.all_gather(activations, "mp", axis=1, tiled=True)
    used_pickers = picker_here[None]
    heads_used = used_pickers.shape[0]
    tokens_here = cotangent.shape[0]
    cot_heads = cotangent.reshape(tokens_here, heads_used, HD)
    gradient = jnp.einsum("thd,tf->hdf", cot_heads, used_inputs, preferred_element_type=jnp.float32)
    padded = take_rows(gradient, used_pickers)
    owned = lax.psum_scatter(padded, "dp", scatter_dimension=0, tiled=True)
    grad_slots = owned.reshape(capacity, width)
    assign_head = lax.dynamic_index_in_dim(assigns, head_here, 0, keepdims=False)
    assign_here = lax.dynamic_index_in_dim(assign_head, owner_here, 0, keepdims=False)
    filled_head = lax.dynamic_index_in_dim(filleds, head_here, 0, keepdims=False)
    filled_here = lax.dynamic_index_in_dim(filled_head, owner_here, 0, keepdims=False)
    moment_new, second_new, master_new = adam_rows(
        grad_slots,
        first_moment[0, 0],
        block_second[0, 0],
        master_rows[0, 0],
        assign_here,
        filled_here,
    )
    low_rows = master_new.astype(jnp.bfloat16)
    every_rows = lax.all_gather(low_rows, "dp", axis=0, tiled=True)
    new_weight = jnp.einsum(
        "cr,cf->rf",
        picker_here.astype(jnp.bfloat16),
        every_rows,
        preferred_element_type=jnp.float32,
    ).astype(jnp.bfloat16)
    return (new_weight, moment_new[None, None], second_new[None, None], master_new[None, None])


def solution(mesh):
    return jax.shard_map(
        body,
        mesh=mesh,
        in_specs=(
            P("dp", "mp"),
            P("dp", "mp"),
            P(),
            P(),
            P("mp", "dp", None, None),
            P("mp", "dp", None),
            P("mp", "dp", None, None),
        ),
        out_specs=(
            P("mp", None),
            P("mp", "dp", None, None),
            P("mp", "dp", None),
            P("mp", "dp", None, None),
        ),
        check_vma=False,
    )
```

profile of v0, /device:TPU:1, one launch (start us, length us, event | category | flops | bytes accessed | tf_op | source)
XLA Modules:
  0.0 387.8 jit_solution(8752980169996369695)
XLA Ops:
  7.2 0.0 all-gather.4.cloned.1.call-start
  7.2 0.7 all-gather.4.cloned.1.call-update
  7.9 0.0 all-reduce.3.cloned.1.call-start
  8.0 0.8 convert_reduce_fusion.2
  8.8 1.2 convert_reduce_fusion.1
  10.0 0.9 select_reduce_fusion.1
  11.0 0.4 convert_reduce_fusion
  11.4 0.4 iota_compare_fusion
  11.7 0.1 fusion.10
  11.8 0.1 select_reduce_fusion.3
  12.0 61.9 %all-gather.4.cloned.1.call-done = bf16[512,4096]{1,0:T(8,128)(2,1)} async-done(((bf16[512,512]{1,0:T(8,128)(2,1)}), bf16[512,4096]{1,0:T(8,128)(2,1)}) %all-gather.4.cloned.1.call-update) | async-done | bytes 4194320 | tf_op jit(solution)/shard_map/all_gather | solution.py:93
  73.9 2.9 fusion.28
  76.8 3.9 gather_fusion
  80.7 5.0 %fusion = f32[256,1,4096]{2,0,1:T(8,128)} fusion(f32[256,4096]{1,0:T(8,128)} %gather_fusion, pred[256]{0:T(512)(128)(4,1)S(1)} %compare_and_fusion, pred[256]{0:T(512)(128)(4,1)S(1)} %fusion.10), kind=kLoop, calls=%fused_computation.3 | loop fusion | flops 2097152 | bytes 8389120 | tf_op jit(solution)/shard_map/jit(_where)/select_n | solution.py:80
  85.8 0.0 all-gather.6.cloned.1.call-start
  85.8 0.2 copy.19
  86.0 0.5 copy.20
  86.5 0.4 select_reduce_fusion
  86.9 0.1 copy.21
  87.1 0.5 copy.22
  87.5 0.2 dynamic-slice_reduce_fusion
  87.7 1.3 dynamic-slice.11
  89.7 0.1 fusion.19
  89.8 199.3 %all-reduce.3.cloned.1.call-done = f32[256,1,4096]{2,0,1:T(8,128)} async-done(((f32[256,1,4096]{2,0,1:T(8,128)}), f32[256,1,4096]{2,0,1:T(8,128)}) %all-reduce.3.cloned.1.call-update) | async-done | bytes 4194320
  289.1 1.1 multiply_reduce_fusion
  290.1 0.1 fusion.8
  290.2 0.1 fusion.4
  290.4 1.6 fusion.18
  292.1 1.7 subtract_select_fusion
  293.7 83.5 %all-gather.6.cloned.1.call-done = bf16[64,4,4096]{2,1,0:T(4,128)(2,1)} async-done(((bf16[1,4,4096]{2,1,0:T(4,128)(2,1)}), bf16[64,4,4096]{2,1,0:T(4,128)(2,1)}) %all-gather.6.cloned.1.call-update) | async-done | bytes 2097168 | tf_op jit(solution)/shard_map/all_gather | solution.py:115
  377.3 2.5 reshape.237
  379.8 1.5 convolution_convert_fusion
  (20 shorter events, 0.1 us)
Async XLA Ops:
  7.2 66.7 %copy-start = (bf16[512,128]{1,0:T(8,128)(2,1)S(1)}, bf16[512,128]{1,0:T(8,128)(2,1)}, u32[]{:S(2)}) copy-start(bf16[512,128]{1,0:T(8,128)(2,1)} %param.8) | copy-start | bytes 393220
  7.2 66.7 %all-gather.4.cloned.1.call-start = ((), (), s32[]{:S(2)}) async-start(), calls=%async_computation | async-start | bytes 4718592 | tf_op jit(solution)/shard_map/all_gather | solution.py:93
  7.9 281.1 %all-reduce.3.cloned.1.call-start = ((), (), s32[]{:S(2)}) async-start(), calls=%async_computation.2 | async-start | bytes 8388608
  85.7 204.4 %copy-start.3 = (f32[1,1,2]{2,1,0:T(1,128)S(1)}, f32[1,1,2]{2,1,0:T(1,128)}, u32[]{:S(2)}) copy-start(f32[1,1,2]{2,1,0:T(1,128)} %param.12) | copy-start | bytes 28
  85.7 204.6 %copy-start.1 = (f32[1,1,4,4096]{3,2,1,0:T(4,128)S(1)}, f32[1,1,4,4096]{3,2,1,0:T(4,128)}, u32[]{:S(2)}) copy-start(f32[1,1,4,4096]{3,2,1,0:T(4,128)} %param.11) | copy-start | bytes 196612
  85.7 204.7 %copy-start.2 = (f32[1,1,4,4096]{3,2,1,0:T(4,128)S(1)}, f32[1,1,4,4096]{3,2,1,0:T(4,128)}, u32[]{:S(2)}) copy-start(f32[1,1,4,4096]{3,2,1,0:T(4,128)} %param.13) | copy-start | bytes 196612
  85.8 291.5 %all-gather.6.cloned.1.call-start = ((), (), s32[]{:S(2)}) async-start(), calls=%async_computation.1 | async-start | bytes 2129920 | tf_op jit(solution)/shard_map/all_gather | solution.py:115
  290.2 91.0 %copy-start.4 = (f32[2]{0:T(128)}, f32[2]{0:T(128)S(1)}, u32[]{:S(2)}) copy-start(f32[2]{0:T(128)S(1)} %fusion.8) | copy-start | bytes 28
Sparse Core Ops, SparseCore 0:
  10.1 63.7 all-gather.3
  85.9 203.1 all-reduce.2
  293.5 83.6 all-gather.5
where the time goes:
time: 388 us
  waiting for transfers between devices  345 us (89%)
  between operations  14.6 us (4%)
  other arithmetic  13.9 us (4%)
  local copies, waits for them, and re-layouts  9.16 us (2%)
  matrix products  4.64 us (1%)
    unnamed x4, waiting for transfers between devices  200 us
    all_gather x1, waiting for transfers between devices, body(): every_rows = lax.all_gather(low_rows, 'dp', axis=0, tiled=True)  83.5 us
    all_gather x1, waiting for transfers between devices, body(): used_inputs = lax.all_gather(activations, 'mp', axis=1, tiled=True)  61.9 us
  transfers between devices with their start and end apart: 3, of which 3 were waited for; matrix products, arithmetic and copies ran while one was open for 2% of the time, Pallas kernels for 0%

commit v1 on v0

v1 whole, which is shorter than its diff:
```python
from functools import partial

import jax
import jax.numpy as jnp
from jax import lax
from jax.sharding import Mesh, PartitionSpec as P

HD = 128
GRID = (4, 8, 2)


beta_one = 0.9
beta_two = 0.95
learn_rate = 0.05
decay_rate = 0.1
epsilon = 1e-08
fix_one = 1.0 - 0.9**10
fix_two = 1.0 - 0.95**10


def block_tables(starts, owners, capacity):
    neuron_ids = jnp.arange(HD, dtype=jnp.int32)
    count_blocks = starts.shape[0]
    block_ids = jnp.sum((starts[None, :] <= neuron_ids[:, None]).astype(jnp.int32), axis=1) - 1
    onehot = block_ids[:, None] == jnp.arange(count_blocks, dtype=jnp.int32)[None, :]
    row_owner = jnp.sum(jnp.where(onehot, owners[None, :], 0), axis=1)
    earlier = (row_owner[:, None] == row_owner[None, :]) & (
        neuron_ids[None, :] < neuron_ids[:, None]
    )
    row_slot = jnp.sum(earlier.astype(jnp.int32), axis=1)
    before_blocks = (owners[:, None] == owners[None, :]) & (starts[None, :] < starts[:, None])
    block_rank = jnp.sum(before_blocks.astype(jnp.int32), axis=1)
    row_rank = jnp.sum(jnp.where(onehot, block_rank[None, :], 0), axis=1)
    return row_owner * capacity + row_slot, row_rank


def adam_rows(grad_slots, moment, second, master, assign, filled):
    width = grad_slots.shape[-1]
    row_squares = jnp.sum(grad_slots * grad_slots, axis=-1)
    block_sums = jnp.sum(assign * row_squares[None, :], axis=-1)
    block_counts = jnp.sum(assign, axis=-1) * width
    block_used = block_counts > 0.0
    block_mean = block_sums / jnp.maximum(block_counts, 1.0)
    second_new = jnp.where(block_used, beta_two * second + (1.0 - beta_two) * block_mean, 0.0)
    slot_second = jnp.sum(assign * second_new[:, None], axis=0)
    slot_second = jnp.where(filled, slot_second, 1.0)
    moment_new = jnp.where(
        filled[..., None], beta_one * moment + (1.0 - beta_one) * grad_slots, 0.0
    )
    update = moment_new / fix_one / (jnp.sqrt(slot_second / fix_two)[..., None] + epsilon)
    master_new = jnp.where(
        filled[..., None], master - learn_rate * (update + decay_rate * master), 0.0
    )
    return (moment_new, second_new, master_new)


SWAP = [(0, 1), (1, 0)]


def body(activations, cotangent, block_start, block_owner, first_moment, block_second, master_rows):
    nx, ny, nc = GRID
    heads, capacity, width = block_start.shape[0], first_moment.shape[2], first_moment.shape[3]
    chips, slots = nx * ny, nx * ny * nc * capacity
    core, head_here = lax.axis_index("c"), lax.axis_index("z")
    owner_here = (lax.axis_index("x") * ny + lax.axis_index("y")) * nc + core
    half = activations.shape[1] // nc

    cot_here = lax.all_gather(cotangent, "z", axis=0)
    act_here = lax.dynamic_slice_in_dim(activations, core * half, half, 1)
    act_give = lax.dynamic_slice_in_dim(activations, (1 - core) * half, half, 1)
    act_other = lax.ppermute(act_give, "c", SWAP)
    cot_other = lax.ppermute(cot_here, "c", SWAP)

    target, row_rank = jax.vmap(partial(block_tables, capacity=capacity))(block_start, block_owner)
    picker = jnp.arange(slots, dtype=jnp.int32)[None, :, None] == target[:, None, :]
    pick = picker.astype(jnp.bfloat16)

    def part(cot, act):
        wide = jnp.einsum("htn,hsn->hts", cot, pick, preferred_element_type=jnp.float32)
        wide = wide.astype(jnp.bfloat16)
        return jnp.einsum("hts,tf->hsf", wide, act, preferred_element_type=jnp.float32)

    padded = part(cot_here, act_here) + part(cot_other, act_other)
    padded = padded.reshape(heads, chips, nc * capacity, half)
    send = jnp.transpose(padded * 0.5, (1, 0, 2, 3)).astype(jnp.float16)
    send = send.reshape(chips * heads, nc * capacity, half)
    got = lax.all_to_all(send, ("x", "y", "z"), 0, 0, tiled=True)
    got = got.reshape(chips, heads, nc * capacity, half).astype(jnp.float32)
    summed = jnp.sum(got, axis=0) * 2.0

    keep = lax.dynamic_slice_in_dim(summed, core * capacity, capacity, 1)
    give = lax.dynamic_slice_in_dim(summed, (1 - core) * capacity, capacity, 1)
    take = lax.ppermute(give, "c", SWAP)
    first = jnp.where(core == 0, keep, take)
    later = jnp.where(core == 0, take, keep)
    grad_slots = jnp.stack([first, later], axis=1)
    grad_slots = jnp.transpose(grad_slots, (2, 0, 1, 3)).reshape(capacity, width)

    target_here = lax.dynamic_index_in_dim(target, head_here, 0, keepdims=False)
    rank_here = lax.dynamic_index_in_dim(row_rank, head_here, 0, keepdims=False)
    slot_ids = owner_here * capacity + jnp.arange(capacity, dtype=jnp.int32)
    mine = slot_ids[:, None] == target_here[None, :]
    filled_here = jnp.any(mine, axis=1)
    slot_rank = jnp.sum(jnp.where(mine, rank_here[None, :], 0), axis=1)
    assign_here = filled_here[None, :] & (
        slot_rank[None, :] == jnp.arange(2, dtype=jnp.int32)[:, None]
    )
    moment_new, second_new, master_new = adam_rows(
        grad_slots,
        first_moment[0, 0],
        block_second[0, 0],
        master_rows[0, 0],
        assign_here.astype(jnp.float32),
        filled_here,
    )

    rows = master_new.astype(jnp.bfloat16)
    rows = lax.all_to_all(jnp.broadcast_to(rows[None], (ny,) + rows.shape), "y", 0, 0, tiled=True)
    rows = lax.all_to_all(jnp.broadcast_to(rows[None], (nx,) + rows.shape), "x", 0, 0, tiled=True)
    rows = rows.reshape(chips * capacity, width)
    rows_other = lax.ppermute(rows, "c", SWAP)
    pick_here = lax.dynamic_index_in_dim(pick, head_here, 0, keepdims=False)
    pick_here = pick_here.reshape(chips, nc, capacity, HD)
    pick_own = lax.dynamic_index_in_dim(pick_here, core, 1, keepdims=False)
    pick_off = lax.dynamic_index_in_dim(pick_here, 1 - core, 1, keepdims=False)
    place = partial(jnp.einsum, "sr,sf->rf", preferred_element_type=jnp.float32)
    new_weight = place(pick_own.reshape(-1, HD), rows) + place(pick_off.reshape(-1, HD), rows_other)
    return (
        new_weight.astype(jnp.bfloat16),
        moment_new[None, None],
        second_new[None, None],
        master_new[None, None],
    )


def solution(mesh):
    dp = ("x", "y", "c")
    fine = Mesh(mesh.devices.reshape(GRID + (-1,)), dp + ("z",))
    return jax.shard_map(
        body,
        mesh=fine,
        in_specs=(
            P(dp, "z"),
            P(dp, "z"),
            P(),
            P(),
            P("z", dp, None, None),
            P("z", dp, None),
            P("z", dp, None, None),
        ),
        out_specs=(
            P("z", None),
            P("z", dp, None, None),
            P("z", dp, None),
            P("z", dp, None, None),
        ),
        check_vma=False,
    )
```

time: 388 us -> 172 us (0.44)
  waiting for transfers between devices: 345 us -> 79.6 us
  starting transfers between devices: 0.12 us -> 43.4 us
  blocking collectives: 0 us -> 15.1 us
  other arithmetic: 13.9 us -> 5.85 us
  local copies, waits for them, and re-layouts: 9.16 us -> 4.86 us
    unnamed x4 -> x1, waiting for transfers between devices: 200 us -> 0.68 us
    all_gather x2 -> x1, waiting for transfers between devices: 145 us -> 34.2 us  [body(): cot_here = lax.all_gather(cotangent, 'z', axis=0)]
    all_to_all x0 -> x2, waiting for transfers between devices: none -> 43 us  [the longest x1 29.9 us: body(): got = lax.all_to_all(send, ('x', 'y', 'z'), 0, 0, tiled=True)]
    ppermute x0 -> x4, starting transfers between devices: none -> 23.9 us  [the longest x1 8.79 us: body(): act_other = lax.ppermute(act_give, 'c', SWAP)]
    all_to_all x0 -> x2, starting transfers between devices: none -> 19.5 us  [the longest x1 15.9 us: body(): got = lax.all_to_all(send, ('x', 'y', 'z'), 0, 0, tiled=True)]
    all_to_all x0 -> x1, blocking collectives: none -> 15.1 us  [body(): lax.all_to_all(jnp.broadcast_to(rows[None], (ny,) + rows.shape), 'y', 0,...]
    select_n x2, other arithmetic: 5.05 us -> 0.53 us  [adam_rows(): jnp.where(block_used, beta_two * second + (1.0 - beta_two) * block_mean,...]
  transfers between devices with their start and end apart: 3 -> 7, of which waited for: 3 -> 5; matrix products, arithmetic and copies ran while one was open for 2% -> 5% of each run, Pallas kernels for 0% -> 0%
where the time goes in v1:
time: 172 us; the launch traced here: 171 us
  waiting for transfers between devices  79.6 us (46%)
  starting transfers between devices  43.4 us (25%)
  blocking collectives  15.1 us (9%)
  between operations  14.3 us (8%)
  matrix products  7.88 us (5%)
  other arithmetic  5.85 us (3%)
  local copies, waits for them, and re-layouts  4.86 us (3%)
    all_gather x1, waiting for transfers between devices, body(): cot_here = lax.all_gather(cotangent, 'z', axis=0)  34.2 us
    all_to_all x1, waiting for transfers between devices, body(): got = lax.all_to_all(send, ('x', 'y', 'z'), 0, 0, tiled=True)  29.9 us
    all_to_all x1, starting transfers between devices, body(): got = lax.all_to_all(send, ('x', 'y', 'z'), 0, 0, tiled=True)  15.9 us
    all_to_all x1, blocking collectives, body(): lax.all_to_all(jnp.broadcast_to(rows[None], (ny,) + rows.shape), 'y', 0,...  15.1 us
    all_to_all x1, waiting for transfers between devices, body(): lax.all_to_all(jnp.broadcast_to(rows[None], (nx,) + rows.shape), 'x', 0,...  13.1 us
    ppermute x1, starting transfers between devices, body(): act_other = lax.ppermute(act_give, 'c', SWAP)  8.79 us
    ppermute x1, starting transfers between devices, body(): cot_other = lax.ppermute(cot_here, 'c', SWAP)  7.13 us
    dot_general x2, matrix products, part(): jnp.einsum('hts,tf->hsf', wide, act, preferred_element_type=jnp.float32)  5.95 us
  transfers between devices with their start and end apart: 7, of which 5 were waited for; matrix products, arithmetic and copies ran while one was open for 5% of the time, Pallas kernels for 0%

profile of v1, /device:TPU:1, one launch (start us, length us, event | category | flops | bytes accessed | tf_op | source)
XLA Modules:
  0.0 171.0 jit_solution(13092869378073305392)
XLA Ops:
  7.2 0.7 all-gather.3.cloned.1.call-update
  7.9 0.3 copy-done
  8.2 8.8 %collective-permute-start.1 = (bf16[512,256]{1,0:T(8,128)(2,1)S(1)}, bf16[512,256]{1,0:T(8,128)(2,1)S(1)}, u32[]{:S(2)}, u32[]{:S(2)}) collective-permute-start(bf16[512,256]{1,0:T(8,128)(2,1)S(1)} %constant_dynamic-slice_fusion.2), channel_id=1, source_target_pairs={{0,8},{8,0},{1,9},{9,1},{2,10},{10,2},{3,11},{11,3},{4,12},{12,4},... | collective-permute-start | bytes 786440 | tf_op jit(solution)/shard_map/ppermute | solution.py:71
  17.0 0.8 convert_reduce_fusion.3
  17.9 1.2 convert_reduce_fusion.2
  19.1 34.2 %all-gather.3.cloned.1.call-done = bf16[4096,128]{1,0:T(8,128)(2,1)} async-done(((bf16[512,128]{1,0:T(8,128)(2,1)}), bf16[4096,128]{1,0:T(8,128)(2,1)}) %all-gather.3.cloned.1.call-update) | async-done | bytes 1048592 | tf_op jit(solution)/shard_map/all_gather | solution.py:68
  53.2 7.1 %collective-permute-start = (bf16[8,512,128]{2,1,0:T(8,128)(2,1)}, bf16[8,512,128]{2,1,0:T(8,128)(2,1)}, u32[]{:S(2)}, u32[]{:S(2)}) collective-permute-start(bf16[8,512,128]{2,1,0:T(8,128)(2,1)} %bitcast.75), channel_id=1, source_target_pairs={{0,8},{8,0},{1,9},{9,1},{2,10},{10,2},{3,11},{11,3},{4,12},{12,4},... | collective-permute-start | bytes 3145736 | tf_op jit(solution)/shard_map/ppermute | solution.py:72
  60.4 0.9 select_reduce_fusion
  61.4 0.4 convert_reduce_fusion.1
  61.7 2.5 %fusion.3 = f32[8,256,256]{2,1,0:T(8,128)S(1)} fusion(bf16[8,512,128]{2,1,0:T(8,128)(2,1)} %bitcast.76, s32[8,128]{1,0:T(8,128)S(1)} %multiply_add_fusion, bf16[512,512]{1,0:T(8,128)(2,1)S(1)} %copy-done, s32[]{:T(128)S(6)} %select_n.94), kind=kOutput, calls=%fused_computation.5 | convolution fusion | flops 806617088 | bytes 3411972 | tf_op jit(solution)/shard_map/hts,tf->hsf/dot_general | solution.py:81
  64.2 3.5 %fusion.13 = f16[8,32,8,256]{3,2,1,0:T(8,128)(2,1)} fusion(f32[8,256,256]{2,1,0:T(8,128)S(1)} %fusion.3, bf16[8,512,128]{2,1,0:T(8,128)(2,1)} %collective-permute-done, s32[8,128]{1,0:T(8,128)S(1)} %multiply_add_fusion, bf16[512,256]{1,0:T(8,128)(2,1)S(1)} %collective-permute-done.1), kind=kOutput, calls=%fused_computation.12 | convolution fusion | flops 808189952 | bytes 4460544 | tf_op jit(solution)/shard_map/hts,tf->hsf/dot_general | solution.py:81
  67.7 2.4 %copy.18 = f16[8,32,8,256]{3,2,0,1:T(8,128)(2,1)} copy(f16[8,32,8,256]{3,2,1,0:T(8,128)(2,1)} %fusion.13) | data formatting | bytes 2097152 | tf_op jit(solution)/shard_map/convert_element_type | solution.py:85
  70.2 15.9 %all-to-all-start = ((f16[256,8,256]{2,1,0:T(8,128)(2,1)}), f16[256,8,256]{2,1,0:T(8,128)(2,1)S(1)}, u32[]{:S(2)}, u32[]{:S(2)}) async-start(f16[256,8,256]{2,1,0:T(8,128)(2,1)} %bitcast.12), calls=%async_computation | async-start | bytes 2097152 | tf_op jit(solution)/shard_map/all_to_all | solution.py:87
  86.1 0.2 fusion.28
  86.3 29.9 %all-to-all-done = f16[256,8,256]{2,1,0:T(8,128)(2,1)S(1)} async-done(((f16[256,8,256]{2,1,0:T(8,128)(2,1)}), f16[256,8,256]{2,1,0:T(8,128)(2,1)S(1)}, u32[]{:S(2)}, u32[]{:S(2)}) %all-to-all-start) | async-done | bytes 1048608 | tf_op jit(solution)/shard_map/all_to_all | solution.py:87
  116.2 0.2 convert_reduce_fusion
  116.4 3.5 %collective-permute-start.2 = (f32[8,4,256]{2,1,0:T(4,128)S(1)}, f32[8,4,256]{2,1,0:T(4,128)S(1)}, u32[]{:S(2)}, u32[]{:S(2)}) collective-permute-start(f32[8,4,256]{2,1,0:T(4,128)S(1)} %constant_dynamic-slice_fusion.1), channel_id=1, source_target_pairs={{0,8},{8,0},{1,9},{9,1},{2,10},{10,2},{3,11},{11,3},{4,12},{12,4},... | collective-permute-start | bytes 98312 | tf_op jit(solution)/shard_map/ppermute | solution.py:93
  120.0 0.2 compare_reduce_fusion
  120.2 0.7 collective-permute-done.2
  121.0 0.1 convert_reduce_fusion.4
  121.1 0.5 bitcast_select_fusion
  122.1 15.1 %all_to_all.15 = bf16[8,4,4096]{2,1,0:T(4,128)(2,1)S(1)} all-to-all(bf16[8,4,4096]{2,1,0:T(4,128)(2,1)S(1)} %broadcast_in_dim.110), channel_id=1, replica_groups=mesh['x'=4,'y'=8,'c'=2,'z'=8] {'y'}, dimensions={0} | all-to-all | bytes 524288 | tf_op jit(solution)/shard_map/all_to_all | solution.py:118
  137.2 1.5 broadcast_in_dim.111
  138.7 3.5 %all-to-all-start.2 = ((bf16[4,8,4,4096]{3,2,1,0:T(4,128)(2,1)}), bf16[4,8,4,4096]{3,2,1,0:T(4,128)(2,1)S(1)}, u32[]{:S(2)}, u32[]{:S(2)}) async-start(bf16[4,8,4,4096]{3,2,1,0:T(4,128)(2,1)} %broadcast_in_dim.111), calls=%async_computation.2 | async-start | bytes 2097152 | tf_op jit(solution)/shard_map/all_to_all | solution.py:119
  142.2 0.2 iota_compare_fusion
  142.5 13.1 %all-to-all-done.2 = bf16[4,8,4,4096]{3,2,1,0:T(4,128)(2,1)S(1)} async-done(((bf16[4,8,4,4096]{3,2,1,0:T(4,128)(2,1)}), bf16[4,8,4,4096]{3,2,1,0:T(4,128)(2,1)S(1)}, u32[]{:S(2)}, u32[]{:S(2)}) %all-to-all-start.2) | async-done | bytes 1048608 | tf_op jit(solution)/shard_map/all_to_all | solution.py:119
  155.7 0.3 reshape.230
  155.9 4.5 %collective-permute-start.3 = (bf16[128,4096]{1,0:T(8,128)(2,1)S(1)}, bf16[128,4096]{1,0:T(8,128)(2,1)S(1)}, u32[]{:S(2)}, u32[]{:S(2)}) collective-permute-start(bf16[128,4096]{1,0:T(8,128)(2,1)S(1)} %reshape.230), channel_id=1, source_target_pairs={{0,8},{8,0},{1,9},{9,1},{2,10},{10,2},{3,11},{11,3},{4,12},{12,4},... | collective-permute-start | bytes 3145736 | tf_op jit(solution)/shard_map/ppermute | solution.py:121
  160.4 0.8 subtract_select_fusion
  161.2 0.5 fusion.33
  161.7 1.0 collective-permute-done.3
  162.7 1.5 fusion
  (30 shorter events, 0.8 us)
Async XLA Ops:
  7.2 1.0 copy-start
  7.2 46.1 %all-gather.3.cloned.1.call-start = ((), (), s32[]{:S(2)}) async-start(), calls=%async_computation.3 | async-start | bytes 1179648 | tf_op jit(solution)/shard_map/all_gather | solution.py:68
  8.2 56.0 %collective-permute-start.1 = (bf16[512,256]{1,0:T(8,128)(2,1)S(1)}, bf16[512,256]{1,0:T(8,128)(2,1)S(1)}, u32[]{:S(2)}, u32[]{:S(2)}) collective-permute-start(bf16[512,256]{1,0:T(8,128)(2,1)S(1)} %constant_dynamic-slice_fusion.2), channel_id=1, source_target_pairs={{0,8},{8,0},{1,9},{9,1},{2,10},{10,2},{3,11},{11,3},{4,12},{12,4},... | collective-permute-start | bytes 786440 | tf_op jit(solution)/shard_map/ppermute | solution.py:71
  53.2 11.0 %collective-permute-start = (bf16[8,512,128]{2,1,0:T(8,128)(2,1)}, bf16[8,512,128]{2,1,0:T(8,128)(2,1)}, u32[]{:S(2)}, u32[]{:S(2)}) collective-permute-start(bf16[8,512,128]{2,1,0:T(8,128)(2,1)} %bitcast.75), channel_id=1, source_target_pairs={{0,8},{8,0},{1,9},{9,1},{2,10},{10,2},{3,11},{11,3},{4,12},{12,4},... | collective-permute-start | bytes 3145736 | tf_op jit(solution)/shard_map/ppermute | solution.py:72
  70.2 51.0 %copy-start.3 = (f32[1,1,2]{2,1,0:T(1,128)S(1)}, f32[1,1,2]{2,1,0:T(1,128)}, u32[]{:S(2)}) copy-start(f32[1,1,2]{2,1,0:T(1,128)} %param.12) | copy-start | bytes 28
  70.2 51.8 %copy-start.1 = (f32[1,1,4,4096]{3,2,1,0:T(4,128)S(1)}, f32[1,1,4,4096]{3,2,1,0:T(4,128)}, u32[]{:S(2)}) copy-start(f32[1,1,4,4096]{3,2,1,0:T(4,128)} %param.13) | copy-start | bytes 196612
  70.2 51.8 %copy-start.2 = (f32[1,1,4,4096]{3,2,1,0:T(4,128)S(1)}, f32[1,1,4,4096]{3,2,1,0:T(4,128)}, u32[]{:S(2)}) copy-start(f32[1,1,4,4096]{3,2,1,0:T(4,128)} %param.11) | copy-start | bytes 196612
  70.2 46.1 %all-to-all-start = ((f16[256,8,256]{2,1,0:T(8,128)(2,1)}), f16[256,8,256]{2,1,0:T(8,128)(2,1)S(1)}, u32[]{:S(2)}, u32[]{:S(2)}) async-start(f16[256,8,256]{2,1,0:T(8,128)(2,1)} %bitcast.12), calls=%async_computation | async-start | bytes 2097152 | tf_op jit(solution)/shard_map/all_to_all | solution.py:87
  116.4 4.4 %collective-permute-start.2 = (f32[8,4,256]{2,1,0:T(4,128)S(1)}, f32[8,4,256]{2,1,0:T(4,128)S(1)}, u32[]{:S(2)}, u32[]{:S(2)}) collective-permute-start(f32[8,4,256]{2,1,0:T(4,128)S(1)} %constant_dynamic-slice_fusion.1), channel_id=1, source_target_pairs={{0,8},{8,0},{1,9},{9,1},{2,10},{10,2},{3,11},{11,3},{4,12},{12,4},... | collective-permute-start | bytes 98312 | tf_op jit(solution)/shard_map/ppermute | solution.py:93
  138.7 17.0 %all-to-all-start.2 = ((bf16[4,8,4,4096]{3,2,1,0:T(4,128)(2,1)}), bf16[4,8,4,4096]{3,2,1,0:T(4,128)(2,1)S(1)}, u32[]{:S(2)}, u32[]{:S(2)}) async-start(bf16[4,8,4,4096]{3,2,1,0:T(4,128)(2,1)} %broadcast_in_dim.111), calls=%async_computation.2 | async-start | bytes 2097152 | tf_op jit(solution)/shard_map/all_to_all | solution.py:119
  155.9 6.8 %collective-permute-start.3 = (bf16[128,4096]{1,0:T(8,128)(2,1)S(1)}, bf16[128,4096]{1,0:T(8,128)(2,1)S(1)}, u32[]{:S(2)}, u32[]{:S(2)}) collective-permute-start(bf16[128,4096]{1,0:T(8,128)(2,1)S(1)} %reshape.230), channel_id=1, source_target_pairs={{0,8},{8,0},{1,9},{9,1},{2,10},{10,2},{3,11},{11,3},{4,12},{12,4},... | collective-permute-start | bytes 3145736 | tf_op jit(solution)/shard_map/ppermute | solution.py:121
Sparse Core Ops, SparseCore 0:
  10.1 43.0 all-gather.2

commit v2 on v1

v2 whole, which is shorter than its diff:
```python
from functools import partial

import jax
import jax.numpy as jnp
from jax import lax
from jax.experimental import pallas as pl
from jax.experimental.pallas import tpu as pltpu
from jax.sharding import Mesh, PartitionSpec as P

HD = 128
GRID = (4, 8, 2)
PAIR = 2
CUT = 4


beta_one = 0.9
beta_two = 0.95
learn_rate = 0.05
decay_rate = 0.1
epsilon = 1e-08
fix_one = 1.0 - 0.9**10
fix_two = 1.0 - 0.95**10


def block_tables(starts, owners, capacity):
    neuron_ids = jnp.arange(HD, dtype=jnp.int32)
    count_blocks = starts.shape[0]
    block_ids = jnp.sum((starts[None, :] <= neuron_ids[:, None]).astype(jnp.int32), axis=1) - 1
    onehot = block_ids[:, None] == jnp.arange(count_blocks, dtype=jnp.int32)[None, :]
    row_owner = jnp.sum(jnp.where(onehot, owners[None, :], 0), axis=1)
    earlier = (row_owner[:, None] == row_owner[None, :]) & (
        neuron_ids[None, :] < neuron_ids[:, None]
    )
    row_slot = jnp.sum(earlier.astype(jnp.int32), axis=1)
    before_blocks = (owners[:, None] == owners[None, :]) & (starts[None, :] < starts[:, None])
    block_rank = jnp.sum(before_blocks.astype(jnp.int32), axis=1)
    row_rank = jnp.sum(jnp.where(onehot, block_rank[None, :], 0), axis=1)
    return row_owner * capacity + row_slot, row_rank


def adam_rows(grad_slots, moment, second, master, assign, filled):
    width = grad_slots.shape[-1]
    row_squares = jnp.sum(grad_slots * grad_slots, axis=-1)
    block_sums = jnp.sum(assign * row_squares[None, :], axis=-1)
    block_counts = jnp.sum(assign, axis=-1) * width
    block_used = block_counts > 0.0
    block_mean = block_sums / jnp.maximum(block_counts, 1.0)
    second_new = jnp.where(block_used, beta_two * second + (1.0 - beta_two) * block_mean, 0.0)
    slot_second = jnp.sum(assign * second_new[:, None], axis=0)
    slot_second = jnp.where(filled, slot_second, 1.0)
    moment_new = jnp.where(
        filled[..., None], beta_one * moment + (1.0 - beta_one) * grad_slots, 0.0
    )
    update = moment_new / fix_one / (jnp.sqrt(slot_second / fix_two)[..., None] + epsilon)
    master_new = jnp.where(
        filled[..., None], master - learn_rate * (update + decay_rate * master), 0.0
    )
    return (moment_new, second_new, master_new)


SWAP = [(0, 1), (1, 0)]


def copies_to_all(block, axis):
    count = lax.axis_size(axis)
    return lax.all_to_all(jnp.broadcast_to(block[None], (count,) + block.shape), axis, 0, 0, tiled=True)


def gradient_kernel(target_ref, cot_here_ref, cot_other_ref, act_here_ref, act_other_ref, out_ref):
    tokens = (((0,), (0,)), ((), ()))
    grad = lax.dot_general(
        cot_here_ref[0], act_here_ref[...], tokens, preferred_element_type=jnp.float32
    ) + lax.dot_general(
        cot_other_ref[0], act_other_ref[...], tokens, preferred_element_type=jnp.float32
    )
    high = grad.astype(jnp.bfloat16)
    low = (grad - high.astype(jnp.float32)).astype(jnp.bfloat16)
    chips, rows, half = out_ref.shape[0], out_ref.shape[2] // 2, out_ref.shape[3]
    slot = lax.broadcasted_iota(jnp.int32, (chips * rows, HD), 0)
    pick = jnp.where(slot == target_ref[0], 0.5, 0.0).astype(jnp.bfloat16)
    padded = jnp.dot(pick, high, preferred_element_type=jnp.float32) + jnp.dot(
        pick, low, preferred_element_type=jnp.float32
    )
    parts = [padded[:, i * half : (i + 1) * half].reshape(chips, rows, half) for i in range(2)]
    out_ref[:, 0] = jnp.concatenate(parts, axis=1).astype(out_ref.dtype)


def padded_gradient(target, cot_here, cot_other, act_here, act_other, chips, rows):
    heads, tokens, _ = cot_here.shape
    features = act_here.shape[1]
    cot = pl.BlockSpec((1, tokens, HD), lambda h: (h, 0, 0))
    act = pl.BlockSpec((tokens, features), lambda h: (0, 0))
    shape = (chips, heads, 2 * rows, features // 2)
    return pl.pallas_call(
        gradient_kernel,
        grid=(heads,),
        in_specs=[pl.BlockSpec((1, 1, HD), lambda h: (h, 0, 0)), cot, cot, act, act],
        out_specs=pl.BlockSpec((chips, 1) + shape[2:], lambda h: (0, h, 0, 0)),
        out_shape=jax.ShapeDtypeStruct(shape, jnp.float32),
        compiler_params=pltpu.CompilerParams(vmem_limit_bytes=32 * 2**20),
    )(target[:, None, :], cot_here, cot_other, act_here, act_other)


def weight_kernel(target_ref, key_here_ref, key_other_ref, here_ref, other_ref, out_ref):
    want = target_ref[...] * CUT + pl.program_id(0)
    pick_here = jnp.where(want == key_here_ref[...], 1.0, 0.0).astype(jnp.bfloat16)
    pick_other = jnp.where(want == key_other_ref[...], 1.0, 0.0).astype(jnp.bfloat16)
    rows = jnp.dot(pick_here, here_ref[...], preferred_element_type=jnp.float32)
    rows += jnp.dot(pick_other, other_ref[...], preferred_element_type=jnp.float32)
    out_ref[...] = rows.astype(jnp.bfloat16)


def place_rows(target, key_here, key_other, here, other):
    count, piece = here.shape
    whole = lambda shape: pl.BlockSpec(shape, lambda j: (0, 0))
    return pl.pallas_call(
        weight_kernel,
        grid=(CUT,),
        in_specs=[whole((HD, 1)), whole((1, count)), whole((1, count))] + [whole((count, piece))] * 2,
        out_specs=pl.BlockSpec((HD, piece), lambda j: (0, j)),
        out_shape=jax.ShapeDtypeStruct((HD, CUT * piece), jnp.bfloat16),
        compiler_params=pltpu.CompilerParams(vmem_limit_bytes=32 * 2**20),
    )(target[:, None], key_here[None, :], key_other[None, :], here, other)


def body(activations, cotangent, block_start, block_owner, first_moment, block_second, master_rows):
    nx, ny, nc = GRID
    capacity, width = first_moment.shape[2], first_moment.shape[3]
    chips, rows = nx * ny, nc * capacity
    core, side, pair = lax.axis_index("c"), lax.axis_index("zl"), lax.axis_index("zh")
    pairs = lax.axis_size("zh")
    chip = lax.axis_index("x") * ny + lax.axis_index("y")
    owner_here = chip * nc + core
    features = activations.shape[1]

    act_pair = lax.ppermute(activations, "zl", SWAP)
    cot_here = copies_to_all(cotangent, "zh")
    own = core == side
    act_here = jnp.where(own, activations, act_pair)
    act_other = lax.ppermute(jnp.where(own, act_pair, activations), "c", SWAP)
    cot_other = lax.ppermute(cot_here, "c", SWAP)

    def of_side(table):
        return lax.dynamic_index_in_dim(table.reshape(pairs, PAIR, -1), side, 1, keepdims=False)

    target, row_rank = jax.vmap(partial(block_tables, capacity=capacity))(
        of_side(block_start), of_side(block_owner)
    )
    target_here = lax.dynamic_index_in_dim(target, pair, 0, keepdims=False)
    rank_here = lax.dynamic_index_in_dim(row_rank, pair, 0, keepdims=False)
    slot_ids = owner_here * capacity + jnp.arange(capacity, dtype=jnp.int32)
    mine = slot_ids[:, None] == target_here[None, :]
    filled_here = jnp.any(mine, axis=1)
    slot_rank = jnp.sum(jnp.where(mine, rank_here[None, :], 0), axis=1)
    assign_here = filled_here[None, :] & (
        slot_rank[None, :] == jnp.arange(2, dtype=jnp.int32)[:, None]
    )

    send = padded_gradient(target, cot_here, cot_other, act_here, act_other, chips, rows)
    send = send.astype(jnp.float16).reshape(nx, ny * pairs, 2 * rows, features // 2)
    got = lax.all_to_all(send, "x", 0, 0, tiled=True)
    send = jnp.sum(got.astype(jnp.float32), axis=0).astype(jnp.float16)
    got = lax.all_to_all(send, ("y", "zh"), 0, 0, tiled=True)
    got = got.reshape(ny, pairs, 2, nc, capacity, features // 2)
    summed = jnp.sum(got.astype(jnp.float32), axis=0) * 2.0

    keep = lax.dynamic_index_in_dim(summed, core, 2, keepdims=False)
    give = lax.dynamic_index_in_dim(summed, 1 - core, 2, keepdims=False)
    take = lax.ppermute(give, "c", SWAP)
    even = jnp.where(core == 0, keep, take)
    odd = jnp.where(core == 0, take, keep)
    grad_slots = jnp.stack([even, odd], axis=1)
    grad_slots = jnp.transpose(grad_slots, (3, 0, 1, 2, 4)).reshape(capacity, width)
    moment_new, second_new, master_new = adam_rows(
        grad_slots,
        first_moment[0, 0],
        block_second[0, 0],
        master_rows[0, 0],
        assign_here.astype(jnp.float32),
        filled_here,
    )

    low = master_new.astype(jnp.bfloat16).reshape(capacity * CUT, width // CUT)
    low = copies_to_all(copies_to_all(low, "y"), "x").reshape(-1, width // CUT)
    low_other = lax.ppermute(low, "c", SWAP)
    row = jnp.arange(low.shape[0], dtype=jnp.int32)
    from_chip, piece = row // (capacity * CUT), row % (capacity * CUT)
    key_here = (from_chip * nc + core) * capacity * CUT + piece
    key_other = (from_chip * nc + 1 - core) * capacity * CUT + piece
    new_weight = place_rows(target_here, key_here, key_other, low, low_other)
    return (new_weight, moment_new[None, None], second_new[None, None], master_new[None, None])


def solution(mesh):
    dp, mp = ("x", "y", "c"), ("zh", "zl")
    fine = Mesh(mesh.devices.reshape(GRID + (-1, PAIR)), dp + mp)
    return jax.shard_map(
        body,
        mesh=fine,
        in_specs=(
            P(dp, mp),
            P(dp, mp),
            P(),
            P(),
            P(mp, dp, None, None),
            P(mp, dp, None),
            P(mp, dp, None, None),
        ),
        out_specs=(
            P(mp, None),
            P(mp, dp, None, None),
            P(mp, dp, None),
            P(mp, dp, None, None),
        ),
        check_vma=False,
    )
```

time: 172 us -> 133 us (0.77)
  waiting for transfers between devices: 79.6 us -> 28.1 us
  blocking collectives: 15.1 us -> 48.5 us
  between operations: 14.3 us -> 0.92 us
  matrix products: 7.88 us -> 0 us
  Pallas kernels: 0 us -> 5.49 us
  starting transfers between devices: 43.4 us -> 41.1 us
    all_gather x1 -> x0, waiting for transfers between devices: 34.2 us -> none  [body(): cot_here = lax.all_gather(cotangent, 'z', axis=0)]
    all_to_all x1 -> x3, blocking collectives: 15.1 us -> 48.5 us  [the longest x2 30.5 us: copies_to_all(): lax.all_to_all(jnp.broadcast_to(block[None], (count,) + block.shape), axi...]
    all_to_all x2, waiting for transfers between devices: 43 us -> 24.5 us  [the longest x1 13.1 us: copies_to_all(): lax.all_to_all(jnp.broadcast_to(block[None], (count,) + block.shape), axi...]
    dot_general x4 -> x0, matrix products: 7.88 us -> none  [the longest x2 5.95 us: part(): jnp.einsum('hts,tf->hsf', wide, act, preferred_element_type=jnp.float32)]
    pallas_call x0 -> x2, Pallas kernels: none -> 5.49 us  [the longest x1 2.9 us: place_rows(): pl.pallas_call(weight_kernel, grid=(CUT,), in_specs=[whole((HD, 1)), whol...]
    convert_element_type x1, local copies, waits for them, and re-layouts: 2.44 us -> 0.15 us  [body(): summed = jnp.sum(got.astype(jnp.float32), axis=0) * 2.0]
    all_to_all x2, starting transfers between devices: 19.5 us -> 17.4 us  [the longest x1 9.12 us: copies_to_all(): lax.all_to_all(jnp.broadcast_to(block[None], (count,) + block.shape), axi...]
    ppermute x1, starting transfers between devices: 3.55 us -> 5.44 us  [body(): take = lax.ppermute(give, 'c', SWAP)]
  transfers between devices with their start and end apart: 7 -> 7, of which waited for: 5 -> 5; matrix products, arithmetic and copies ran while one was open for 5% -> 3% of each run, Pallas kernels for 0% -> 0%
where the time goes in v2:
time: 133 us; the launch traced here: 132 us
  blocking collectives  48.5 us (36%)
  starting transfers between devices  41.1 us (31%)
  waiting for transfers between devices  28.1 us (21%)
  Pallas kernels  5.49 us (4%)
  other arithmetic  4.47 us (3%)
  local copies, waits for them, and re-layouts  3.46 us (3%)
    all_to_all x2, blocking collectives, copies_to_all(): lax.all_to_all(jnp.broadcast_to(block[None], (count,) + block.shape), axi...  30.5 us
    all_to_all x1, blocking collectives, body(): got = lax.all_to_all(send, 'x', 0, 0, tiled=True)  18 us
    all_to_all x1, waiting for transfers between devices, copies_to_all(): lax.all_to_all(jnp.broadcast_to(block[None], (count,) + block.shape), axi...  13.1 us
    all_to_all x1, waiting for transfers between devices, body(): got = lax.all_to_all(send, ('y', 'zh'), 0, 0, tiled=True)  11.4 us
    all_to_all x1, starting transfers between devices, copies_to_all(): lax.all_to_all(jnp.broadcast_to(block[None], (count,) + block.shape), axi...  9.12 us
    all_to_all x1, starting transfers between devices, body(): got = lax.all_to_all(send, ('y', 'zh'), 0, 0, tiled=True)  8.31 us
    ppermute x1, starting transfers between devices, body(): take = lax.ppermute(give, 'c', SWAP)  5.44 us
    ppermute x1, starting transfers between devices, body(): cot_other = lax.ppermute(cot_here, 'c', SWAP)  5.36 us
  transfers between devices with their start and end apart: 7, of which 5 were waited for; matrix products, arithmetic and copies ran while one was open for 3% of the time, Pallas kernels for 0%

profile of v2, /device:TPU:1, one launch (start us, length us, event | category | flops | bytes accessed | tf_op | source)
XLA Modules:
  0.0 132.1 jit_solution(11740527976542706070)
XLA Ops:
  0.6 5.0 %collective-permute-start.1 = (bf16[512,512]{1,0:T(8,128)(2,1)}, bf16[512,512]{1,0:T(8,128)(2,1)S(1)}, u32[]{:S(2)}, u32[]{:S(2)}) collective-permute-start(bf16[512,512]{1,0:T(8,128)(2,1)} %param.7), channel_id=1, source_target_pairs={{0,1},{1,0},{2,3},{3,2},{4,5},{5,4},{6,7},{7,6},{8,9},{9,8},{10,11... | collective-permute-start | bytes 1572872 | tf_op jit(solution)/shard_map/ppermute | solution.py:136
  5.6 1.8 %broadcast_in_dim.123 = bf16[4,512,128]{2,1,0:T(8,128)(2,1)} broadcast(bf16[512,128]{1,0:T(8,128)(2,1)} %param.8), dimensions={1,2} | broadcast | bytes 655360 | tf_op jit(solution)/shard_map/broadcast_in_dim | solution.py:66
  7.4 9.1 %all-to-all-start = ((bf16[4,512,128]{2,1,0:T(8,128)(2,1)}), bf16[4,512,128]{2,1,0:T(8,128)(2,1)S(1)}, u32[]{:S(2)}, u32[]{:S(2)}) async-start(bf16[4,512,128]{2,1,0:T(8,128)(2,1)} %broadcast_in_dim.123), calls=%async_computation | async-start | bytes 1048576 | tf_op jit(solution)/shard_map/all_to_all | solution.py:66
  16.5 0.7 constant_dynamic-slice_fusion.2
  17.3 0.3 convert_reduce_fusion.2
  17.7 3.5 %collective-permute-start.2 = (bf16[512,512]{1,0:T(8,128)(2,1)S(1)}, bf16[512,512]{1,0:T(8,128)(2,1)S(1)}, u32[]{:S(2)}, u32[]{:S(2)}) collective-permute-start(bf16[512,512]{1,0:T(8,128)(2,1)S(1)} %get-tuple-element.12), channel_id=1, source_target_pairs={{0,8},{8,0},{1,9},{9,1},{2,10},{10,2},{3,11},{11,3},{4,12},{12,4},... | collective-permute-start | bytes 1572872 | tf_op jit(solution)/shard_map/ppermute | solution.py:140
  21.2 13.1 %all-to-all-done.cot_here_ref = bf16[4,512,128]{2,1,0:T(8,128)(2,1)S(1)} async-done(((bf16[4,512,128]{2,1,0:T(8,128)(2,1)}), bf16[4,512,128]{2,1,0:T(8,128)(2,1)S(1)}, u32[]{:S(2)}, u32[]{:S(2)}) %all-to-all-start) | async-done | bytes 524320 | tf_op jit(solution)/shard_map/all_to_all | solution.py:66
  34.3 5.4 %collective-permute-start = (bf16[4,512,128]{2,1,0:T(8,128)(2,1)S(1)}, bf16[4,512,128]{2,1,0:T(8,128)(2,1)S(1)}, u32[]{:S(2)}, u32[]{:S(2)}) collective-permute-start(bf16[4,512,128]{2,1,0:T(8,128)(2,1)S(1)} %all-to-all-done.cot_here_ref), channel_id=1, source_target_pairs={{0,8},{8,0},{1,9},{9,1},{2,10},{10,2},{3,11},{11,3},{4,12},{12,4},... | collective-permute-start | bytes 1572872 | tf_op jit(solution)/shard_map/ppermute | solution.py:141
  39.7 0.2 select_reduce_fusion
  39.8 0.2 convert_reduce_fusion.1
  40.1 1.1 collective-permute-done.cot_other_ref
  41.2 2.6 %shard_map.102 = f32[32,4,16,256]{3,2,1,0:T(8,128)S(1)} custom-call(s32[4,1,128]{2,1,0:T(1,128)S(1)} %bitcast.40, bf16[4,512,128]{2,1,0:T(8,128)(2,1)S(1)} %all-to-all-done.cot_here_ref, bf16[4,512,128]{2,1,0:T(8,128)(2,1)S(1)} %collective-permute-done.cot_other_ref, bf16[512,512]{1,0:T(8,128)(2,1)S(1)} %get-tuple-element.13.act_here_ref, ...), custom_call_target="tpu_custom_call" | custom-call | tf_op jit(solution)/shard_map/pallas_call | solution.py:94
  43.8 0.3 convert_element_type.36
  44.1 18.0 %all_to_all.25 = f16[4,32,16,256]{3,2,1,0:T(8,128)(2,1)S(1)} all-to-all(f16[4,32,16,256]{3,2,1,0:T(8,128)(2,1)S(1)} %bitcast.41), channel_id=1, replica_groups=mesh['x'=4,'y'=8,'c'=2,'zh'=4,'zl'=2] {'x'}, dimensions={0} | all-to-all | bytes 2097152 | tf_op jit(solution)/shard_map/all_to_all | solution.py:161
  62.1 0.2 convert_reduce_fusion
  62.3 0.7 convert_element_type.38
  63.1 8.3 %all-to-all-start.2 = ((f16[32,16,256]{2,1,0:T(8,128)(2,1)}), f16[32,16,256]{2,1,0:T(8,128)(2,1)S(1)}, u32[]{:S(2)}, u32[]{:S(2)}) async-start(f16[32,16,256]{2,1,0:T(8,128)(2,1)} %convert_element_type.38), calls=%async_computation.2 | async-start | bytes 524288 | tf_op jit(solution)/shard_map/all_to_all | solution.py:163
  71.4 0.2 fusion.2
  71.6 11.4 %all-to-all-done.2 = f16[32,16,256]{2,1,0:T(8,128)(2,1)S(1)} async-done(((f16[32,16,256]{2,1,0:T(8,128)(2,1)}), f16[32,16,256]{2,1,0:T(8,128)(2,1)S(1)}, u32[]{:S(2)}, u32[]{:S(2)}) %all-to-all-start.2) | async-done | bytes 262176 | tf_op jit(solution)/shard_map/all_to_all | solution.py:163
  83.1 0.1 reshape.313
  83.4 5.4 %collective-permute-start.3 = (f32[4,2,4,256]{3,2,1,0:T(4,128)S(1)}, f32[4,2,4,256]{3,2,1,0:T(4,128)S(1)}, u32[]{:S(2)}, u32[]{:S(2)}) collective-permute-start(f32[4,2,4,256]{3,2,1,0:T(4,128)S(1)} %dynamic-slice_bitcast_fusion), channel_id=1, source_target_pairs={{0,8},{8,0},{1,9},{9,1},{2,10},{10,2},{3,11},{11,3},{4,12},{12,4},... | collective-permute-start | bytes 98312 | tf_op jit(solution)/shard_map/ppermute | solution.py:169
  88.8 0.2 compare_reduce_fusion
  89.2 0.4 collective-permute-done.3
  89.7 0.1 multiply_reduce_fusion
  90.0 0.1 convert_reduce_fusion.4
  90.2 0.5 bitcast_select_fusion.2
  90.8 0.8 subtract_select_fusion
  91.9 14.6 %all_to_all.26 = bf16[8,16,1024]{2,1,0:T(8,128)(2,1)S(1)} all-to-all(bf16[8,16,1024]{2,1,0:T(8,128)(2,1)S(1)} %broadcast_in_dim.130), channel_id=1, replica_groups=mesh['x'=4,'y'=8,'c'=2,'zh'=4,'zl'=2] {'y'}, dimensions={0} | all-to-all | bytes 524288 | tf_op jit(solution)/shard_map/all_to_all | solution.py:66
  106.6 15.9 %all_to_all.27 = bf16[4,8,16,1024]{3,2,1,0:T(8,128)(2,1)S(1)} all-to-all(bf16[4,8,16,1024]{3,2,1,0:T(8,128)(2,1)S(1)} %broadcast_in_dim.131), channel_id=1, replica_groups=mesh['x'=4,'y'=8,'c'=2,'zh'=4,'zl'=2] {'x'}, dimensions={0} | all-to-all | bytes 2097152 | tf_op jit(solution)/shard_map/all_to_all | solution.py:66
  122.5 4.5 %collective-permute-start.4 = (bf16[512,1024]{1,0:T(8,128)(2,1)S(1)}, bf16[512,1024]{1,0:T(8,128)(2,1)S(1)}, u32[]{:S(2)}, u32[]{:S(2)}) collective-permute-start(bf16[512,1024]{1,0:T(8,128)(2,1)S(1)} %bitcast.38), channel_id=1, source_target_pairs={{0,8},{8,0},{1,9},{9,1},{2,10},{10,2},{3,11},{11,3},{4,12},{12,4},... | collective-permute-start | bytes 3145736 | tf_op jit(solution)/shard_map/ppermute | solution.py:185
  127.1 2.1 %collective-permute-done.4.other_ref = bf16[512,1024]{1,0:T(8,128)(2,1)S(1)} collective-permute-done((bf16[512,1024]{1,0:T(8,128)(2,1)S(1)}, bf16[512,1024]{1,0:T(8,128)(2,1)S(1)}, u32[]{:S(2)}, u32[]{:S(2)}) %collective-permute-start.4) | collective-permute-done | bytes 1048608 | tf_op jit(solution)/shard_map/ppermute | solution.py:185
  129.2 2.9 %shard_map.103 = bf16[128,4096]{1,0:T(8,128)(2,1)} custom-call(s32[128,1]{1,0:T(8,128)S(1)} %copy.21.target_ref, s32[1,512]{1,0:T(1,128)S(1)} %get-tuple-element.22.key_here_ref, s32[1,512]{1,0:T(1,128)S(1)} %get-tuple-element.21.key_other_ref, bf16[512,1024]{1,0:T(8,128)(2,1)S(1)} %bitcast.39, bf16[512,1024]{1,0:T(8,128)(2,1)S(1)} %collective-permute-done.4.other_ref), custom_call_target="tpu_custom_call" | custom-call | tf_op jit(solution)/shard_map/pallas_call | solution.py:116
  (40 shorter events, 1.5 us)
Async XLA Ops:
  0.6 17.0 %copy-start = (bf16[512,512]{1,0:T(8,128)(2,1)S(1)}, bf16[512,512]{1,0:T(8,128)(2,1)}, u32[]{:S(2)}) copy-start(bf16[512,512]{1,0:T(8,128)(2,1)} %param.7) | copy-start | bytes 1572868
  0.6 17.0 %collective-permute-start.1 = (bf16[512,512]{1,0:T(8,128)(2,1)}, bf16[512,512]{1,0:T(8,128)(2,1)S(1)}, u32[]{:S(2)}, u32[]{:S(2)}) collective-permute-start(bf16[512,512]{1,0:T(8,128)(2,1)} %param.7), channel_id=1, source_target_pairs={{0,1},{1,0},{2,3},{3,2},{4,5},{5,4},{6,7},{7,6},{8,9},{9,8},{10,11... | collective-permute-start | bytes 1572872 | tf_op jit(solution)/shard_map/ppermute | solution.py:136
  7.4 26.9 %all-to-all-start = ((bf16[4,512,128]{2,1,0:T(8,128)(2,1)}), bf16[4,512,128]{2,1,0:T(8,128)(2,1)S(1)}, u32[]{:S(2)}, u32[]{:S(2)}) async-start(bf16[4,512,128]{2,1,0:T(8,128)(2,1)} %broadcast_in_dim.123), calls=%async_computation | async-start | bytes 1048576 | tf_op jit(solution)/shard_map/all_to_all | solution.py:66
  17.7 22.4 %collective-permute-start.2 = (bf16[512,512]{1,0:T(8,128)(2,1)S(1)}, bf16[512,512]{1,0:T(8,128)(2,1)S(1)}, u32[]{:S(2)}, u32[]{:S(2)}) collective-permute-start(bf16[512,512]{1,0:T(8,128)(2,1)S(1)} %get-tuple-element.12), channel_id=1, source_target_pairs={{0,8},{8,0},{1,9},{9,1},{2,10},{10,2},{3,11},{11,3},{4,12},{12,4},... | collective-permute-start | bytes 1572872 | tf_op jit(solution)/shard_map/ppermute | solution.py:140
  34.3 6.9 %collective-permute-start = (bf16[4,512,128]{2,1,0:T(8,128)(2,1)S(1)}, bf16[4,512,128]{2,1,0:T(8,128)(2,1)S(1)}, u32[]{:S(2)}, u32[]{:S(2)}) collective-permute-start(bf16[4,512,128]{2,1,0:T(8,128)(2,1)S(1)} %all-to-all-done.cot_here_ref), channel_id=1, source_target_pairs={{0,8},{8,0},{1,9},{9,1},{2,10},{10,2},{3,11},{11,3},{4,12},{12,4},... | collective-permute-start | bytes 1572872 | tf_op jit(solution)/shard_map/ppermute | solution.py:141
  62.3 26.9 %copy-start.1 = (f32[1,1,4,4096]{3,2,1,0:T(4,128)S(1)}, f32[1,1,4,4096]{3,2,1,0:T(4,128)}, u32[]{:S(2)}) copy-start(f32[1,1,4,4096]{3,2,1,0:T(4,128)} %param.13) | copy-start | bytes 196612
  63.1 27.1 %copy-start.3 = (f32[1,1,2]{2,1,0:T(1,128)S(1)}, f32[1,1,2]{2,1,0:T(1,128)}, u32[]{:S(2)}) copy-start(f32[1,1,2]{2,1,0:T(1,128)} %param.12) | copy-start | bytes 28
  63.1 27.7 %copy-start.2 = (f32[1,1,4,4096]{3,2,1,0:T(4,128)S(1)}, f32[1,1,4,4096]{3,2,1,0:T(4,128)}, u32[]{:S(2)}) copy-start(f32[1,1,4,4096]{3,2,1,0:T(4,128)} %param.11) | copy-start | bytes 196612
  63.1 19.9 %all-to-all-start.2 = ((f16[32,16,256]{2,1,0:T(8,128)(2,1)}), f16[32,16,256]{2,1,0:T(8,128)(2,1)S(1)}, u32[]{:S(2)}, u32[]{:S(2)}) async-start(f16[32,16,256]{2,1,0:T(8,128)(2,1)} %convert_element_type.38), calls=%async_computation.2 | async-start | bytes 524288 | tf_op jit(solution)/shard_map/all_to_all | solution.py:163
  83.4 6.3 %collective-permute-start.3 = (f32[4,2,4,256]{3,2,1,0:T(4,128)S(1)}, f32[4,2,4,256]{3,2,1,0:T(4,128)S(1)}, u32[]{:S(2)}, u32[]{:S(2)}) collective-permute-start(f32[4,2,4,256]{3,2,1,0:T(4,128)S(1)} %dynamic-slice_bitcast_fusion), channel_id=1, source_target_pairs={{0,8},{8,0},{1,9},{9,1},{2,10},{10,2},{3,11},{11,3},{4,12},{12,4},... | collective-permute-start | bytes 98312 | tf_op jit(solution)/shard_map/ppermute | solution.py:169
  122.5 6.7 %collective-permute-start.4 = (bf16[512,1024]{1,0:T(8,128)(2,1)S(1)}, bf16[512,1024]{1,0:T(8,128)(2,1)S(1)}, u32[]{:S(2)}, u32[]{:S(2)}) collective-permute-start(bf16[512,1024]{1,0:T(8,128)(2,1)S(1)} %bitcast.38), channel_id=1, source_target_pairs={{0,8},{8,0},{1,9},{9,1},{2,10},{10,2},{3,11},{11,3},{4,12},{12,4},... | collective-permute-start | bytes 3145736 | tf_op jit(solution)/shard_map/ppermute | solution.py:185

commit v3 on v2

--- a/solution.py
+++ b/solution.py
@@ -10,7 +10,7 @@
 HD = 128
 GRID = (4, 8, 2)
 PAIR = 2
-CUT = 4
+CUT = 2
 
 
 beta_one = 0.9
@@ -66,78 +66,110 @@
     return lax.all_to_all(jnp.broadcast_to(block[None], (count,) + block.shape), axis, 0, 0, tiled=True)
 
 
-def gradient_kernel(target_ref, cot_here_ref, cot_other_ref, act_here_ref, act_other_ref, out_ref):
-    tokens = (((0,), (0,)), ((), ()))
-    grad = lax.dot_general(
-        cot_here_ref[0], act_here_ref[...], tokens, preferred_element_type=jnp.float32
-    ) + lax.dot_general(
-        cot_other_ref[0], act_other_ref[...], tokens, preferred_element_type=jnp.float32
+TOKEN_DOT = (((0,), (0,)), ((), ()))
+PARAMS = pltpu.CompilerParams(vmem_limit_bytes=32 * 2**20)
+
+
+def cost(flops, moved):
+    return pl.CostEstimate(flops=flops, bytes_accessed=moved, transcendentals=0)
+
+
+def first_kernel(cot_ref, act_ref, out_ref):
+    out_ref[0] = lax.dot_general(
+        cot_ref[0], act_ref[...], TOKEN_DOT, preferred_element_type=jnp.float32
+    )
+
+
+def padded_kernel(target_ref, first_ref, cot_ref, act_ref, out_ref):
+    grad = first_ref[0] + lax.dot_general(
+        cot_ref[0], act_ref[...], TOKEN_DOT, preferred_element_type=jnp.float32
     )
     high = grad.astype(jnp.bfloat16)
     low = (grad - high.astype(jnp.float32)).astype(jnp.bfloat16)
-    chips, rows, half = out_ref.shape[0], out_ref.shape[2] // 2, out_ref.shape[3]
-    slot = lax.broadcasted_iota(jnp.int32, (chips * rows, HD), 0)
-    pick = jnp.where(slot == target_ref[0], 0.5, 0.0).astype(jnp.bfloat16)
-    padded = jnp.dot(pick, high, preferred_element_type=jnp.float32) + jnp.dot(
-        pick, low, preferred_element_type=jnp.float32
-    )
-    parts = [padded[:, i * half : (i + 1) * half].reshape(chips, rows, half) for i in range(2)]
-    out_ref[:, 0] = jnp.concatenate(parts, axis=1).astype(out_ref.dtype)
-
-
-def padded_gradient(target, cot_here, cot_other, act_here, act_other, chips, rows):
+    chips, cores, _, rows, half = out_ref.shape
+    capacity = rows // 2
+    row = lax.broadcasted_iota(jnp.int32, (chips * cores * rows, HD), 0)
+    slot = row // rows * capacity + row % capacity
+    taken = slot == target_ref[0]
+    padded = jnp.zeros((chips * cores * rows, half), jnp.float32)
+    for part in range(2):
+        pick = jnp.where(taken & (row // capacity % 2 == part), 0.5, 0.0).astype(jnp.bfloat16)
+        span = slice(part * half, (part + 1) * half)
+        padded += jnp.dot(pick, high[:, span], preferred_element_type=jnp.float32)
+        padded += jnp.dot(pick, low[:, span], preferred_element_type=jnp.float32)
+    out_ref[:, :, 0] = padded.reshape(chips, cores, rows, half)
+
+
+def padded_gradient(target, cot_here, cot_other, act_here, act_other, chips, cores, capacity):
     heads, tokens, _ = cot_here.shape
     features = act_here.shape[1]
     cot = pl.BlockSpec((1, tokens, HD), lambda h: (h, 0, 0))
     act = pl.BlockSpec((tokens, features), lambda h: (0, 0))
-    shape = (chips, heads, 2 * rows, features // 2)
+    grad = pl.BlockSpec((1, HD, features), lambda h: (h, 0, 0))
+    first = pl.pallas_call(
+        first_kernel,
+        grid=(heads,),
+        in_specs=[cot, act],
+        out_specs=grad,
+        out_shape=jax.ShapeDtypeStruct((heads, HD, features), jnp.float32),
+        compiler_params=PARAMS,
+        cost_estimate=cost(2 * heads * tokens * HD * features, 2 * 2**20),
+    )(cot_here, act_here)
+    tail = (2 * capacity, features // 2)
     return pl.pallas_call(
-        gradient_kernel,
+        padded_kernel,
         grid=(heads,),
-        in_specs=[pl.BlockSpec((1, 1, HD), lambda h: (h, 0, 0)), cot, cot, act, act],
-        out_specs=pl.BlockSpec((chips, 1) + shape[2:], lambda h: (0, h, 0, 0)),
-        out_shape=jax.ShapeDtypeStruct(shape, jnp.float32),
-        compiler_params=pltpu.CompilerParams(vmem_limit_bytes=32 * 2**20),
-    )(target[:, None, :], cot_here, cot_other, act_here, act_other)
-
-
-def weight_kernel(target_ref, key_here_ref, key_other_ref, here_ref, other_ref, out_ref):
+        in_specs=[pl.BlockSpec((1, 1, HD), lambda h: (h, 0, 0)), grad, cot, act],
+        out_specs=pl.BlockSpec((chips, cores, 1) + tail, lambda h: (0, 0, h, 0, 0)),
+        out_shape=jax.ShapeDtypeStruct((chips, cores, heads) + tail, jnp.float32),
+        compiler_params=PARAMS,
+        cost_estimate=cost(4 * heads * tokens * HD * features, 4 * 2**20),
+    )(target[:, None, :], first, cot_other, act_other)
+
+
+def place_kernel(target_ref, key_ref, rows_ref, *refs):
     want = target_ref[...] * CUT + pl.program_id(0)
-    pick_here = jnp.where(want == key_here_ref[...], 1.0, 0.0).astype(jnp.bfloat16)
-    pick_other = jnp.where(want == key_other_ref[...], 1.0, 0.0).astype(jnp.bfloat16)
-    rows = jnp.dot(pick_here, here_ref[...], preferred_element_type=jnp.float32)
-    rows += jnp.dot(pick_other, other_ref[...], preferred_element_type=jnp.float32)
-    out_ref[...] = rows.astype(jnp.bfloat16)
-
-
-def place_rows(target, key_here, key_other, here, other):
-    count, piece = here.shape
+    pick = jnp.where(want == key_ref[...], 1.0, 0.0).astype(jnp.bfloat16)
+    placed = jnp.dot(pick, rows_ref[...], preferred_element_type=jnp.float32)
+    for ref in refs[:-1]:
+        placed += ref[...].astype(jnp.float32)
+    refs[-1][...] = placed.astype(jnp.bfloat16)
+
+
+def place_rows(target, key, rows, *placed):
+    count, piece = rows.shape
     whole = lambda shape: pl.BlockSpec(shape, lambda j: (0, 0))
+    piece_spec = pl.BlockSpec((HD, piece), lambda j: (0, j))
     return pl.pallas_call(
-        weight_kernel,
+        place_kernel,
         grid=(CUT,),
-        in_specs=[whole((HD, 1)), whole((1, count)), whole((1, count))] + [whole((count, piece))] * 2,
-        out_specs=pl.BlockSpec((HD, piece), lambda j: (0, j)),
+        in_specs=[whole((HD, 1)), whole((1, count)), whole((count, piece))] + [piece_spec] * len(placed),
+        out_specs=piece_spec,
         out_shape=jax.ShapeDtypeStruct((HD, CUT * piece), jnp.bfloat16),
-        compiler_params=pltpu.CompilerParams(vmem_limit_bytes=32 * 2**20),
-    )(target[:, None], key_here[None, :], key_other[None, :], here, other)
+        compiler_params=PARAMS,
+        cost_estimate=cost(2 * CUT * HD * count * piece, 2 * 2**20),
+    )(target[:, None], key[None, :], rows, *placed)
+
+
+FIRST_HAND = [(0, 1), (3, 2), (2, 0), (1, 3)]
+SECOND_HAND = [(2, 1), (1, 2)]
 
 
 def body(activations, cotangent, block_start, block_owner, first_moment, block_second, master_rows):
     nx, ny, nc = GRID
     capacity, width = first_moment.shape[2], first_moment.shape[3]
-    chips, rows = nx * ny, nc * capacity
+    chips = nx * ny
     core, side, pair = lax.axis_index("c"), lax.axis_index("zl"), lax.axis_index("zh")
     pairs = lax.axis_size("zh")
     chip = lax.axis_index("x") * ny + lax.axis_index("y")
     owner_here = chip * nc + core
-    features = activations.shape[1]
-
-    act_pair = lax.ppermute(activations, "zl", SWAP)
+    half = activations.shape[1] // 2
+
     cot_here = copies_to_all(cotangent, "zh")
-    own = core == side
-    act_here = jnp.where(own, activations, act_pair)
-    act_other = lax.ppermute(jnp.where(own, act_pair, activations), "c", SWAP)
+    hand_one = lax.ppermute(activations, ("c", "zl"), FIRST_HAND)
+    hand_two = lax.ppermute(activations, ("c", "zl"), SECOND_HAND)
+    act_here = jnp.where(core == side, activations, hand_one)
+    act_other = jnp.where(core == side, hand_one, hand_two)
     cot_other = lax.ppermute(cot_here, "c", SWAP)
 
     def of_side(table):
@@ -156,21 +188,16 @@
         slot_rank[None, :] == jnp.arange(2, dtype=jnp.int32)[:, None]
     )
 
-    send = padded_gradient(target, cot_here, cot_other, act_here, act_other, chips, rows)
-    send = send.astype(jnp.float16).reshape(nx, ny * pairs, 2 * rows, features // 2)
+    send = padded_gradient(
+        target, cot_here, cot_other, act_here, act_other, chips, nc, capacity
+    ).astype(jnp.float16)
+    send = send.reshape(nx, ny * nc * pairs, 2 * capacity, half)
     got = lax.all_to_all(send, "x", 0, 0, tiled=True)
     send = jnp.sum(got.astype(jnp.float32), axis=0).astype(jnp.float16)
-    got = lax.all_to_all(send, ("y", "zh"), 0, 0, tiled=True)
-    got = got.reshape(ny, pairs, 2, nc, capacity, features // 2)
+    got = lax.all_to_all(send, ("y", "c", "zh"), 0, 0, tiled=True)
+    got = got.reshape(ny, nc, pairs, 2, capacity, half)
     summed = jnp.sum(got.astype(jnp.float32), axis=0) * 2.0
-
-    keep = lax.dynamic_index_in_dim(summed, core, 2, keepdims=False)
-    give = lax.dynamic_index_in_dim(summed, 1 - core, 2, keepdims=False)
-    take = lax.ppermute(give, "c", SWAP)
-    even = jnp.where(core == 0, keep, take)
-    odd = jnp.where(core == 0, take, keep)
-    grad_slots = jnp.stack([even, odd], axis=1)
-    grad_slots = jnp.transpose(grad_slots, (3, 0, 1, 2, 4)).reshape(capacity, width)
+    grad_slots = jnp.transpose(summed, (3, 1, 0, 2, 4)).reshape(capacity, width)
     moment_new, second_new, master_new = adam_rows(
         grad_slots,
         first_moment[0, 0],
@@ -187,7 +214,8 @@
     from_chip, piece = row // (capacity * CUT), row % (capacity * CUT)
     key_here = (from_chip * nc + core) * capacity * CUT + piece
     key_other = (from_chip * nc + 1 - core) * capacity * CUT + piece
-    new_weight = place_rows(target_here, key_here, key_other, low, low_other)
+    placed = place_rows(target_here, key_here, low)
+    new_weight = place_rows(target_here, key_other, low_other, placed)
     return (new_weight, moment_new[None, None], second_new[None, None], master_new[None, None])
 
 

time: 133 us -> 131 us (0.985)
  blocking collectives: 48.5 us -> 27.8 us
  waiting for transfers between devices: 28.1 us -> 48.5 us
  starting transfers between devices: 41.1 us -> 38.4 us
    all_to_all x1 -> x0, blocking collectives: 18 us -> none  [body(): got = lax.all_to_all(send, 'x', 0, 0, tiled=True)]
    all_to_all x1 -> x2, waiting for transfers between devices: 11.4 us -> 28.8 us  [the longest x1 14.8 us: body(): got = lax.all_to_all(send, 'x', 0, 0, tiled=True)]
    all_to_all x1 -> x2, starting transfers between devices: 8.31 us -> 14.1 us  [the longest x1 9.92 us: body(): got = lax.all_to_all(send, ('y', 'c', 'zh'), 0, 0, tiled=True)]
    all_to_all x1, waiting for transfers between devices: 13.1 us -> 17.7 us  [copies_to_all(): lax.all_to_all(jnp.broadcast_to(block[None], (count,) + block.shape), axi...]
    ppermute x1, starting transfers between devices: 5.36 us -> 1.91 us  [body(): cot_other = lax.ppermute(cot_here, 'c', SWAP)]
    all_to_all x1, starting transfers between devices: 9.12 us -> 5.72 us  [copies_to_all(): lax.all_to_all(jnp.broadcast_to(block[None], (count,) + block.shape), axi...]
    ppermute x3 -> x2, starting transfers between devices: 13.9 us -> 10.8 us  [the longest x1 8.92 us: body(): hand_one = lax.ppermute(activations, ('c', 'zl'), FIRST_HAND)]
    all_to_all x2, blocking collectives: 30.5 us -> 27.8 us  [copies_to_all(): lax.all_to_all(jnp.broadcast_to(block[None], (count,) + block.shape), axi...]
  transfers between devices with their start and end apart: 7 -> 7, of which waited for: 5 -> 5; matrix products, arithmetic and copies ran while one was open for 3% -> 3% of each run, Pallas kernels for 0% -> 1%
where the time goes in v3:
time: 131 us
  waiting for transfers between devices  48.5 us (37%)
  starting transfers between devices  38.4 us (29%)
  blocking collectives  27.8 us (21%)
  Pallas kernels  6.31 us (5%)
  other arithmetic  5.35 us (4%)
  local copies, waits for them, and re-layouts  3.43 us (3%)
    all_to_all x2, blocking collectives, copies_to_all(): lax.all_to_all(jnp.broadcast_to(block[None], (count,) + block.shape), axi...  27.8 us
    all_to_all x1, waiting for transfers between devices, copies_to_all(): lax.all_to_all(jnp.broadcast_to(block[None], (count,) + block.shape), axi...  17.7 us
    all_to_all x1, waiting for transfers between devices, body(): got = lax.all_to_all(send, 'x', 0, 0, tiled=True)  14.8 us
    all_to_all x1, waiting for transfers between devices, body(): got = lax.all_to_all(send, ('y', 'c', 'zh'), 0, 0, tiled=True)  14.1 us
    all_to_all x1, starting transfers between devices, body(): got = lax.all_to_all(send, ('y', 'c', 'zh'), 0, 0, tiled=True)  9.92 us
    ppermute x1, starting transfers between devices, body(): hand_one = lax.ppermute(activations, ('c', 'zl'), FIRST_HAND)  8.92 us
    ppermute x1, starting transfers between devices, body(): low_other = lax.ppermute(low, 'c', SWAP)  5.82 us
    all_to_all x1, starting transfers between devices, copies_to_all(): lax.all_to_all(jnp.broadcast_to(block[None], (count,) + block.shape), axi...  5.72 us
  transfers between devices with their start and end apart: 7, of which 5 were waited for; matrix products, arithmetic and copies ran while one was open for 3% of the time, Pallas kernels for 1%

profile of v3, /device:TPU:1, one launch (start us, length us, event | category | flops | bytes accessed | tf_op | source)
XLA Modules:
  0.0 130.7 jit_solution(4438263683000452602)
XLA Ops:
  0.6 8.9 %collective-permute-start = (bf16[512,512]{1,0:T(8,128)(2,1)}, bf16[512,512]{1,0:T(8,128)(2,1)S(1)}, u32[]{:S(2)}, u32[]{:S(2)}) collective-permute-start(bf16[512,512]{1,0:T(8,128)(2,1)} %param.7), channel_id=1, source_target_pairs={{0,1},{9,8},{8,0},{1,9},{2,3},{11,10},{10,2},{3,11},{4,5},{13,12},... | collective-permute-start | bytes 1572872 | tf_op jit(solution)/shard_map/ppermute | solution.py:169
  9.6 1.9 %collective-permute-start.2 = (bf16[512,512]{1,0:T(8,128)(2,1)}, bf16[512,512]{1,0:T(8,128)(2,1)S(1)}, u32[]{:S(2)}, u32[]{:S(2)}) collective-permute-start(bf16[512,512]{1,0:T(8,128)(2,1)} %param.7), channel_id=1, source_target_pairs={{8,1},{1,8},{10,3},{3,10},{12,5},{5,12},{14,7},{7,14},{24,17},{17,... | collective-permute-start | bytes 1572872 | tf_op jit(solution)/shard_map/ppermute | solution.py:170
  11.5 1.8 %broadcast_in_dim.124 = bf16[4,512,128]{2,1,0:T(8,128)(2,1)} broadcast(bf16[512,128]{1,0:T(8,128)(2,1)} %param.8), dimensions={1,2} | broadcast | bytes 655360 | tf_op jit(solution)/shard_map/broadcast_in_dim | solution.py:66
  13.3 5.7 %all-to-all-start = ((bf16[4,512,128]{2,1,0:T(8,128)(2,1)}), bf16[4,512,128]{2,1,0:T(8,128)(2,1)S(1)}, u32[]{:S(2)}, u32[]{:S(2)}) async-start(bf16[4,512,128]{2,1,0:T(8,128)(2,1)} %broadcast_in_dim.124), calls=%async_computation | async-start | bytes 1048576 | tf_op jit(solution)/shard_map/all_to_all | solution.py:66
  19.0 0.7 constant_dynamic-slice_fusion.2
  19.8 0.3 convert_reduce_fusion.2
  20.1 0.2 select_reduce_fusion
  20.3 0.2 convert_reduce_fusion.1
  20.5 17.7 %all-to-all-done.cot_ref = bf16[4,512,128]{2,1,0:T(8,128)(2,1)S(1)} async-done(((bf16[4,512,128]{2,1,0:T(8,128)(2,1)}), bf16[4,512,128]{2,1,0:T(8,128)(2,1)S(1)}, u32[]{:S(2)}, u32[]{:S(2)}) %all-to-all-start) | async-done | bytes 524320 | tf_op jit(solution)/shard_map/all_to_all | solution.py:66
  38.2 1.9 %collective-permute-start.1 = (bf16[4,512,128]{2,1,0:T(8,128)(2,1)S(1)}, bf16[4,512,128]{2,1,0:T(8,128)(2,1)S(1)}, u32[]{:S(2)}, u32[]{:S(2)}) collective-permute-start(bf16[4,512,128]{2,1,0:T(8,128)(2,1)S(1)} %all-to-all-done.cot_ref), channel_id=1, source_target_pairs={{0,8},{8,0},{1,9},{9,1},{2,10},{10,2},{3,11},{11,3},{4,12},{12,4},... | collective-permute-start | bytes 1572872 | tf_op jit(solution)/shard_map/ppermute | solution.py:173
  40.3 1.1 shard_map.102.first_ref
  41.3 0.7 collective-permute-done.1.cot_ref
  42.0 2.9 %shard_map.103 = f32[32,2,4,8,256]{4,3,2,1,0:T(8,128)S(1)} custom-call(s32[4,1,128]{2,1,0:T(1,128)S(1)} %bitcast.27, f32[4,128,512]{2,1,0:T(8,128)S(1)} %shard_map.102.first_ref, bf16[4,512,128]{2,1,0:T(8,128)(2,1)S(1)} %collective-permute-done.1.cot_ref, bf16[512,512]{1,0:T(8,128)(2,1)S(1)} %get-tuple-element.12.act_ref), custom_call_target="tpu_custom_call" | custom-call | flops 536870912 | bytes 4194304 | tf_op jit(solution)/shard_map/pallas_call | solution.py:119
  44.9 1.3 convert_element_type.36
  46.1 4.1 %all-to-all-start.1 = ((f16[4,64,8,256]{3,2,1,0:T(8,128)(2,1)}), f16[4,64,8,256]{3,2,1,0:T(8,128)(2,1)S(1)}, u32[]{:S(2)}, u32[]{:S(2)}) async-start(f16[4,64,8,256]{3,2,1,0:T(8,128)(2,1)} %bitcast.7), calls=%async_computation.1 | async-start | bytes 2097152 | tf_op jit(solution)/shard_map/all_to_all | solution.py:195
  50.3 14.8 %all-to-all-done.1 = f16[4,64,8,256]{3,2,1,0:T(8,128)(2,1)S(1)} async-done(((f16[4,64,8,256]{3,2,1,0:T(8,128)(2,1)}), f16[4,64,8,256]{3,2,1,0:T(8,128)(2,1)S(1)}, u32[]{:S(2)}, u32[]{:S(2)}) %all-to-all-start.1) | async-done | bytes 1048608 | tf_op jit(solution)/shard_map/all_to_all | solution.py:195
  65.2 0.7 convert_element_type.38
  66.0 9.9 %all-to-all-start.2 = ((f16[64,8,256]{2,1,0:T(8,128)(2,1)}), f16[64,8,256]{2,1,0:T(8,128)(2,1)S(1)}, u32[]{:S(2)}, u32[]{:S(2)}) async-start(f16[64,8,256]{2,1,0:T(8,128)(2,1)} %convert_element_type.38), calls=%async_computation.2 | async-start | bytes 524288 | tf_op jit(solution)/shard_map/all_to_all | solution.py:197
  75.9 0.2 compare_reduce_fusion
  76.3 0.2 fusion
  76.5 14.1 %all-to-all-done.2 = f16[64,8,256]{2,1,0:T(8,128)(2,1)S(1)} async-done(((f16[64,8,256]{2,1,0:T(8,128)(2,1)}), f16[64,8,256]{2,1,0:T(8,128)(2,1)S(1)}, u32[]{:S(2)}, u32[]{:S(2)}) %all-to-all-start.2) | async-done | bytes 262176 | tf_op jit(solution)/shard_map/all_to_all | solution.py:197
  90.6 0.1 reshape.313
  90.9 0.1 multiply_reduce_fusion
  91.2 0.1 convert_reduce_fusion.4
  91.4 0.5 bitcast_select_fusion
  92.0 0.8 subtract_select_fusion
  93.1 13.3 %all_to_all.25 = bf16[8,8,2048]{2,1,0:T(8,128)(2,1)S(1)} all-to-all(bf16[8,8,2048]{2,1,0:T(8,128)(2,1)S(1)} %broadcast_in_dim.131), channel_id=1, replica_groups=mesh['x'=4,'y'=8,'c'=2,'zh'=4,'zl'=2] {'y'}, dimensions={0} | all-to-all | bytes 524288 | tf_op jit(solution)/shard_map/all_to_all | solution.py:66
  106.5 14.5 %all_to_all.26 = bf16[4,8,8,2048]{3,2,1,0:T(8,128)(2,1)S(1)} all-to-all(bf16[4,8,8,2048]{3,2,1,0:T(8,128)(2,1)S(1)} %broadcast_in_dim.132), channel_id=1, replica_groups=mesh['x'=4,'y'=8,'c'=2,'zh'=4,'zl'=2] {'x'}, dimensions={0} | all-to-all | bytes 2097152 | tf_op jit(solution)/shard_map/all_to_all | solution.py:66
  121.0 5.8 %collective-permute-start.3 = (bf16[256,2048]{1,0:T(8,128)(2,1)S(1)}, bf16[256,2048]{1,0:T(8,128)(2,1)S(1)}, u32[]{:S(2)}, u32[]{:S(2)}) collective-permute-start(bf16[256,2048]{1,0:T(8,128)(2,1)S(1)} %bitcast.25), channel_id=1, source_target_pairs={{0,8},{8,0},{1,9},{9,1},{2,10},{10,2},{3,11},{11,3},{4,12},{12,4},... | collective-permute-start | bytes 3145736 | tf_op jit(solution)/shard_map/ppermute | solution.py:212
  127.0 0.8 shard_map.104.refs_0_
  127.8 1.3 %collective-permute-done.3.rows_ref = bf16[256,2048]{1,0:T(8,128)(2,1)S(1)} collective-permute-done((bf16[256,2048]{1,0:T(8,128)(2,1)S(1)}, bf16[256,2048]{1,0:T(8,128)(2,1)S(1)}, u32[]{:S(2)}, u32[]{:S(2)}) %collective-permute-start.3) | collective-permute-done | bytes 1048608 | tf_op jit(solution)/shard_map/ppermute | solution.py:212
  129.1 1.6 %shard_map.105 = bf16[128,4096]{1,0:T(8,128)(2,1)} custom-call(s32[128,1]{1,0:T(8,128)S(1)} %copy.20.target_ref, s32[1,256]{1,0:T(1,128)S(1)} %get-tuple-element.20.key_ref, bf16[256,2048]{1,0:T(8,128)(2,1)S(1)} %collective-permute-done.3.rows_ref, bf16[128,4096]{1,0:T(8,128)(2,1)S(1)} %shard_map.104.refs_0_), custom_call_target="tpu_custom_call" | custom-call | flops 268435456 | bytes 2097152 | tf_op jit(solution)/shard_map/pallas_call | solution.py:143
  (38 shorter events, 1.5 us)
Async XLA Ops:
  0.6 39.5 %copy-start = (bf16[512,512]{1,0:T(8,128)(2,1)S(1)}, bf16[512,512]{1,0:T(8,128)(2,1)}, u32[]{:S(2)}) copy-start(bf16[512,512]{1,0:T(8,128)(2,1)} %param.7) | copy-start | bytes 1572868
  0.6 39.5 %collective-permute-start = (bf16[512,512]{1,0:T(8,128)(2,1)}, bf16[512,512]{1,0:T(8,128)(2,1)S(1)}, u32[]{:S(2)}, u32[]{:S(2)}) collective-permute-start(bf16[512,512]{1,0:T(8,128)(2,1)} %param.7), channel_id=1, source_target_pairs={{0,1},{9,8},{8,0},{1,9},{2,3},{11,10},{10,2},{3,11},{4,5},{13,12},... | collective-permute-start | bytes 1572872 | tf_op jit(solution)/shard_map/ppermute | solution.py:169
  9.6 30.6 %collective-permute-start.2 = (bf16[512,512]{1,0:T(8,128)(2,1)}, bf16[512,512]{1,0:T(8,128)(2,1)S(1)}, u32[]{:S(2)}, u32[]{:S(2)}) collective-permute-start(bf16[512,512]{1,0:T(8,128)(2,1)} %param.7), channel_id=1, source_target_pairs={{8,1},{1,8},{10,3},{3,10},{12,5},{5,12},{14,7},{7,14},{24,17},{17,... | collective-permute-start | bytes 1572872 | tf_op jit(solution)/shard_map/ppermute | solution.py:170
  13.3 24.9 %all-to-all-start = ((bf16[4,512,128]{2,1,0:T(8,128)(2,1)}), bf16[4,512,128]{2,1,0:T(8,128)(2,1)S(1)}, u32[]{:S(2)}, u32[]{:S(2)}) async-start(bf16[4,512,128]{2,1,0:T(8,128)(2,1)} %broadcast_in_dim.124), calls=%async_computation | async-start | bytes 1048576 | tf_op jit(solution)/shard_map/all_to_all | solution.py:66
  38.2 3.8 %collective-permute-start.1 = (bf16[4,512,128]{2,1,0:T(8,128)(2,1)S(1)}, bf16[4,512,128]{2,1,0:T(8,128)(2,1)S(1)}, u32[]{:S(2)}, u32[]{:S(2)}) collective-permute-start(bf16[4,512,128]{2,1,0:T(8,128)(2,1)S(1)} %all-to-all-done.cot_ref), channel_id=1, source_target_pairs={{0,8},{8,0},{1,9},{9,1},{2,10},{10,2},{3,11},{11,3},{4,12},{12,4},... | collective-permute-start | bytes 1572872 | tf_op jit(solution)/shard_map/ppermute | solution.py:173
  46.1 30.2 %copy-start.1 = (f32[1,1,4,4096]{3,2,1,0:T(4,128)S(1)}, f32[1,1,4,4096]{3,2,1,0:T(4,128)}, u32[]{:S(2)}) copy-start(f32[1,1,4,4096]{3,2,1,0:T(4,128)} %param.13) | copy-start | bytes 196612
  46.1 18.9 %all-to-all-start.1 = ((f16[4,64,8,256]{3,2,1,0:T(8,128)(2,1)}), f16[4,64,8,256]{3,2,1,0:T(8,128)(2,1)S(1)}, u32[]{:S(2)}, u32[]{:S(2)}) async-start(f16[4,64,8,256]{3,2,1,0:T(8,128)(2,1)} %bitcast.7), calls=%async_computation.1 | async-start | bytes 2097152 | tf_op jit(solution)/shard_map/all_to_all | solution.py:195
  65.2 26.2 %copy-start.3 = (f32[1,1,2]{2,1,0:T(1,128)S(1)}, f32[1,1,2]{2,1,0:T(1,128)}, u32[]{:S(2)}) copy-start(f32[1,1,2]{2,1,0:T(1,128)} %param.12) | copy-start | bytes 28
  65.2 26.8 %copy-start.2 = (f32[1,1,4,4096]{3,2,1,0:T(4,128)S(1)}, f32[1,1,4,4096]{3,2,1,0:T(4,128)}, u32[]{:S(2)}) copy-start(f32[1,1,4,4096]{3,2,1,0:T(4,128)} %param.11) | copy-start | bytes 196612
  66.0 24.6 %all-to-all-start.2 = ((f16[64,8,256]{2,1,0:T(8,128)(2,1)}), f16[64,8,256]{2,1,0:T(8,128)(2,1)S(1)}, u32[]{:S(2)}, u32[]{:S(2)}) async-start(f16[64,8,256]{2,1,0:T(8,128)(2,1)} %convert_element_type.38), calls=%async_computation.2 | async-start | bytes 524288 | tf_op jit(solution)/shard_map/all_to_all | solution.py:197
  121.0 8.1 %collective-permute-start.3 = (bf16[256,2048]{1,0:T(8,128)(2,1)S(1)}, bf16[256,2048]{1,0:T(8,128)(2,1)S(1)}, u32[]{:S(2)}, u32[]{:S(2)}) collective-permute-start(bf16[256,2048]{1,0:T(8,128)(2,1)S(1)} %bitcast.25), channel_id=1, source_target_pairs={{0,8},{8,0},{1,9},{9,1},{2,10},{10,2},{3,11},{11,3},{4,12},{12,4},... | collective-permute-start | bytes 3145736 | tf_op jit(solution)/shard_map/ppermute | solution.py:212

commit v4 on v3

--- a/solution.py
+++ b/solution.py
@@ -74,57 +74,62 @@
     return pl.CostEstimate(flops=flops, bytes_accessed=moved, transcendentals=0)
 
 
-def first_kernel(cot_ref, act_ref, out_ref):
-    out_ref[0] = lax.dot_general(
-        cot_ref[0], act_ref[...], TOKEN_DOT, preferred_element_type=jnp.float32
-    )
-
-
-def padded_kernel(target_ref, first_ref, cot_ref, act_ref, out_ref):
-    grad = first_ref[0] + lax.dot_general(
-        cot_ref[0], act_ref[...], TOKEN_DOT, preferred_element_type=jnp.float32
-    )
-    high = grad.astype(jnp.bfloat16)
-    low = (grad - high.astype(jnp.float32)).astype(jnp.bfloat16)
+def first_kernel(cot_ref, own_ref, near_ref, out_ref):
+    half = own_ref.shape[1]
+    for part, act_ref in enumerate((own_ref, near_ref)):
+        out_ref[0, :, part * half : (part + 1) * half] = lax.dot_general(
+            cot_ref[0], act_ref[...], TOKEN_DOT, preferred_element_type=jnp.float32
+        )
+
+
+def padded_kernel(target_ref, first_ref, cot_ref, own_ref, near_ref, out_ref):
     chips, cores, _, rows, half = out_ref.shape
     capacity = rows // 2
     row = lax.broadcasted_iota(jnp.int32, (chips * cores * rows, HD), 0)
     slot = row // rows * capacity + row % capacity
     taken = slot == target_ref[0]
     padded = jnp.zeros((chips * cores * rows, half), jnp.float32)
-    for part in range(2):
+    for part, act_ref in enumerate((own_ref, near_ref)):
+        grad = first_ref[0, :, part * half : (part + 1) * half] + lax.dot_general(
+            cot_ref[0], act_ref[...], TOKEN_DOT, preferred_element_type=jnp.float32
+        )
+        high = grad.astype(jnp.bfloat16)
+        low = (grad - high.astype(jnp.float32)).astype(jnp.bfloat16)
         pick = jnp.where(taken & (row // capacity % 2 == part), 0.5, 0.0).astype(jnp.bfloat16)
-        span = slice(part * half, (part + 1) * half)
-        padded += jnp.dot(pick, high[:, span], preferred_element_type=jnp.float32)
-        padded += jnp.dot(pick, low[:, span], preferred_element_type=jnp.float32)
+        padded += jnp.dot(
+            jnp.concatenate([pick, pick], axis=1),
+            jnp.concatenate([high, low], axis=0),
+            preferred_element_type=jnp.float32,
+        )
     out_ref[:, :, 0] = padded.reshape(chips, cores, rows, half)
 
 
 def padded_gradient(target, cot_here, cot_other, act_here, act_other, chips, cores, capacity):
     heads, tokens, _ = cot_here.shape
-    features = act_here.shape[1]
+    half = act_here[0].shape[1]
+    features = 2 * half
     cot = pl.BlockSpec((1, tokens, HD), lambda h: (h, 0, 0))
-    act = pl.BlockSpec((tokens, features), lambda h: (0, 0))
+    act = pl.BlockSpec((tokens, half), lambda h: (0, 0))
     grad = pl.BlockSpec((1, HD, features), lambda h: (h, 0, 0))
     first = pl.pallas_call(
         first_kernel,
         grid=(heads,),
-        in_specs=[cot, act],
+        in_specs=[cot, act, act],
         out_specs=grad,
         out_shape=jax.ShapeDtypeStruct((heads, HD, features), jnp.float32),
         compiler_params=PARAMS,
         cost_estimate=cost(2 * heads * tokens * HD * features, 2 * 2**20),
-    )(cot_here, act_here)
-    tail = (2 * capacity, features // 2)
+    )(cot_here, *act_here)
+    tail = (2 * capacity, half)
     return pl.pallas_call(
         padded_kernel,
         grid=(heads,),
-        in_specs=[pl.BlockSpec((1, 1, HD), lambda h: (h, 0, 0)), grad, cot, act],
+        in_specs=[pl.BlockSpec((1, 1, HD), lambda h: (h, 0, 0)), grad, cot, act, act],
         out_specs=pl.BlockSpec((chips, cores, 1) + tail, lambda h: (0, 0, h, 0, 0)),
         out_shape=jax.ShapeDtypeStruct((chips, cores, heads) + tail, jnp.float32),
         compiler_params=PARAMS,
         cost_estimate=cost(4 * heads * tokens * HD * features, 4 * 2**20),
-    )(target[:, None, :], first, cot_other, act_other)
+    )(target[:, None, :], first, cot_other, *act_other)
 
 
 def place_kernel(target_ref, key_ref, rows_ref, *refs):
@@ -151,10 +156,6 @@
     )(target[:, None], key[None, :], rows, *placed)
 
 
-FIRST_HAND = [(0, 1), (3, 2), (2, 0), (1, 3)]
-SECOND_HAND = [(2, 1), (1, 2)]
-
-
 def body(activations, cotangent, block_start, block_owner, first_moment, block_second, master_rows):
     nx, ny, nc = GRID
     capacity, width = first_moment.shape[2], first_moment.shape[3]
@@ -166,10 +167,14 @@
     half = activations.shape[1] // 2
 
     cot_here = copies_to_all(cotangent, "zh")
-    hand_one = lax.ppermute(activations, ("c", "zl"), FIRST_HAND)
-    hand_two = lax.ppermute(activations, ("c", "zl"), SECOND_HAND)
-    act_here = jnp.where(core == side, activations, hand_one)
-    act_other = jnp.where(core == side, hand_one, hand_two)
+    keep = lax.dynamic_slice_in_dim(activations, core * half, half, 1)
+    give = lax.dynamic_slice_in_dim(activations, (1 - core) * half, half, 1)
+    depth = PAIR * pairs
+    to_chip = lambda core_to, z: core_to * depth + (z + 2 * core_to - 1) % depth
+    same = [(c * depth + z, to_chip(c, z)) for c in range(nc) for z in range(depth)]
+    cross = [(c * depth + z, to_chip(1 - c, z)) for c in range(nc) for z in range(depth)]
+    act_here = (keep, lax.ppermute(keep, ("c", "zh", "zl"), same))
+    act_other = (lax.ppermute(give, "c", SWAP), lax.ppermute(give, ("c", "zh", "zl"), cross))
     cot_other = lax.ppermute(cot_here, "c", SWAP)
 
     def of_side(table):
@@ -197,7 +202,12 @@
     got = lax.all_to_all(send, ("y", "c", "zh"), 0, 0, tiled=True)
     got = got.reshape(ny, nc, pairs, 2, capacity, half)
     summed = jnp.sum(got.astype(jnp.float32), axis=0) * 2.0
-    grad_slots = jnp.transpose(summed, (3, 1, 0, 2, 4)).reshape(capacity, width)
+    lower = summed[0].reshape(2 * pairs, capacity, half)
+    upper = summed[1, :, ::-1].reshape(2 * pairs, capacity, half)
+    lower = jnp.where(side == 0, lower, jnp.roll(lower, 1, 0))
+    upper = jnp.where(side == 0, jnp.roll(upper, -1, 0), upper)
+    grad_slots = jnp.stack([lower, upper], axis=1)
+    grad_slots = jnp.transpose(grad_slots, (2, 0, 1, 3)).reshape(capacity, width)
     moment_new, second_new, master_new = adam_rows(
         grad_slots,
         first_moment[0, 0],

time: 131 us -> 126 us (0.962)
  waiting for transfers between devices: 48.5 us -> 33.6 us
  starting transfers between devices: 38.4 us -> 47.8 us
    all_to_all x1, waiting for transfers between devices: 17.7 us -> 0.01 us  [copies_to_all(): lax.all_to_all(jnp.broadcast_to(block[None], (count,) + block.shape), axi...]
    all_to_all x1, starting transfers between devices: 5.72 us -> 10.8 us  [copies_to_all(): lax.all_to_all(jnp.broadcast_to(block[None], (count,) + block.shape), axi...]
    ppermute x2 -> x3, waiting for transfers between devices: 0.01 us -> 3.59 us  [the longest x1 3.58 us: body(): act_here = (keep, lax.ppermute(keep, ('c', 'zh', 'zl'), same))]
    ppermute x1, starting transfers between devices: 1.91 us -> 5.45 us  [body(): cot_other = lax.ppermute(cot_here, 'c', SWAP)]
    ppermute x2 -> x3, starting transfers between devices: 10.8 us -> 10.5 us  [the longest x1 5.67 us: body(): lax.ppermute(give, ('c', 'zh', 'zl'), cross)]
  transfers between devices with their start and end apart: 7 -> 8, of which waited for: 5 -> 4; matrix products, arithmetic and copies ran while one was open for 3% -> 2% of each run, Pallas kernels for 1% -> 2%
where the time goes in v4:
time: 126 us; the launch traced here: 125 us
  starting transfers between devices  47.8 us (38%)
  waiting for transfers between devices  33.6 us (27%)
  blocking collectives  28 us (22%)
  Pallas kernels  5.88 us (5%)
  other arithmetic  5.3 us (4%)
  local copies, waits for them, and re-layouts  3.85 us (3%)
    all_to_all x2, blocking collectives, copies_to_all(): lax.all_to_all(jnp.broadcast_to(block[None], (count,) + block.shape), axi...  28 us
    all_to_all x1, waiting for transfers between devices, body(): got = lax.all_to_all(send, 'x', 0, 0, tiled=True)  14.6 us
    all_to_all x1, waiting for transfers between devices, body(): got = lax.all_to_all(send, ('y', 'c', 'zh'), 0, 0, tiled=True)  14.1 us
    all_to_all x1, starting transfers between devices, body(): got = lax.all_to_all(send, ('y', 'c', 'zh'), 0, 0, tiled=True)  11.1 us
    all_to_all x1, starting transfers between devices, copies_to_all(): lax.all_to_all(jnp.broadcast_to(block[None], (count,) + block.shape), axi...  10.8 us
    ppermute x1, starting transfers between devices, body(): low_other = lax.ppermute(low, 'c', SWAP)  5.79 us
    ppermute x1, starting transfers between devices, body(): lax.ppermute(give, ('c', 'zh', 'zl'), cross)  5.67 us
    ppermute x1, starting transfers between devices, body(): cot_other = lax.ppermute(cot_here, 'c', SWAP)  5.45 us
  transfers between devices with their start and end apart: 8, of which 4 were waited for; matrix products, arithmetic and copies ran while one was open for 2% of the time, Pallas kernels for 2%

profile of v4, /device:TPU:1, one launch (start us, length us, event | category | flops | bytes accessed | tf_op | source)
XLA Modules:
  0.0 125.3 jit_solution(16624938395770360796)
XLA Ops:
  0.7 1.8 %broadcast_in_dim.124 = bf16[4,512,128]{2,1,0:T(8,128)(2,1)} broadcast(bf16[512,128]{1,0:T(8,128)(2,1)} %param.8), dimensions={1,2} | broadcast | bytes 655360 | tf_op jit(solution)/shard_map/broadcast_in_dim | solution.py:66
  2.4 10.8 %all-to-all-start = ((bf16[4,512,128]{2,1,0:T(8,128)(2,1)}), bf16[4,512,128]{2,1,0:T(8,128)(2,1)S(1)}, u32[]{:S(2)}, u32[]{:S(2)}) async-start(bf16[4,512,128]{2,1,0:T(8,128)(2,1)} %broadcast_in_dim.124), calls=%async_computation | async-start | bytes 1048576 | tf_op jit(solution)/shard_map/all_to_all | solution.py:66
  13.3 1.1 constant_dynamic-slice_fusion.1
  14.3 2.9 %collective-permute-start.2 = (bf16[512,256]{1,0:T(8,128)(2,1)S(1)}, bf16[512,256]{1,0:T(8,128)(2,1)S(1)}, u32[]{:S(2)}, u32[]{:S(2)}) collective-permute-start(bf16[512,256]{1,0:T(8,128)(2,1)S(1)} %get-tuple-element.12), channel_id=1, source_target_pairs={{0,8},{8,0},{1,9},{9,1},{2,10},{10,2},{3,11},{11,3},{4,12},{12,4},... | collective-permute-start | bytes 786440 | tf_op jit(solution)/shard_map/ppermute | solution.py:177
  17.2 5.7 %collective-permute-start.3 = (bf16[512,256]{1,0:T(8,128)(2,1)S(1)}, bf16[512,256]{1,0:T(8,128)(2,1)S(1)}, u32[]{:S(2)}, u32[]{:S(2)}) collective-permute-start(bf16[512,256]{1,0:T(8,128)(2,1)S(1)} %get-tuple-element.12), channel_id=1, source_target_pairs={{0,9},{1,10},{2,11},{3,12},{4,13},{5,14},{6,15},{7,8},{8,7},{9,0},... | collective-permute-start | bytes 786440 | tf_op jit(solution)/shard_map/ppermute | solution.py:177
  22.9 1.9 %collective-permute-start = (bf16[512,256]{1,0:T(8,128)(2,1)S(1)}, bf16[512,256]{1,0:T(8,128)(2,1)S(1)}, u32[]{:S(2)}, u32[]{:S(2)}) collective-permute-start(bf16[512,256]{1,0:T(8,128)(2,1)S(1)} %get-tuple-element.13.own_ref), channel_id=1, source_target_pairs={{0,7},{1,0},{2,1},{3,2},{4,3},{5,4},{6,5},{7,6},{8,9},{9,10},{10,1... | collective-permute-start | bytes 786440 | tf_op jit(solution)/shard_map/ppermute | solution.py:176
  25.0 0.3 convert_reduce_fusion.2
  25.3 5.5 %collective-permute-start.1 = (bf16[4,512,128]{2,1,0:T(8,128)(2,1)S(1)}, bf16[4,512,128]{2,1,0:T(8,128)(2,1)S(1)}, u32[]{:S(2)}, u32[]{:S(2)}) collective-permute-start(bf16[4,512,128]{2,1,0:T(8,128)(2,1)S(1)} %all-to-all-done.cot_ref), channel_id=1, source_target_pairs={{0,8},{8,0},{1,9},{9,1},{2,10},{10,2},{3,11},{11,3},{4,12},{12,4},... | collective-permute-start | bytes 1572872 | tf_op jit(solution)/shard_map/ppermute | solution.py:178
  30.8 0.2 select_reduce_fusion
  30.9 0.2 convert_reduce_fusion.1
  31.2 3.6 %collective-permute-done.near_ref = bf16[512,256]{1,0:T(8,128)(2,1)S(1)} collective-permute-done((bf16[512,256]{1,0:T(8,128)(2,1)S(1)}, bf16[512,256]{1,0:T(8,128)(2,1)S(1)}, u32[]{:S(2)}, u32[]{:S(2)}) %collective-permute-start) | collective-permute-done | bytes 262176 | tf_op jit(solution)/shard_map/ppermute | solution.py:176
  34.8 1.1 shard_map.102.first_ref
  35.9 2.4 %shard_map.103 = f32[32,2,4,8,256]{4,3,2,1,0:T(8,128)S(1)} custom-call(s32[4,1,128]{2,1,0:T(1,128)S(1)} %bitcast.39, f32[4,128,512]{2,1,0:T(8,128)S(1)} %shard_map.102.first_ref, bf16[4,512,128]{2,1,0:T(8,128)(2,1)S(1)} %collective-permute-done.1.cot_ref, bf16[512,256]{1,0:T(8,128)(2,1)S(1)} %collective-permute-done.2.own_ref, ...), custom_call_target="tpu_custom_call" | custom-call | flops 536870912 | bytes 4194304 | tf_op jit(solution)/shard_map/pallas_call | solution.py:124
  38.3 1.3 %convert_element_type.36 = f16[32,2,4,8,256]{4,3,2,1,0:T(8,128)(2,1)} convert(f32[32,2,4,8,256]{4,3,2,1,0:T(8,128)S(1)} %shard_map.103) | non-fusion elementwise | flops 524288 | bytes 3145728 | tf_op jit(solution)/shard_map/convert_element_type | solution.py:198
  39.6 4.1 %all-to-all-start.1 = ((f16[4,64,8,256]{3,2,1,0:T(8,128)(2,1)}), f16[4,64,8,256]{3,2,1,0:T(8,128)(2,1)S(1)}, u32[]{:S(2)}, u32[]{:S(2)}) async-start(f16[4,64,8,256]{3,2,1,0:T(8,128)(2,1)} %bitcast.7), calls=%async_computation.1 | async-start | bytes 2097152 | tf_op jit(solution)/shard_map/all_to_all | solution.py:200
  43.7 14.6 %all-to-all-done.1 = f16[4,64,8,256]{3,2,1,0:T(8,128)(2,1)S(1)} async-done(((f16[4,64,8,256]{3,2,1,0:T(8,128)(2,1)}), f16[4,64,8,256]{3,2,1,0:T(8,128)(2,1)S(1)}, u32[]{:S(2)}, u32[]{:S(2)}) %all-to-all-start.1) | async-done | bytes 1048608 | tf_op jit(solution)/shard_map/all_to_all | solution.py:200
  58.4 0.7 convert_element_type.38
  59.1 11.1 %all-to-all-start.2 = ((f16[64,8,256]{2,1,0:T(8,128)(2,1)}), f16[64,8,256]{2,1,0:T(8,128)(2,1)S(1)}, u32[]{:S(2)}, u32[]{:S(2)}) async-start(f16[64,8,256]{2,1,0:T(8,128)(2,1)} %convert_element_type.38), calls=%async_computation.2 | async-start | bytes 524288 | tf_op jit(solution)/shard_map/all_to_all | solution.py:202
  70.3 0.2 compare_reduce_fusion
  70.7 0.2 fusion
  70.9 14.1 %all-to-all-done.2 = f16[64,8,256]{2,1,0:T(8,128)(2,1)S(1)} async-done(((f16[64,8,256]{2,1,0:T(8,128)(2,1)}), f16[64,8,256]{2,1,0:T(8,128)(2,1)S(1)}, u32[]{:S(2)}, u32[]{:S(2)}) %all-to-all-start.2) | async-done | bytes 262176 | tf_op jit(solution)/shard_map/all_to_all | solution.py:202
  85.0 0.1 reshape.385
  85.4 0.1 multiply_reduce_fusion
  85.7 0.1 convert_reduce_fusion.4
  85.9 0.5 bitcast_select_fusion
  86.5 0.8 subtract_select_fusion
  87.6 13.4 %all_to_all.25 = bf16[8,8,2048]{2,1,0:T(8,128)(2,1)S(1)} all-to-all(bf16[8,8,2048]{2,1,0:T(8,128)(2,1)S(1)} %broadcast_in_dim.131), channel_id=1, replica_groups=mesh['x'=4,'y'=8,'c'=2,'zh'=4,'zl'=2] {'y'}, dimensions={0} | all-to-all | bytes 524288 | tf_op jit(solution)/shard_map/all_to_all | solution.py:66
  101.1 14.6 %all_to_all.26 = bf16[4,8,8,2048]{3,2,1,0:T(8,128)(2,1)S(1)} all-to-all(bf16[4,8,8,2048]{3,2,1,0:T(8,128)(2,1)S(1)} %broadcast_in_dim.132), channel_id=1, replica_groups=mesh['x'=4,'y'=8,'c'=2,'zh'=4,'zl'=2] {'x'}, dimensions={0} | all-to-all | bytes 2097152 | tf_op jit(solution)/shard_map/all_to_all | solution.py:66
  115.7 5.8 %collective-permute-start.4 = (bf16[256,2048]{1,0:T(8,128)(2,1)S(1)}, bf16[256,2048]{1,0:T(8,128)(2,1)S(1)}, u32[]{:S(2)}, u32[]{:S(2)}) collective-permute-start(bf16[256,2048]{1,0:T(8,128)(2,1)S(1)} %bitcast.37), channel_id=1, source_target_pairs={{0,8},{8,0},{1,9},{9,1},{2,10},{10,2},{3,11},{11,3},{4,12},{12,4},... | collective-permute-start | bytes 3145736 | tf_op jit(solution)/shard_map/ppermute | solution.py:222
  121.6 0.8 shard_map.104.refs_0_
  122.4 1.3 %collective-permute-done.4.rows_ref = bf16[256,2048]{1,0:T(8,128)(2,1)S(1)} collective-permute-done((bf16[256,2048]{1,0:T(8,128)(2,1)S(1)}, bf16[256,2048]{1,0:T(8,128)(2,1)S(1)}, u32[]{:S(2)}, u32[]{:S(2)}) %collective-permute-start.4) | collective-permute-done | bytes 1048608 | tf_op jit(solution)/shard_map/ppermute | solution.py:222
  123.7 1.6 %shard_map.105 = bf16[128,4096]{1,0:T(8,128)(2,1)} custom-call(s32[128,1]{1,0:T(8,128)S(1)} %copy.28.target_ref, s32[1,256]{1,0:T(1,128)S(1)} %get-tuple-element.22.key_ref, bf16[256,2048]{1,0:T(8,128)(2,1)S(1)} %collective-permute-done.4.rows_ref, bf16[128,4096]{1,0:T(8,128)(2,1)S(1)} %shard_map.104.refs_0_), custom_call_target="tpu_custom_call" | custom-call | flops 268435456 | bytes 2097152 | tf_op jit(solution)/shard_map/pallas_call | solution.py:148
  (51 shorter events, 1.5 us)
Async XLA Ops:
  0.6 24.2 %copy-start.4 = (s32[8,80]{1,0:T(8,128)S(1)}, s32[8,80]{1,0:T(8,128)}, u32[]{:S(2)}) copy-start(s32[8,80]{1,0:T(8,128)} %param.9) | copy-start | bytes 7684
  0.6 24.2 %copy-start.3 = (s32[8,80]{1,0:T(8,128)S(1)}, s32[8,80]{1,0:T(8,128)}, u32[]{:S(2)}) copy-start(s32[8,80]{1,0:T(8,128)} %param.10) | copy-start | bytes 7684
  2.4 22.8 %all-to-all-start = ((bf16[4,512,128]{2,1,0:T(8,128)(2,1)}), bf16[4,512,128]{2,1,0:T(8,128)(2,1)S(1)}, u32[]{:S(2)}, u32[]{:S(2)}) async-start(bf16[4,512,128]{2,1,0:T(8,128)(2,1)} %broadcast_in_dim.124), calls=%async_computation | async-start | bytes 1048576 | tf_op jit(solution)/shard_map/all_to_all | solution.py:66
  14.3 21.5 %collective-permute-start.2 = (bf16[512,256]{1,0:T(8,128)(2,1)S(1)}, bf16[512,256]{1,0:T(8,128)(2,1)S(1)}, u32[]{:S(2)}, u32[]{:S(2)}) collective-permute-start(bf16[512,256]{1,0:T(8,128)(2,1)S(1)} %get-tuple-element.12), channel_id=1, source_target_pairs={{0,8},{8,0},{1,9},{9,1},{2,10},{10,2},{3,11},{11,3},{4,12},{12,4},... | collective-permute-start | bytes 786440 | tf_op jit(solution)/shard_map/ppermute | solution.py:177
  17.2 18.7 %collective-permute-start.3 = (bf16[512,256]{1,0:T(8,128)(2,1)S(1)}, bf16[512,256]{1,0:T(8,128)(2,1)S(1)}, u32[]{:S(2)}, u32[]{:S(2)}) collective-permute-start(bf16[512,256]{1,0:T(8,128)(2,1)S(1)} %get-tuple-element.12), channel_id=1, source_target_pairs={{0,9},{1,10},{2,11},{3,12},{4,13},{5,14},{6,15},{7,8},{8,7},{9,0},... | collective-permute-start | bytes 786440 | tf_op jit(solution)/shard_map/ppermute | solution.py:177
  22.9 11.9 %collective-permute-start = (bf16[512,256]{1,0:T(8,128)(2,1)S(1)}, bf16[512,256]{1,0:T(8,128)(2,1)S(1)}, u32[]{:S(2)}, u32[]{:S(2)}) collective-permute-start(bf16[512,256]{1,0:T(8,128)(2,1)S(1)} %get-tuple-element.13.own_ref), channel_id=1, source_target_pairs={{0,7},{1,0},{2,1},{3,2},{4,3},{5,4},{6,5},{7,6},{8,9},{9,10},{10,1... | collective-permute-start | bytes 786440 | tf_op jit(solution)/shard_map/ppermute | solution.py:176
  25.3 10.6 %collective-permute-start.1 = (bf16[4,512,128]{2,1,0:T(8,128)(2,1)S(1)}, bf16[4,512,128]{2,1,0:T(8,128)(2,1)S(1)}, u32[]{:S(2)}, u32[]{:S(2)}) collective-permute-start(bf16[4,512,128]{2,1,0:T(8,128)(2,1)S(1)} %all-to-all-done.cot_ref), channel_id=1, source_target_pairs={{0,8},{8,0},{1,9},{9,1},{2,10},{10,2},{3,11},{11,3},{4,12},{12,4},... | collective-permute-start | bytes 1572872 | tf_op jit(solution)/shard_map/ppermute | solution.py:178
  39.6 31.1 %copy-start = (f32[1,1,4,4096]{3,2,1,0:T(4,128)S(1)}, f32[1,1,4,4096]{3,2,1,0:T(4,128)}, u32[]{:S(2)}) copy-start(f32[1,1,4,4096]{3,2,1,0:T(4,128)} %param.13) | copy-start | bytes 196612
  39.6 18.7 %all-to-all-start.1 = ((f16[4,64,8,256]{3,2,1,0:T(8,128)(2,1)}), f16[4,64,8,256]{3,2,1,0:T(8,128)(2,1)S(1)}, u32[]{:S(2)}, u32[]{:S(2)}) async-start(f16[4,64,8,256]{3,2,1,0:T(8,128)(2,1)} %bitcast.7), calls=%async_computation.1 | async-start | bytes 2097152 | tf_op jit(solution)/shard_map/all_to_all | solution.py:200
  59.1 26.7 %copy-start.2 = (f32[1,1,2]{2,1,0:T(1,128)S(1)}, f32[1,1,2]{2,1,0:T(1,128)}, u32[]{:S(2)}) copy-start(f32[1,1,2]{2,1,0:T(1,128)} %param.12) | copy-start | bytes 28
  59.1 27.4 %copy-start.1 = (f32[1,1,4,4096]{3,2,1,0:T(4,128)S(1)}, f32[1,1,4,4096]{3,2,1,0:T(4,128)}, u32[]{:S(2)}) copy-start(f32[1,1,4,4096]{3,2,1,0:T(4,128)} %param.11) | copy-start | bytes 196612
  59.1 25.8 %all-to-all-start.2 = ((f16[64,8,256]{2,1,0:T(8,128)(2,1)}), f16[64,8,256]{2,1,0:T(8,128)(2,1)S(1)}, u32[]{:S(2)}, u32[]{:S(2)}) async-start(f16[64,8,256]{2,1,0:T(8,128)(2,1)} %convert_element_type.38), calls=%async_computation.2 | async-start | bytes 524288 | tf_op jit(solution)/shard_map/all_to_all | solution.py:202
  115.7 8.1 %collective-permute-start.4 = (bf16[256,2048]{1,0:T(8,128)(2,1)S(1)}, bf16[256,2048]{1,0:T(8,128)(2,1)S(1)}, u32[]{:S(2)}, u32[]{:S(2)}) collective-permute-start(bf16[256,2048]{1,0:T(8,128)(2,1)S(1)} %bitcast.37), channel_id=1, source_target_pairs={{0,8},{8,0},{1,9},{9,1},{2,10},{10,2},{3,11},{11,3},{4,12},{12,4},... | collective-permute-start | bytes 3145736 | tf_op jit(solution)/shard_map/ppermute | solution.py:222

commit v5 on v4

--- a/solution.py
+++ b/solution.py
@@ -38,24 +38,60 @@
     return row_owner * capacity + row_slot, row_rank
 
 
-def adam_rows(grad_slots, moment, second, master, assign, filled):
-    width = grad_slots.shape[-1]
-    row_squares = jnp.sum(grad_slots * grad_slots, axis=-1)
-    block_sums = jnp.sum(assign * row_squares[None, :], axis=-1)
-    block_counts = jnp.sum(assign, axis=-1) * width
-    block_used = block_counts > 0.0
-    block_mean = block_sums / jnp.maximum(block_counts, 1.0)
-    second_new = jnp.where(block_used, beta_two * second + (1.0 - beta_two) * block_mean, 0.0)
-    slot_second = jnp.sum(assign * second_new[:, None], axis=0)
-    slot_second = jnp.where(filled, slot_second, 1.0)
-    moment_new = jnp.where(
-        filled[..., None], beta_one * moment + (1.0 - beta_one) * grad_slots, 0.0
-    )
-    update = moment_new / fix_one / (jnp.sqrt(slot_second / fix_two)[..., None] + epsilon)
-    master_new = jnp.where(
-        filled[..., None], master - learn_rate * (update + decay_rate * master), 0.0
-    )
-    return (moment_new, second_new, master_new)
+def adam_kernel(side_ref, rank_ref, sums_ref, moment_ref, second_ref, master_ref, *outs):
+    moment_out, second_out, master_out, rows_out = outs
+    even = side_ref[0] == 0
+    capacity, width = moment_ref.shape
+    half = sums_ref.shape[-1]
+    blocks = width // (2 * half)
+    low = lambda j: sums_ref[0, j // 2, j % 2]
+    high = lambda j: sums_ref[1, j // 2, 1 - j % 2]
+    slots = lax.broadcasted_iota(jnp.int32, (capacity, 1), 0)
+    rank = sum(jnp.where(slots == slot, rank_ref[slot], 0) for slot in range(capacity))
+    grads = []
+    for block in range(blocks):
+        grads.append(jnp.where(even, low(block), low((block - 1) % blocks)))
+        grads.append(jnp.where(even, high((block + 1) % blocks), high(block)))
+    squares = sum(jnp.sum(grad * grad, axis=1, keepdims=True) for grad in grads)
+    slot_second = jnp.ones((capacity, 1), jnp.float32)
+    for slot in range(2):
+        here = rank == slot
+        count = jnp.sum(jnp.where(here, float(width), 0.0), axis=0, keepdims=True)
+        mean = jnp.sum(jnp.where(here, squares, 0.0), axis=0, keepdims=True) / jnp.maximum(count, 1.0)
+        fresh = beta_two * second_ref[:, slot : slot + 1] + (1.0 - beta_two) * mean
+        fresh = jnp.where(count > 0.0, fresh, 0.0)
+        second_out[:, slot : slot + 1] = fresh
+        slot_second = jnp.where(here, fresh, slot_second)
+    filled = rank >= 0
+    scale = 1.0 / (fix_one * (jnp.sqrt(slot_second / fix_two) + epsilon))
+    for part, grad in enumerate(grads):
+        span = slice(part * half, (part + 1) * half)
+        moment = jnp.where(filled, beta_one * moment_ref[:, span] + (1.0 - beta_one) * grad, 0.0)
+        master = master_ref[:, span]
+        master = master - learn_rate * (moment * scale + decay_rate * master)
+        master = jnp.where(filled, master, 0.0)
+        moment_out[:, span] = moment
+        master_out[:, span] = master
+        piece, place = divmod(part * half, width // CUT)
+        rows_out[piece * capacity : (piece + 1) * capacity, place : place + half] = master
+
+
+def adam_rows(side, rank, sums, moment, second, master):
+    capacity, width = moment.shape
+    shape = lambda *dims: jax.ShapeDtypeStruct(dims, jnp.float32)
+    vmem = pl.BlockSpec(memory_space=pltpu.VMEM)
+    return pl.pallas_call(
+        adam_kernel,
+        in_specs=[pl.BlockSpec(memory_space=pltpu.SMEM)] * 2 + [vmem] * 4,
+        out_specs=[vmem] * 4,
+        out_shape=[
+            shape(capacity, width),
+            shape(1, 2),
+            shape(capacity, width),
+            shape(capacity * CUT, width // CUT),
+        ],
+        compiler_params=pltpu.CompilerParams(vmem_limit_bytes=32 * 2**20),
+    )(side[None], rank, sums, moment, second[None], master)
 
 
 SWAP = [(0, 1), (1, 0)]
@@ -153,7 +189,7 @@
         out_shape=jax.ShapeDtypeStruct((HD, CUT * piece), jnp.bfloat16),
         compiler_params=PARAMS,
         cost_estimate=cost(2 * CUT * HD * count * piece, 2 * 2**20),
-    )(target[:, None], key[None, :], rows, *placed)
+    )(target, key, rows, *placed)
 
 
 def body(activations, cotangent, block_start, block_owner, first_moment, block_second, master_rows):
@@ -167,6 +203,13 @@
     half = activations.shape[1] // 2
 
     cot_here = copies_to_all(cotangent, "zh")
+    def of_side(table):
+        return lax.dynamic_index_in_dim(table.reshape(pairs, PAIR, -1), side, 1, keepdims=False)
+
+    target, row_rank = jax.vmap(partial(block_tables, capacity=capacity))(
+        of_side(block_start), of_side(block_owner)
+    )
+    target, activations = lax.optimization_barrier((target, activations))
     keep = lax.dynamic_slice_in_dim(activations, core * half, half, 1)
     give = lax.dynamic_slice_in_dim(activations, (1 - core) * half, half, 1)
     depth = PAIR * pairs
@@ -177,56 +220,38 @@
     act_other = (lax.ppermute(give, "c", SWAP), lax.ppermute(give, ("c", "zh", "zl"), cross))
     cot_other = lax.ppermute(cot_here, "c", SWAP)
 
-    def of_side(table):
-        return lax.dynamic_index_in_dim(table.reshape(pairs, PAIR, -1), side, 1, keepdims=False)
-
-    target, row_rank = jax.vmap(partial(block_tables, capacity=capacity))(
-        of_side(block_start), of_side(block_owner)
-    )
     target_here = lax.dynamic_index_in_dim(target, pair, 0, keepdims=False)
     rank_here = lax.dynamic_index_in_dim(row_rank, pair, 0, keepdims=False)
     slot_ids = owner_here * capacity + jnp.arange(capacity, dtype=jnp.int32)
     mine = slot_ids[:, None] == target_here[None, :]
-    filled_here = jnp.any(mine, axis=1)
-    slot_rank = jnp.sum(jnp.where(mine, rank_here[None, :], 0), axis=1)
-    assign_here = filled_here[None, :] & (
-        slot_rank[None, :] == jnp.arange(2, dtype=jnp.int32)[:, None]
-    )
+    rank = jnp.max(jnp.where(mine, rank_here[None, :], -1), axis=1)
+    row = jnp.arange(chips * capacity * CUT, dtype=jnp.int32)
+    from_chip, cut, slot = row // (capacity * CUT), row // capacity % CUT, row % capacity
+    key_here = ((from_chip * nc + core) * capacity + slot) * CUT + cut
+    key_other = ((from_chip * nc + 1 - core) * capacity + slot) * CUT + cut
 
     send = padded_gradient(
         target, cot_here, cot_other, act_here, act_other, chips, nc, capacity
     ).astype(jnp.float16)
     send = send.reshape(nx, ny * nc * pairs, 2 * capacity, half)
+    send, target_here, rank, key_here, key_other = lax.optimization_barrier(
+        (send, target_here[:, None], rank, key_here[None, :], key_other[None, :])
+    )
     got = lax.all_to_all(send, "x", 0, 0, tiled=True)
     send = jnp.sum(got.astype(jnp.float32), axis=0).astype(jnp.float16)
     got = lax.all_to_all(send, ("y", "c", "zh"), 0, 0, tiled=True)
     got = got.reshape(ny, nc, pairs, 2, capacity, half)
     summed = jnp.sum(got.astype(jnp.float32), axis=0) * 2.0
-    lower = summed[0].reshape(2 * pairs, capacity, half)
-    upper = summed[1, :, ::-1].reshape(2 * pairs, capacity, half)
-    lower = jnp.where(side == 0, lower, jnp.roll(lower, 1, 0))
-    upper = jnp.where(side == 0, jnp.roll(upper, -1, 0), upper)
-    grad_slots = jnp.stack([lower, upper], axis=1)
-    grad_slots = jnp.transpose(grad_slots, (2, 0, 1, 3)).reshape(capacity, width)
-    moment_new, second_new, master_new = adam_rows(
-        grad_slots,
-        first_moment[0, 0],
-        block_second[0, 0],
-        master_rows[0, 0],
-        assign_here.astype(jnp.float32),
-        filled_here,
-    )
-
-    low = master_new.astype(jnp.bfloat16).reshape(capacity * CUT, width // CUT)
-    low = copies_to_all(copies_to_all(low, "y"), "x").reshape(-1, width // CUT)
+    moment_new, second_new, master_new, low = adam_rows(
+        side, rank, summed, first_moment[0, 0], block_second[0, 0], master_rows[0, 0]
+    )
+
+    low = copies_to_all(copies_to_all(low.astype(jnp.bfloat16), "y"), "x")
+    low = low.reshape(-1, width // CUT)
     low_other = lax.ppermute(low, "c", SWAP)
-    row = jnp.arange(low.shape[0], dtype=jnp.int32)
-    from_chip, piece = row // (capacity * CUT), row % (capacity * CUT)
-    key_here = (from_chip * nc + core) * capacity * CUT + piece
-    key_other = (from_chip * nc + 1 - core) * capacity * CUT + piece
     placed = place_rows(target_here, key_here, low)
     new_weight = place_rows(target_here, key_other, low_other, placed)
-    return (new_weight, moment_new[None, None], second_new[None, None], master_new[None, None])
+    return (new_weight, moment_new[None, None], second_new[None], master_new[None, None])
 
 
 def solution(mesh):

time: 126 us -> 123 us (0.976)
  blocking collectives: 28 us -> 72 us
  waiting for transfers between devices: 33.6 us -> 5.14 us
  starting transfers between devices: 47.8 us -> 32.4 us
  other arithmetic: 5.3 us -> 1.64 us
  Pallas kernels: 5.88 us -> 7.36 us
    all_to_all x0 -> x2, blocking collectives: none -> 43.9 us  [the longest x1 25.6 us: body(): got = lax.all_to_all(send, ('y', 'c', 'zh'), 0, 0, tiled=True)]
    all_to_all x2 -> x0, waiting for transfers between devices: 28.6 us -> none  [the longest x1 14.6 us: body(): got = lax.all_to_all(send, 'x', 0, 0, tiled=True)]
    all_to_all x2 -> x0, starting transfers between devices: 15.2 us -> none  [the longest x1 11.1 us: body(): got = lax.all_to_all(send, ('y', 'c', 'zh'), 0, 0, tiled=True)]
    pallas_call x0 -> x1, Pallas kernels: none -> 1.48 us  [adam_rows(): pl.pallas_call(adam_kernel, in_specs=[pl.BlockSpec(memory_space=pltpu.SME...]
    select_n x5 -> x0, other arithmetic: 1.32 us -> none  [the longest x1 0.76 us: adam_rows(): jnp.where(filled[..., None], master - learn_rate * (update + decay_rate *...]
  transfers between devices with their start and end apart: 8 -> 6, of which waited for: 4 -> 2; matrix products, arithmetic and copies ran while one was open for 2% -> 2% of each run, Pallas kernels for 2% -> 2%
where the time goes in v5:
time: 123 us; the launch traced here: 122 us
  blocking collectives  72 us (59%)
  starting transfers between devices  32.4 us (26%)
  Pallas kernels  7.36 us (6%)
  waiting for transfers between devices  5.14 us (4%)
  local copies, waits for them, and re-layouts  3.02 us (2%)
  other arithmetic  1.64 us (1%)
    all_to_all x2, blocking collectives, copies_to_all(): lax.all_to_all(jnp.broadcast_to(block[None], (count,) + block.shape), axi...  28.1 us
    all_to_all x1, blocking collectives, body(): got = lax.all_to_all(send, ('y', 'c', 'zh'), 0, 0, tiled=True)  25.6 us
    all_to_all x1, blocking collectives, body(): got = lax.all_to_all(send, 'x', 0, 0, tiled=True)  18.4 us
    all_to_all x1, starting transfers between devices, copies_to_all(): lax.all_to_all(jnp.broadcast_to(block[None], (count,) + block.shape), axi...  10.8 us
    ppermute x1, starting transfers between devices, body(): lax.ppermute(give, ('c', 'zh', 'zl'), cross)  6.61 us
    ppermute x1, starting transfers between devices, body(): low_other = lax.ppermute(low, 'c', SWAP)  5.75 us
    ppermute x1, starting transfers between devices, body(): cot_other = lax.ppermute(cot_here, 'c', SWAP)  5.32 us
    ppermute x1, waiting for transfers between devices, body(): act_here = (keep, lax.ppermute(keep, ('c', 'zh', 'zl'), same))  3.77 us
  transfers between devices with their start and end apart: 6, of which 2 were waited for; matrix products, arithmetic and copies ran while one was open for 2% of the time, Pallas kernels for 2%

profile of v5, /device:TPU:1, one launch (start us, length us, event | category | flops | bytes accessed | tf_op | source)
XLA Modules:
  0.0 122.5 jit_solution(14690939696740012194)
XLA Ops:
  0.6 1.8 %broadcast_in_dim.92 = bf16[4,512,128]{2,1,0:T(8,128)(2,1)} broadcast(bf16[512,128]{1,0:T(8,128)(2,1)} %param.8), dimensions={1,2} | broadcast | bytes 655360 | tf_op jit(solution)/shard_map/broadcast_in_dim | solution.py:102
  2.5 10.8 %all-to-all-start = ((bf16[4,512,128]{2,1,0:T(8,128)(2,1)}), bf16[4,512,128]{2,1,0:T(8,128)(2,1)S(1)}, u32[]{:S(2)}, u32[]{:S(2)}) async-start(bf16[4,512,128]{2,1,0:T(8,128)(2,1)} %broadcast_in_dim.92), calls=%async_computation | async-start | bytes 1048576 | tf_op jit(solution)/shard_map/all_to_all | solution.py:102
  13.3 0.7 constant_dynamic-slice_fusion.4
  14.0 0.1 convert_reduce_fusion.3
  14.2 0.3 convert_reduce_fusion.2
  14.5 0.2 select_reduce_fusion
  14.6 0.2 convert_reduce_fusion.1
  14.9 6.6 %collective-permute-start.3 = (bf16[512,256]{1,0:T(8,128)(2,1)S(1)}, bf16[512,256]{1,0:T(8,128)(2,1)S(1)}, u32[]{:S(2)}, u32[]{:S(2)}) collective-permute-start(bf16[512,256]{1,0:T(8,128)(2,1)S(1)} %get-tuple-element.28), channel_id=1, source_target_pairs={{0,9},{1,10},{2,11},{3,12},{4,13},{5,14},{6,15},{7,8},{8,7},{9,0},... | collective-permute-start | bytes 786440 | tf_op jit(solution)/shard_map/ppermute | solution.py:220
  21.6 1.9 %collective-permute-start.2 = (bf16[512,256]{1,0:T(8,128)(2,1)S(1)}, bf16[512,256]{1,0:T(8,128)(2,1)S(1)}, u32[]{:S(2)}, u32[]{:S(2)}) collective-permute-start(bf16[512,256]{1,0:T(8,128)(2,1)S(1)} %get-tuple-element.28), channel_id=1, source_target_pairs={{0,8},{8,0},{1,9},{9,1},{2,10},{10,2},{3,11},{11,3},{4,12},{12,4},... | collective-permute-start | bytes 786440 | tf_op jit(solution)/shard_map/ppermute | solution.py:220
  23.5 1.9 %collective-permute-start = (bf16[512,256]{1,0:T(8,128)(2,1)S(1)}, bf16[512,256]{1,0:T(8,128)(2,1)S(1)}, u32[]{:S(2)}, u32[]{:S(2)}) collective-permute-start(bf16[512,256]{1,0:T(8,128)(2,1)S(1)} %get-tuple-element.29.own_ref), channel_id=1, source_target_pairs={{0,7},{1,0},{2,1},{3,2},{4,3},{5,4},{6,5},{7,6},{8,9},{9,10},{10,1... | collective-permute-start | bytes 786440 | tf_op jit(solution)/shard_map/ppermute | solution.py:219
  25.4 5.3 %collective-permute-start.1 = (bf16[4,512,128]{2,1,0:T(8,128)(2,1)S(1)}, bf16[4,512,128]{2,1,0:T(8,128)(2,1)S(1)}, u32[]{:S(2)}, u32[]{:S(2)}) collective-permute-start(bf16[4,512,128]{2,1,0:T(8,128)(2,1)S(1)} %all-to-all-done.cot_ref), channel_id=1, source_target_pairs={{0,8},{8,0},{1,9},{9,1},{2,10},{10,2},{3,11},{11,3},{4,12},{12,4},... | collective-permute-start | bytes 1572872 | tf_op jit(solution)/shard_map/ppermute | solution.py:221
  30.8 0.2 select_reduce_fusion.2.rank_ref
  31.0 3.8 %collective-permute-done.near_ref = bf16[512,256]{1,0:T(8,128)(2,1)S(1)} collective-permute-done((bf16[512,256]{1,0:T(8,128)(2,1)S(1)}, bf16[512,256]{1,0:T(8,128)(2,1)S(1)}, u32[]{:S(2)}, u32[]{:S(2)}) %collective-permute-start) | collective-permute-done | bytes 262176 | tf_op jit(solution)/shard_map/ppermute | solution.py:219
  34.8 1.1 shard_map.102.first_ref
  35.9 2.4 %shard_map.103 = f32[32,2,4,8,256]{4,3,2,1,0:T(8,128)S(1)} custom-call(s32[4,1,128]{2,1,0:T(1,128)S(1)} %bitcast.24, f32[4,128,512]{2,1,0:T(8,128)S(1)} %shard_map.102.first_ref, bf16[4,512,128]{2,1,0:T(8,128)(2,1)S(1)} %collective-permute-done.1.cot_ref, bf16[512,256]{1,0:T(8,128)(2,1)S(1)} %collective-permute-done.2.own_ref, ...), custom_call_target="tpu_custom_call" | custom-call | flops 536870912 | bytes 4194304 | tf_op jit(solution)/shard_map/pallas_call | solution.py:160
  38.3 0.3 convert_element_type.29
  38.6 18.4 %all_to_all.25 = f16[4,64,8,256]{3,2,1,0:T(8,128)(2,1)S(1)} all-to-all(f16[4,64,8,256]{3,2,1,0:T(8,128)(2,1)S(1)} %bitcast.26), channel_id=1, replica_groups=mesh['x'=4,'y'=8,'c'=2,'zh'=4,'zl'=2] {'x'}, dimensions={0} | all-to-all | bytes 2097152 | tf_op jit(solution)/shard_map/all_to_all | solution.py:240
  57.0 0.1 convert_reduce_fusion
  57.1 0.0 copy-start
  57.2 0.0 copy-start.2
  57.2 25.6 %all_to_all.26 = f16[64,8,256]{2,1,0:T(8,128)(2,1)S(1)} all-to-all(f16[64,8,256]{2,1,0:T(8,128)(2,1)S(1)} %convert_element_type.32), channel_id=1, replica_groups=mesh['x'=4,'y'=8,'c'=2,'zh'=4,'zl'=2] {'y','c','zh'}, dimensions={0} | all-to-all | bytes 524288 | tf_op jit(solution)/shard_map/all_to_all | solution.py:242
  82.8 0.1 reshape.200
  83.0 0.1 reduce_sum.69
  83.1 1.5 %shard_map.104 = (f32[4,4096]{1,0:T(4,128)}, f32[1,2]{1,0:T(1,128)}, f32[4,4096]{1,0:T(4,128)}, f32[8,2048]{1,0:T(8,128)S(1)}) custom-call(s32[1]{0:T(128)} %bitcast.9.side_ref, s32[4]{0:T(128)S(1)} %select_reduce_fusion.2.rank_ref, f32[2,4,2,4,256]{4,3,2,1,0:T(4,128)S(1)} %broadcast_multiply_fusion.sums_ref, f32[4,4096]{1,0:T(4,128)S(1)} %bitcast.22, ...), custom_call_target="tpu_custom_call" | custom-call | tf_op jit(solution)/shard_map/pallas_call | solution.py:83
  84.6 13.5 %all_to_all.27 = bf16[8,8,2048]{2,1,0:T(8,128)(2,1)S(1)} all-to-all(bf16[8,8,2048]{2,1,0:T(8,128)(2,1)S(1)} %broadcast_in_dim.98), channel_id=1, replica_groups=mesh['x'=4,'y'=8,'c'=2,'zh'=4,'zl'=2] {'y'}, dimensions={0} | all-to-all | bytes 524288 | tf_op jit(solution)/shard_map/all_to_all | solution.py:102
  98.1 0.1 broadcast_in_dim.99
  98.3 14.6 %all_to_all.28 = bf16[4,8,8,2048]{3,2,1,0:T(8,128)(2,1)S(1)} all-to-all(bf16[4,8,8,2048]{3,2,1,0:T(8,128)(2,1)S(1)} %broadcast_in_dim.99), channel_id=1, replica_groups=mesh['x'=4,'y'=8,'c'=2,'zh'=4,'zl'=2] {'x'}, dimensions={0} | all-to-all | bytes 2097152 | tf_op jit(solution)/shard_map/all_to_all | solution.py:102
  112.9 5.8 %collective-permute-start.4 = (bf16[256,2048]{1,0:T(8,128)(2,1)S(1)}, bf16[256,2048]{1,0:T(8,128)(2,1)S(1)}, u32[]{:S(2)}, u32[]{:S(2)}) collective-permute-start(bf16[256,2048]{1,0:T(8,128)(2,1)S(1)} %bitcast.20), channel_id=1, source_target_pairs={{0,8},{8,0},{1,9},{9,1},{2,10},{10,2},{3,11},{11,3},{4,12},{12,4},... | collective-permute-start | bytes 3145736 | tf_op jit(solution)/shard_map/ppermute | solution.py:251
  118.6 0.1 copy.17.target_ref
  118.7 0.8 shard_map.105.refs_0_
  119.5 1.4 %collective-permute-done.4.rows_ref = bf16[256,2048]{1,0:T(8,128)(2,1)S(1)} collective-permute-done((bf16[256,2048]{1,0:T(8,128)(2,1)S(1)}, bf16[256,2048]{1,0:T(8,128)(2,1)S(1)}, u32[]{:S(2)}, u32[]{:S(2)}) %collective-permute-start.4) | collective-permute-done | bytes 1048608 | tf_op jit(solution)/shard_map/ppermute | solution.py:251
  120.9 1.6 %shard_map.106 = bf16[128,4096]{1,0:T(8,128)(2,1)} custom-call(s32[128,1]{1,0:T(8,128)S(1)} %copy.17.target_ref, s32[1,256]{1,0:T(1,128)S(1)} %get-tuple-element.18.key_ref, bf16[256,2048]{1,0:T(8,128)(2,1)S(1)} %collective-permute-done.4.rows_ref, bf16[128,4096]{1,0:T(8,128)(2,1)S(1)} %shard_map.105.refs_0_), custom_call_target="tpu_custom_call" | custom-call | flops 268435456 | bytes 2097152 | tf_op jit(solution)/shard_map/pallas_call | solution.py:184
  (23 shorter events, 0.3 us)
Async XLA Ops:
  0.6 14.3 %copy-start.3 = (bf16[512,512]{1,0:T(8,128)(2,1)S(1)}, bf16[512,512]{1,0:T(8,128)(2,1)}, u32[]{:S(2)}) copy-start(bf16[512,512]{1,0:T(8,128)(2,1)} %param.7) | copy-start | bytes 1572868
  2.5 23.0 %all-to-all-start = ((bf16[4,512,128]{2,1,0:T(8,128)(2,1)}), bf16[4,512,128]{2,1,0:T(8,128)(2,1)S(1)}, u32[]{:S(2)}, u32[]{:S(2)}) async-start(bf16[4,512,128]{2,1,0:T(8,128)(2,1)} %broadcast_in_dim.92), calls=%async_computation | async-start | bytes 1048576 | tf_op jit(solution)/shard_map/all_to_all | solution.py:102
  14.9 21.0 %collective-permute-start.3 = (bf16[512,256]{1,0:T(8,128)(2,1)S(1)}, bf16[512,256]{1,0:T(8,128)(2,1)S(1)}, u32[]{:S(2)}, u32[]{:S(2)}) collective-permute-start(bf16[512,256]{1,0:T(8,128)(2,1)S(1)} %get-tuple-element.28), channel_id=1, source_target_pairs={{0,9},{1,10},{2,11},{3,12},{4,13},{5,14},{6,15},{7,8},{8,7},{9,0},... | collective-permute-start | bytes 786440 | tf_op jit(solution)/shard_map/ppermute | solution.py:220
  21.6 14.4 %collective-permute-start.2 = (bf16[512,256]{1,0:T(8,128)(2,1)S(1)}, bf16[512,256]{1,0:T(8,128)(2,1)S(1)}, u32[]{:S(2)}, u32[]{:S(2)}) collective-permute-start(bf16[512,256]{1,0:T(8,128)(2,1)S(1)} %get-tuple-element.28), channel_id=1, source_target_pairs={{0,8},{8,0},{1,9},{9,1},{2,10},{10,2},{3,11},{11,3},{4,12},{12,4},... | collective-permute-start | bytes 786440 | tf_op jit(solution)/shard_map/ppermute | solution.py:220
  23.5 11.3 %collective-permute-start = (bf16[512,256]{1,0:T(8,128)(2,1)S(1)}, bf16[512,256]{1,0:T(8,128)(2,1)S(1)}, u32[]{:S(2)}, u32[]{:S(2)}) collective-permute-start(bf16[512,256]{1,0:T(8,128)(2,1)S(1)} %get-tuple-element.29.own_ref), channel_id=1, source_target_pairs={{0,7},{1,0},{2,1},{3,2},{4,3},{5,4},{6,5},{7,6},{8,9},{9,10},{10,1... | collective-permute-start | bytes 786440 | tf_op jit(solution)/shard_map/ppermute | solution.py:219
  25.4 10.5 %collective-permute-start.1 = (bf16[4,512,128]{2,1,0:T(8,128)(2,1)S(1)}, bf16[4,512,128]{2,1,0:T(8,128)(2,1)S(1)}, u32[]{:S(2)}, u32[]{:S(2)}) collective-permute-start(bf16[4,512,128]{2,1,0:T(8,128)(2,1)S(1)} %all-to-all-done.cot_ref), channel_id=1, source_target_pairs={{0,8},{8,0},{1,9},{9,1},{2,10},{10,2},{3,11},{11,3},{4,12},{12,4},... | collective-permute-start | bytes 1572872 | tf_op jit(solution)/shard_map/ppermute | solution.py:221
  57.1 26.0 %copy-start = (f32[1,1,4,4096]{3,2,1,0:T(4,128)S(1)}, f32[1,1,4,4096]{3,2,1,0:T(4,128)}, u32[]{:S(2)}) copy-start(f32[1,1,4,4096]{3,2,1,0:T(4,128)} %param.11) | copy-start | bytes 196612
  57.1 26.0 %copy-start.1 = (f32[1,1,4,4096]{3,2,1,0:T(4,128)S(1)}, f32[1,1,4,4096]{3,2,1,0:T(4,128)}, u32[]{:S(2)}) copy-start(f32[1,1,4,4096]{3,2,1,0:T(4,128)} %param.13) | copy-start | bytes 196612
  57.2 26.0 %copy-start.2 = (f32[1,1,2]{2,1,0:T(1,128)S(1)}, f32[1,1,2]{2,1,0:T(1,128)}, u32[]{:S(2)}) copy-start(f32[1,1,2]{2,1,0:T(1,128)} %param.12) | copy-start | bytes 28
  112.9 8.0 %collective-permute-start.4 = (bf16[256,2048]{1,0:T(8,128)(2,1)S(1)}, bf16[256,2048]{1,0:T(8,128)(2,1)S(1)}, u32[]{:S(2)}, u32[]{:S(2)}) collective-permute-start(bf16[256,2048]{1,0:T(8,128)(2,1)S(1)} %bitcast.20), channel_id=1, source_target_pairs={{0,8},{8,0},{1,9},{9,1},{2,10},{10,2},{3,11},{11,3},{4,12},{12,4},... | collective-permute-start | bytes 3145736 | tf_op jit(solution)/shard_map/ppermute | solution.py:251

commit v6 on v5

--- a/solution.py
+++ b/solution.py
@@ -44,8 +44,8 @@
     capacity, width = moment_ref.shape
     half = sums_ref.shape[-1]
     blocks = width // (2 * half)
-    low = lambda j: sums_ref[0, j // 2, j % 2]
-    high = lambda j: sums_ref[1, j // 2, 1 - j % 2]
+    low = lambda j: sums_ref[j // 2, 0, j % 2]
+    high = lambda j: sums_ref[j // 2, 1, 1 - j % 2]
     slots = lax.broadcasted_iota(jnp.int32, (capacity, 1), 0)
     rank = sum(jnp.where(slots == slot, rank_ref[slot], 0) for slot in range(capacity))
     grads = []
@@ -119,12 +119,13 @@
 
 
 def padded_kernel(target_ref, first_ref, cot_ref, own_ref, near_ref, out_ref):
-    chips, cores, _, rows, half = out_ref.shape
-    capacity = rows // 2
-    row = lax.broadcasted_iota(jnp.int32, (chips * cores * rows, HD), 0)
-    slot = row // rows * capacity + row % capacity
-    taken = slot == target_ref[0]
-    padded = jnp.zeros((chips * cores * rows, half), jnp.float32)
+    lines, spots, _, rows, half = out_ref.shape
+    count, cores, capacity = lines * spots * rows, GRID[2], rows // 2
+    row = lax.broadcasted_iota(jnp.int32, (count, HD), 0)
+    line, spot = row // (spots * rows), row // rows % spots
+    owner = (line // cores * spots + spot) * cores + line % cores
+    taken = owner * capacity + row % capacity == target_ref[0]
+    padded = jnp.zeros((count, half), jnp.float32)
     for part, act_ref in enumerate((own_ref, near_ref)):
         grad = first_ref[0, :, part * half : (part + 1) * half] + lax.dot_general(
             cot_ref[0], act_ref[...], TOKEN_DOT, preferred_element_type=jnp.float32
@@ -137,10 +138,10 @@
             jnp.concatenate([high, low], axis=0),
             preferred_element_type=jnp.float32,
         )
-    out_ref[:, :, 0] = padded.reshape(chips, cores, rows, half)
-
-
-def padded_gradient(target, cot_here, cot_other, act_here, act_other, chips, cores, capacity):
+    out_ref[:, :, 0] = padded.reshape(lines, spots, rows, half)
+
+
+def padded_gradient(target, cot_here, cot_other, act_here, act_other, lines, spots, capacity):
     heads, tokens, _ = cot_here.shape
     half = act_here[0].shape[1]
     features = 2 * half
@@ -161,8 +162,8 @@
         padded_kernel,
         grid=(heads,),
         in_specs=[pl.BlockSpec((1, 1, HD), lambda h: (h, 0, 0)), grad, cot, act, act],
-        out_specs=pl.BlockSpec((chips, cores, 1) + tail, lambda h: (0, 0, h, 0, 0)),
-        out_shape=jax.ShapeDtypeStruct((chips, cores, heads) + tail, jnp.float32),
+        out_specs=pl.BlockSpec((lines, spots, 1) + tail, lambda h: (0, 0, h, 0, 0)),
+        out_shape=jax.ShapeDtypeStruct((lines, spots, heads) + tail, jnp.float32),
         compiler_params=PARAMS,
         cost_estimate=cost(4 * heads * tokens * HD * features, 4 * 2**20),
     )(target[:, None, :], first, cot_other, *act_other)
@@ -231,16 +232,17 @@
     key_other = ((from_chip * nc + 1 - core) * capacity + slot) * CUT + cut
 
     send = padded_gradient(
-        target, cot_here, cot_other, act_here, act_other, chips, nc, capacity
+        target, cot_here, cot_other, act_here, act_other, nx * nc, ny, capacity
     ).astype(jnp.float16)
-    send = send.reshape(nx, ny * nc * pairs, 2 * capacity, half)
+    send = send.reshape(nx * nc, ny * pairs, 2 * capacity, half)
     send, target_here, rank, key_here, key_other = lax.optimization_barrier(
         (send, target_here[:, None], rank, key_here[None, :], key_other[None, :])
     )
-    got = lax.all_to_all(send, "x", 0, 0, tiled=True)
+    got = lax.all_to_all(send, ("x", "c"), 0, 0, tiled=True)
+    got = got.reshape(nx, nc, ny * pairs, 2 * capacity, half)
     send = jnp.sum(got.astype(jnp.float32), axis=0).astype(jnp.float16)
-    got = lax.all_to_all(send, ("y", "c", "zh"), 0, 0, tiled=True)
-    got = got.reshape(ny, nc, pairs, 2, capacity, half)
+    got = lax.all_to_all(jnp.swapaxes(send, 0, 1), ("y", "zh"), 0, 0, tiled=True)
+    got = got.reshape(ny, pairs, nc, 2, capacity, half)
     summed = jnp.sum(got.astype(jnp.float32), axis=0) * 2.0
     moment_new, second_new, master_new, low = adam_rows(
         side, rank, summed, first_moment[0, 0], block_second[0, 0], master_rows[0, 0]

time: 123 us -> 120 us (0.976)
  blocking collectives: 72 us -> 68.2 us
    all_to_all x2, blocking collectives: 43.9 us -> 40.5 us  [the longest x1 21.3 us: body(): lax.all_to_all(jnp.swapaxes(send, 0, 1), ('y', 'zh'), 0, 0, tiled=True)]
where the time goes in v6:
time: 120 us
  blocking collectives  68.2 us (57%)
  starting transfers between devices  33.3 us (28%)
  Pallas kernels  7.43 us (6%)
  waiting for transfers between devices  5.14 us (4%)
  local copies, waits for them, and re-layouts  3.07 us (3%)
  other arithmetic  1.68 us (1%)
    all_to_all x2, blocking collectives, copies_to_all(): lax.all_to_all(jnp.broadcast_to(block[None], (count,) + block.shape), axi...  27.7 us
    all_to_all x1, blocking collectives, body(): lax.all_to_all(jnp.swapaxes(send, 0, 1), ('y', 'zh'), 0, 0, tiled=True)  21.3 us
    all_to_all x1, blocking collectives, body(): got = lax.all_to_all(send, ('x', 'c'), 0, 0, tiled=True)  19.3 us
    all_to_all x1, starting transfers between devices, copies_to_all(): lax.all_to_all(jnp.broadcast_to(block[None], (count,) + block.shape), axi...  10.8 us
    ppermute x1, starting transfers between devices, body(): low_other = lax.ppermute(low, 'c', SWAP)  6.64 us
    ppermute x1, starting transfers between devices, body(): lax.ppermute(give, ('c', 'zh', 'zl'), cross)  6.61 us
    ppermute x1, starting transfers between devices, body(): cot_other = lax.ppermute(cot_here, 'c', SWAP)  5.32 us
    ppermute x1, waiting for transfers between devices, body(): act_here = (keep, lax.ppermute(keep, ('c', 'zh', 'zl'), same))  3.77 us
  transfers between devices with their start and end apart: 6, of which 2 were waited for; matrix products, arithmetic and copies ran while one was open for 2% of the time, Pallas kernels for 2%

profile of v6, /device:TPU:1, one launch (start us, length us, event | category | flops | bytes accessed | tf_op | source)
XLA Modules:
  0.0 119.7 jit_solution(3164176014517941290)
XLA Ops:
  0.6 1.8 %broadcast_in_dim.92 = bf16[4,512,128]{2,1,0:T(8,128)(2,1)} broadcast(bf16[512,128]{1,0:T(8,128)(2,1)} %param.8), dimensions={1,2} | broadcast | bytes 655360 | tf_op jit(solution)/shard_map/broadcast_in_dim | solution.py:102
  2.5 10.8 %all-to-all-start = ((bf16[4,512,128]{2,1,0:T(8,128)(2,1)}), bf16[4,512,128]{2,1,0:T(8,128)(2,1)S(1)}, u32[]{:S(2)}, u32[]{:S(2)}) async-start(bf16[4,512,128]{2,1,0:T(8,128)(2,1)} %broadcast_in_dim.92), calls=%async_computation | async-start | bytes 1048576 | tf_op jit(solution)/shard_map/all_to_all | solution.py:102
  13.3 0.7 constant_dynamic-slice_fusion.4
  14.0 0.1 convert_reduce_fusion.3
  14.2 0.3 convert_reduce_fusion.2
  14.5 0.2 select_reduce_fusion
  14.6 0.2 convert_reduce_fusion.1
  14.9 6.6 %collective-permute-start.3 = (bf16[512,256]{1,0:T(8,128)(2,1)S(1)}, bf16[512,256]{1,0:T(8,128)(2,1)S(1)}, u32[]{:S(2)}, u32[]{:S(2)}) collective-permute-start(bf16[512,256]{1,0:T(8,128)(2,1)S(1)} %get-tuple-element.28), channel_id=1, source_target_pairs={{0,9},{1,10},{2,11},{3,12},{4,13},{5,14},{6,15},{7,8},{8,7},{9,0},... | collective-permute-start | bytes 786440 | tf_op jit(solution)/shard_map/ppermute | solution.py:221
  21.6 1.9 %collective-permute-start.2 = (bf16[512,256]{1,0:T(8,128)(2,1)S(1)}, bf16[512,256]{1,0:T(8,128)(2,1)S(1)}, u32[]{:S(2)}, u32[]{:S(2)}) collective-permute-start(bf16[512,256]{1,0:T(8,128)(2,1)S(1)} %get-tuple-element.28), channel_id=1, source_target_pairs={{0,8},{8,0},{1,9},{9,1},{2,10},{10,2},{3,11},{11,3},{4,12},{12,4},... | collective-permute-start | bytes 786440 | tf_op jit(solution)/shard_map/ppermute | solution.py:221
  23.5 1.9 %collective-permute-start = (bf16[512,256]{1,0:T(8,128)(2,1)S(1)}, bf16[512,256]{1,0:T(8,128)(2,1)S(1)}, u32[]{:S(2)}, u32[]{:S(2)}) collective-permute-start(bf16[512,256]{1,0:T(8,128)(2,1)S(1)} %get-tuple-element.29.own_ref), channel_id=1, source_target_pairs={{0,7},{1,0},{2,1},{3,2},{4,3},{5,4},{6,5},{7,6},{8,9},{9,10},{10,1... | collective-permute-start | bytes 786440 | tf_op jit(solution)/shard_map/ppermute | solution.py:220
  25.4 5.3 %collective-permute-start.1 = (bf16[4,512,128]{2,1,0:T(8,128)(2,1)S(1)}, bf16[4,512,128]{2,1,0:T(8,128)(2,1)S(1)}, u32[]{:S(2)}, u32[]{:S(2)}) collective-permute-start(bf16[4,512,128]{2,1,0:T(8,128)(2,1)S(1)} %all-to-all-done.cot_ref), channel_id=1, source_target_pairs={{0,8},{8,0},{1,9},{9,1},{2,10},{10,2},{3,11},{11,3},{4,12},{12,4},... | collective-permute-start | bytes 1572872 | tf_op jit(solution)/shard_map/ppermute | solution.py:222
  30.8 0.2 select_reduce_fusion.2.rank_ref
  31.0 3.8 %collective-permute-done.near_ref = bf16[512,256]{1,0:T(8,128)(2,1)S(1)} collective-permute-done((bf16[512,256]{1,0:T(8,128)(2,1)S(1)}, bf16[512,256]{1,0:T(8,128)(2,1)S(1)}, u32[]{:S(2)}, u32[]{:S(2)}) %collective-permute-start) | collective-permute-done | bytes 262176 | tf_op jit(solution)/shard_map/ppermute | solution.py:220
  34.8 1.1 shard_map.102.first_ref
  35.9 2.5 %shard_map.103 = f32[8,8,4,8,256]{4,3,2,1,0:T(8,128)S(1)} custom-call(s32[4,1,128]{2,1,0:T(1,128)S(1)} %bitcast.30, f32[4,128,512]{2,1,0:T(8,128)S(1)} %shard_map.102.first_ref, bf16[4,512,128]{2,1,0:T(8,128)(2,1)S(1)} %collective-permute-done.1.cot_ref, bf16[512,256]{1,0:T(8,128)(2,1)S(1)} %collective-permute-done.2.own_ref, ...), custom_call_target="tpu_custom_call" | custom-call | flops 536870912 | bytes 4194304 | tf_op jit(solution)/shard_map/pallas_call | solution.py:161
  38.4 0.3 convert_element_type.36
  38.7 19.3 %all_to_all.25 = f16[8,32,8,256]{3,2,1,0:T(8,128)(2,1)S(1)} all-to-all(f16[8,32,8,256]{3,2,1,0:T(8,128)(2,1)S(1)} %bitcast.32), channel_id=1, replica_groups=mesh['x'=4,'y'=8,'c'=2,'zh'=4,'zl'=2] {'x','c'}, dimensions={0} | all-to-all | bytes 2097152 | tf_op jit(solution)/shard_map/all_to_all | solution.py:241
  58.0 0.1 convert_reduce_fusion
  58.2 0.0 copy-start.2
  58.3 21.3 %all_to_all.26 = f16[32,2,8,256]{3,2,1,0:T(8,128)(2,1)S(1)} all-to-all(f16[32,2,8,256]{3,2,1,0:T(8,128)(2,1)S(1)} %copy.18), channel_id=1, replica_groups=mesh['x'=4,'y'=8,'c'=2,'zh'=4,'zl'=2] {'y','zh'}, dimensions={0} | all-to-all | bytes 524288 | tf_op jit(solution)/shard_map/all_to_all | solution.py:244
  79.5 0.1 convert_element_type.46
  79.6 0.1 reshape.204
  79.7 0.1 reduce_sum.69
  79.9 1.5 %shard_map.104 = (f32[4,4096]{1,0:T(4,128)}, f32[1,2]{1,0:T(1,128)}, f32[4,4096]{1,0:T(4,128)}, f32[8,2048]{1,0:T(8,128)S(1)}) custom-call(s32[1]{0:T(128)} %bitcast.9.side_ref, s32[4]{0:T(128)S(1)} %select_reduce_fusion.2.rank_ref, f32[4,2,2,4,256]{4,3,2,1,0:T(4,128)S(1)} %broadcast_multiply_fusion.sums_ref, f32[4,4096]{1,0:T(4,128)S(1)} %bitcast.28, ...), custom_call_target="tpu_custom_call" | custom-call | tf_op jit(solution)/shard_map/pallas_call | solution.py:83
  81.4 13.9 %all_to_all.27 = bf16[8,8,2048]{2,1,0:T(8,128)(2,1)S(1)} all-to-all(bf16[8,8,2048]{2,1,0:T(8,128)(2,1)S(1)} %broadcast_in_dim.98), channel_id=1, replica_groups=mesh['x'=4,'y'=8,'c'=2,'zh'=4,'zl'=2] {'y'}, dimensions={0} | all-to-all | bytes 524288 | tf_op jit(solution)/shard_map/all_to_all | solution.py:102
  95.3 0.1 broadcast_in_dim.99
  95.5 13.7 %all_to_all.28 = bf16[4,8,8,2048]{3,2,1,0:T(8,128)(2,1)S(1)} all-to-all(bf16[4,8,8,2048]{3,2,1,0:T(8,128)(2,1)S(1)} %broadcast_in_dim.99), channel_id=1, replica_groups=mesh['x'=4,'y'=8,'c'=2,'zh'=4,'zl'=2] {'x'}, dimensions={0} | all-to-all | bytes 2097152 | tf_op jit(solution)/shard_map/all_to_all | solution.py:102
  109.2 6.6 %collective-permute-start.4 = (bf16[256,2048]{1,0:T(8,128)(2,1)S(1)}, bf16[256,2048]{1,0:T(8,128)(2,1)S(1)}, u32[]{:S(2)}, u32[]{:S(2)}) collective-permute-start(bf16[256,2048]{1,0:T(8,128)(2,1)S(1)} %bitcast.26), channel_id=1, source_target_pairs={{0,8},{8,0},{1,9},{9,1},{2,10},{10,2},{3,11},{11,3},{4,12},{12,4},... | collective-permute-start | bytes 3145736 | tf_op jit(solution)/shard_map/ppermute | solution.py:253
  115.8 0.1 copy.20.target_ref
  115.9 0.8 shard_map.105.refs_0_
  116.7 1.4 %collective-permute-done.4.rows_ref = bf16[256,2048]{1,0:T(8,128)(2,1)S(1)} collective-permute-done((bf16[256,2048]{1,0:T(8,128)(2,1)S(1)}, bf16[256,2048]{1,0:T(8,128)(2,1)S(1)}, u32[]{:S(2)}, u32[]{:S(2)}) %collective-permute-start.4) | collective-permute-done | bytes 1048608 | tf_op jit(solution)/shard_map/ppermute | solution.py:253
  118.1 1.6 %shard_map.106 = bf16[128,4096]{1,0:T(8,128)(2,1)} custom-call(s32[128,1]{1,0:T(8,128)S(1)} %copy.20.target_ref, s32[1,256]{1,0:T(1,128)S(1)} %get-tuple-element.18.key_ref, bf16[256,2048]{1,0:T(8,128)(2,1)S(1)} %collective-permute-done.4.rows_ref, bf16[128,4096]{1,0:T(8,128)(2,1)S(1)} %shard_map.105.refs_0_), custom_call_target="tpu_custom_call" | custom-call | flops 268435456 | bytes 2097152 | tf_op jit(solution)/shard_map/pallas_call | solution.py:185
  (24 shorter events, 0.3 us)
Async XLA Ops:
  0.6 14.3 %copy-start.3 = (bf16[512,512]{1,0:T(8,128)(2,1)S(1)}, bf16[512,512]{1,0:T(8,128)(2,1)}, u32[]{:S(2)}) copy-start(bf16[512,512]{1,0:T(8,128)(2,1)} %param.7) | copy-start | bytes 1572868
  2.5 23.0 %all-to-all-start = ((bf16[4,512,128]{2,1,0:T(8,128)(2,1)}), bf16[4,512,128]{2,1,0:T(8,128)(2,1)S(1)}, u32[]{:S(2)}, u32[]{:S(2)}) async-start(bf16[4,512,128]{2,1,0:T(8,128)(2,1)} %broadcast_in_dim.92), calls=%async_computation | async-start | bytes 1048576 | tf_op jit(solution)/shard_map/all_to_all | solution.py:102
  14.9 21.0 %collective-permute-start.3 = (bf16[512,256]{1,0:T(8,128)(2,1)S(1)}, bf16[512,256]{1,0:T(8,128)(2,1)S(1)}, u32[]{:S(2)}, u32[]{:S(2)}) collective-permute-start(bf16[512,256]{1,0:T(8,128)(2,1)S(1)} %get-tuple-element.28), channel_id=1, source_target_pairs={{0,9},{1,10},{2,11},{3,12},{4,13},{5,14},{6,15},{7,8},{8,7},{9,0},... | collective-permute-start | bytes 786440 | tf_op jit(solution)/shard_map/ppermute | solution.py:221
  21.6 14.4 %collective-permute-start.2 = (bf16[512,256]{1,0:T(8,128)(2,1)S(1)}, bf16[512,256]{1,0:T(8,128)(2,1)S(1)}, u32[]{:S(2)}, u32[]{:S(2)}) collective-permute-start(bf16[512,256]{1,0:T(8,128)(2,1)S(1)} %get-tuple-element.28), channel_id=1, source_target_pairs={{0,8},{8,0},{1,9},{9,1},{2,10},{10,2},{3,11},{11,3},{4,12},{12,4},... | collective-permute-start | bytes 786440 | tf_op jit(solution)/shard_map/ppermute | solution.py:221
  23.5 11.3 %collective-permute-start = (bf16[512,256]{1,0:T(8,128)(2,1)S(1)}, bf16[512,256]{1,0:T(8,128)(2,1)S(1)}, u32[]{:S(2)}, u32[]{:S(2)}) collective-permute-start(bf16[512,256]{1,0:T(8,128)(2,1)S(1)} %get-tuple-element.29.own_ref), channel_id=1, source_target_pairs={{0,7},{1,0},{2,1},{3,2},{4,3},{5,4},{6,5},{7,6},{8,9},{9,10},{10,1... | collective-permute-start | bytes 786440 | tf_op jit(solution)/shard_map/ppermute | solution.py:220
  25.4 10.5 %collective-permute-start.1 = (bf16[4,512,128]{2,1,0:T(8,128)(2,1)S(1)}, bf16[4,512,128]{2,1,0:T(8,128)(2,1)S(1)}, u32[]{:S(2)}, u32[]{:S(2)}) collective-permute-start(bf16[4,512,128]{2,1,0:T(8,128)(2,1)S(1)} %all-to-all-done.cot_ref), channel_id=1, source_target_pairs={{0,8},{8,0},{1,9},{9,1},{2,10},{10,2},{3,11},{11,3},{4,12},{12,4},... | collective-permute-start | bytes 1572872 | tf_op jit(solution)/shard_map/ppermute | solution.py:222
  58.1 21.7 %copy-start = (f32[1,1,4,4096]{3,2,1,0:T(4,128)S(1)}, f32[1,1,4,4096]{3,2,1,0:T(4,128)}, u32[]{:S(2)}) copy-start(f32[1,1,4,4096]{3,2,1,0:T(4,128)} %param.11) | copy-start | bytes 196612
  58.1 21.7 %copy-start.1 = (f32[1,1,4,4096]{3,2,1,0:T(4,128)S(1)}, f32[1,1,4,4096]{3,2,1,0:T(4,128)}, u32[]{:S(2)}) copy-start(f32[1,1,4,4096]{3,2,1,0:T(4,128)} %param.13) | copy-start | bytes 196612
  58.2 21.7 %copy-start.2 = (f32[1,1,2]{2,1,0:T(1,128)S(1)}, f32[1,1,2]{2,1,0:T(1,128)}, u32[]{:S(2)}) copy-start(f32[1,1,2]{2,1,0:T(1,128)} %param.12) | copy-start | bytes 28
  109.2 8.9 %collective-permute-start.4 = (bf16[256,2048]{1,0:T(8,128)(2,1)S(1)}, bf16[256,2048]{1,0:T(8,128)(2,1)S(1)}, u32[]{:S(2)}, u32[]{:S(2)}) collective-permute-start(bf16[256,2048]{1,0:T(8,128)(2,1)S(1)} %bitcast.26), channel_id=1, source_target_pairs={{0,8},{8,0},{1,9},{9,1},{2,10},{10,2},{3,11},{11,3},{4,12},{12,4},... | collective-permute-start | bytes 3145736 | tf_op jit(solution)/shard_map/ppermute | solution.py:253

commit v7 on v6

--- a/solution.py
+++ b/solution.py
@@ -110,63 +110,58 @@
     return pl.CostEstimate(flops=flops, bytes_accessed=moved, transcendentals=0)
 
 
-def first_kernel(cot_ref, own_ref, near_ref, out_ref):
-    half = own_ref.shape[1]
-    for part, act_ref in enumerate((own_ref, near_ref)):
-        out_ref[0, :, part * half : (part + 1) * half] = lax.dot_general(
-            cot_ref[0], act_ref[...], TOKEN_DOT, preferred_element_type=jnp.float32
+def first_kernel(cot_ref, act_ref, out_ref):
+    for head in range(cot_ref.shape[0]):
+        out_ref[head] = lax.dot_general(
+            cot_ref[head], act_ref[...], TOKEN_DOT, preferred_element_type=jnp.float32
         )
 
 
-def padded_kernel(target_ref, first_ref, cot_ref, own_ref, near_ref, out_ref):
-    lines, spots, _, rows, half = out_ref.shape
+def padded_kernel(target_ref, first_ref, here_ref, other_ref, own_ref, near_ref, far_ref, out_ref):
+    lines, spots, heads, rows, half = out_ref.shape
     count, cores, capacity = lines * spots * rows, GRID[2], rows // 2
     row = lax.broadcasted_iota(jnp.int32, (count, HD), 0)
     line, spot = row // (spots * rows), row // rows % spots
     owner = (line // cores * spots + spot) * cores + line % cores
-    taken = owner * capacity + row % capacity == target_ref[0]
-    padded = jnp.zeros((count, half), jnp.float32)
-    for part, act_ref in enumerate((own_ref, near_ref)):
-        grad = first_ref[0, :, part * half : (part + 1) * half] + lax.dot_general(
-            cot_ref[0], act_ref[...], TOKEN_DOT, preferred_element_type=jnp.float32
-        )
-        high = grad.astype(jnp.bfloat16)
-        low = (grad - high.astype(jnp.float32)).astype(jnp.bfloat16)
-        pick = jnp.where(taken & (row // capacity % 2 == part), 0.5, 0.0).astype(jnp.bfloat16)
-        padded += jnp.dot(
-            jnp.concatenate([pick, pick], axis=1),
-            jnp.concatenate([high, low], axis=0),
-            preferred_element_type=jnp.float32,
-        )
-    out_ref[:, :, 0] = padded.reshape(lines, spots, rows, half)
+    slot, part_of = owner * capacity + row % capacity, row // capacity % 2
+    dot = partial(lax.dot_general, dimension_numbers=TOKEN_DOT, preferred_element_type=jnp.float32)
+    for head in range(heads):
+        taken = slot == target_ref[head]
+        own = first_ref[head] + dot(other_ref[head], own_ref[...])
+        near = dot(here_ref[head], near_ref[...]) + dot(other_ref[head], far_ref[...])
+        padded = jnp.zeros((count, half), jnp.float32)
+        for part, grad in enumerate((own, near)):
+            high = grad.astype(jnp.bfloat16)
+            low = (grad - high.astype(jnp.float32)).astype(jnp.bfloat16)
+            pick = jnp.where(taken & (part_of == part), 0.5, 0.0).astype(jnp.bfloat16)
+            padded += jnp.dot(
+                jnp.concatenate([pick, pick], axis=1),
+                jnp.concatenate([high, low], axis=0),
+                preferred_element_type=jnp.float32,
+            )
+        out_ref[:, :, head] = padded.reshape(lines, spots, rows, half)
 
 
 def padded_gradient(target, cot_here, cot_other, act_here, act_other, lines, spots, capacity):
     heads, tokens, _ = cot_here.shape
     half = act_here[0].shape[1]
-    features = 2 * half
-    cot = pl.BlockSpec((1, tokens, HD), lambda h: (h, 0, 0))
-    act = pl.BlockSpec((tokens, half), lambda h: (0, 0))
-    grad = pl.BlockSpec((1, HD, features), lambda h: (h, 0, 0))
+    vmem = pl.BlockSpec(memory_space=pltpu.VMEM)
     first = pl.pallas_call(
         first_kernel,
-        grid=(heads,),
-        in_specs=[cot, act, act],
-        out_specs=grad,
-        out_shape=jax.ShapeDtypeStruct((heads, HD, features), jnp.float32),
+        in_specs=[vmem] * 2,
+        out_specs=vmem,
+        out_shape=jax.ShapeDtypeStruct((heads, HD, half), jnp.float32),
         compiler_params=PARAMS,
-        cost_estimate=cost(2 * heads * tokens * HD * features, 2 * 2**20),
-    )(cot_here, *act_here)
-    tail = (2 * capacity, half)
+        cost_estimate=cost(2 * heads * tokens * HD * half, 2**20),
+    )(cot_here, act_here[0])
     return pl.pallas_call(
         padded_kernel,
-        grid=(heads,),
-        in_specs=[pl.BlockSpec((1, 1, HD), lambda h: (h, 0, 0)), grad, cot, act, act],
-        out_specs=pl.BlockSpec((lines, spots, 1) + tail, lambda h: (0, 0, h, 0, 0)),
-        out_shape=jax.ShapeDtypeStruct((lines, spots, heads) + tail, jnp.float32),
+        in_specs=[vmem] * 7,
+        out_specs=vmem,
+        out_shape=jax.ShapeDtypeStruct((lines, spots, heads, 2 * capacity, half), jnp.float32),
         compiler_params=PARAMS,
-        cost_estimate=cost(4 * heads * tokens * HD * features, 4 * 2**20),
-    )(target[:, None, :], first, cot_other, *act_other)
+        cost_estimate=cost(10 * heads * tokens * HD * half, 4 * 2**20),
+    )(target[:, None, :], first, cot_here, cot_other, act_other[0], act_here[1], act_other[1])
 
 
 def place_kernel(target_ref, key_ref, rows_ref, *refs):

time: 120 us -> 118 us (0.983)
  Pallas kernels: 7.43 us -> 6.04 us
    ppermute x1, waiting for transfers between devices: 3.77 us -> 0.01 us  [body(): act_here = (keep, lax.ppermute(keep, ('c', 'zh', 'zl'), same))]
    ppermute x1, waiting for transfers between devices: 0.01 us -> 3.52 us  [body(): lax.ppermute(give, ('c', 'zh', 'zl'), cross)]
    pallas_call x2, Pallas kernels: 3.56 us -> 2.18 us  [the longest x1 1.84 us: padded_gradient(): pl.pallas_call(padded_kernel, in_specs=[vmem] * 7, out_specs=vmem, out_sh...]
  transfers between devices with their start and end apart: 6 -> 6, of which waited for: 2 -> 2; matrix products, arithmetic and copies ran while one was open for 2% -> 2% of each run, Pallas kernels for 2% -> 1%
where the time goes in v7:
time: 118 us
  blocking collectives  68.1 us (58%)
  starting transfers between devices  33.2 us (28%)
  Pallas kernels  6.04 us (5%)
  waiting for transfers between devices  4.89 us (4%)
  local copies, waits for them, and re-layouts  3.07 us (3%)
  other arithmetic  1.68 us (1%)
    all_to_all x2, blocking collectives, copies_to_all(): lax.all_to_all(jnp.broadcast_to(block[None], (count,) + block.shape), axi...  27.7 us
    all_to_all x1, blocking collectives, body(): lax.all_to_all(jnp.swapaxes(send, 0, 1), ('y', 'zh'), 0, 0, tiled=True)  21.1 us
    all_to_all x1, blocking collectives, body(): got = lax.all_to_all(send, ('x', 'c'), 0, 0, tiled=True)  19.3 us
    all_to_all x1, starting transfers between devices, copies_to_all(): lax.all_to_all(jnp.broadcast_to(block[None], (count,) + block.shape), axi...  10.8 us
    ppermute x1, starting transfers between devices, body(): low_other = lax.ppermute(low, 'c', SWAP)  6.62 us
    ppermute x1, starting transfers between devices, body(): lax.ppermute(give, ('c', 'zh', 'zl'), cross)  6.61 us
    ppermute x1, starting transfers between devices, body(): cot_other = lax.ppermute(cot_here, 'c', SWAP)  5.32 us
    ppermute x1, waiting for transfers between devices, body(): lax.ppermute(give, ('c', 'zh', 'zl'), cross)  3.52 us
  transfers between devices with their start and end apart: 6, of which 2 were waited for; matrix products, arithmetic and copies ran while one was open for 2% of the time, Pallas kernels for 1%

profile of v7, /device:TPU:1, one launch (start us, length us, event | category | flops | bytes accessed | tf_op | source)
XLA Modules:
  0.0 117.9 jit_solution(13004968827999375289)
XLA Ops:
  0.6 1.8 %broadcast_in_dim.92 = bf16[4,512,128]{2,1,0:T(8,128)(2,1)} broadcast(bf16[512,128]{1,0:T(8,128)(2,1)} %param.8), dimensions={1,2} | broadcast | bytes 655360 | tf_op jit(solution)/shard_map/broadcast_in_dim | solution.py:102
  2.5 10.8 %all-to-all-start = ((bf16[4,512,128]{2,1,0:T(8,128)(2,1)}), bf16[4,512,128]{2,1,0:T(8,128)(2,1)S(1)}, u32[]{:S(2)}, u32[]{:S(2)}) async-start(bf16[4,512,128]{2,1,0:T(8,128)(2,1)} %broadcast_in_dim.92), calls=%async_computation | async-start | bytes 1048576 | tf_op jit(solution)/shard_map/all_to_all | solution.py:102
  13.3 0.7 constant_dynamic-slice_fusion.4
  14.0 0.1 convert_reduce_fusion.3
  14.2 0.3 convert_reduce_fusion.2
  14.5 0.2 select_reduce_fusion
  14.6 0.2 convert_reduce_fusion.1
  14.9 6.6 %collective-permute-start.3 = (bf16[512,256]{1,0:T(8,128)(2,1)S(1)}, bf16[512,256]{1,0:T(8,128)(2,1)S(1)}, u32[]{:S(2)}, u32[]{:S(2)}) collective-permute-start(bf16[512,256]{1,0:T(8,128)(2,1)S(1)} %get-tuple-element.28), channel_id=1, source_target_pairs={{0,9},{1,10},{2,11},{3,12},{4,13},{5,14},{6,15},{7,8},{8,7},{9,0},... | collective-permute-start | bytes 786440 | tf_op jit(solution)/shard_map/ppermute | solution.py:216
  21.6 1.9 %collective-permute-start.1 = (bf16[512,256]{1,0:T(8,128)(2,1)S(1)}, bf16[512,256]{1,0:T(8,128)(2,1)S(1)}, u32[]{:S(2)}, u32[]{:S(2)}) collective-permute-start(bf16[512,256]{1,0:T(8,128)(2,1)S(1)} %get-tuple-element.28), channel_id=1, source_target_pairs={{0,8},{8,0},{1,9},{9,1},{2,10},{10,2},{3,11},{11,3},{4,12},{12,4},... | collective-permute-start | bytes 786440 | tf_op jit(solution)/shard_map/ppermute | solution.py:216
  23.5 1.9 %collective-permute-start.2 = (bf16[512,256]{1,0:T(8,128)(2,1)S(1)}, bf16[512,256]{1,0:T(8,128)(2,1)S(1)}, u32[]{:S(2)}, u32[]{:S(2)}) collective-permute-start(bf16[512,256]{1,0:T(8,128)(2,1)S(1)} %get-tuple-element.29.act_ref), channel_id=1, source_target_pairs={{0,7},{1,0},{2,1},{3,2},{4,3},{5,4},{6,5},{7,6},{8,9},{9,10},{10,1... | collective-permute-start | bytes 786440 | tf_op jit(solution)/shard_map/ppermute | solution.py:215
  25.4 5.3 %collective-permute-start = (bf16[4,512,128]{2,1,0:T(8,128)(2,1)S(1)}, bf16[4,512,128]{2,1,0:T(8,128)(2,1)S(1)}, u32[]{:S(2)}, u32[]{:S(2)}) collective-permute-start(bf16[4,512,128]{2,1,0:T(8,128)(2,1)S(1)} %all-to-all-done.cot_ref.here_ref), channel_id=1, source_target_pairs={{0,8},{8,0},{1,9},{9,1},{2,10},{10,2},{3,11},{11,3},{4,12},{12,4},... | collective-permute-start | bytes 1572872 | tf_op jit(solution)/shard_map/ppermute | solution.py:217
  30.8 0.2 select_reduce_fusion.2.rank_ref
  31.0 0.3 shard_map.102.first_ref
  31.4 3.5 %collective-permute-done.3.far_ref = bf16[512,256]{1,0:T(8,128)(2,1)S(1)} collective-permute-done((bf16[512,256]{1,0:T(8,128)(2,1)S(1)}, bf16[512,256]{1,0:T(8,128)(2,1)S(1)}, u32[]{:S(2)}, u32[]{:S(2)}) %collective-permute-start.3) | collective-permute-done | bytes 262176 | tf_op jit(solution)/shard_map/ppermute | solution.py:216
  34.9 1.8 %shard_map.103 = f32[8,8,4,8,256]{4,3,2,1,0:T(8,128)S(1)} custom-call(s32[4,1,128]{2,1,0:T(1,128)S(1)} %bitcast.30, f32[4,128,256]{2,1,0:T(8,128)S(1)} %shard_map.102.first_ref, bf16[4,512,128]{2,1,0:T(8,128)(2,1)S(1)} %all-to-all-done.cot_ref.here_ref, bf16[4,512,128]{2,1,0:T(8,128)(2,1)S(1)} %collective-permute-done.other_ref, ...), custom_call_target="tpu_custom_call" | custom-call | flops 671088640 | bytes 4194304 | tf_op jit(solution)/shard_map/pallas_call | solution.py:157
  36.8 0.3 convert_element_type.36
  37.0 19.3 %all_to_all.25 = f16[8,32,8,256]{3,2,1,0:T(8,128)(2,1)S(1)} all-to-all(f16[8,32,8,256]{3,2,1,0:T(8,128)(2,1)S(1)} %bitcast.32), channel_id=1, replica_groups=mesh['x'=4,'y'=8,'c'=2,'zh'=4,'zl'=2] {'x','c'}, dimensions={0} | all-to-all | bytes 2097152 | tf_op jit(solution)/shard_map/all_to_all | solution.py:236
  56.3 0.1 convert_reduce_fusion
  56.5 0.0 copy-start
  56.6 21.1 %all_to_all.26 = f16[32,2,8,256]{3,2,1,0:T(8,128)(2,1)S(1)} all-to-all(f16[32,2,8,256]{3,2,1,0:T(8,128)(2,1)S(1)} %copy.18), channel_id=1, replica_groups=mesh['x'=4,'y'=8,'c'=2,'zh'=4,'zl'=2] {'y','zh'}, dimensions={0} | all-to-all | bytes 524288 | tf_op jit(solution)/shard_map/all_to_all | solution.py:239
  77.7 0.1 convert_element_type.46
  77.8 0.1 reshape.204
  78.0 0.1 reduce_sum.69
  78.1 1.5 %shard_map.104 = (f32[4,4096]{1,0:T(4,128)}, f32[1,2]{1,0:T(1,128)}, f32[4,4096]{1,0:T(4,128)}, f32[8,2048]{1,0:T(8,128)S(1)}) custom-call(s32[1]{0:T(128)} %bitcast.9.side_ref, s32[4]{0:T(128)S(1)} %select_reduce_fusion.2.rank_ref, f32[4,2,2,4,256]{4,3,2,1,0:T(4,128)S(1)} %broadcast_multiply_fusion.sums_ref, f32[4,4096]{1,0:T(4,128)S(1)} %bitcast.28, ...), custom_call_target="tpu_custom_call" | custom-call | tf_op jit(solution)/shard_map/pallas_call | solution.py:83
  79.6 13.9 %all_to_all.27 = bf16[8,8,2048]{2,1,0:T(8,128)(2,1)S(1)} all-to-all(bf16[8,8,2048]{2,1,0:T(8,128)(2,1)S(1)} %broadcast_in_dim.98), channel_id=1, replica_groups=mesh['x'=4,'y'=8,'c'=2,'zh'=4,'zl'=2] {'y'}, dimensions={0} | all-to-all | bytes 524288 | tf_op jit(solution)/shard_map/all_to_all | solution.py:102
  93.6 0.1 broadcast_in_dim.99
  93.7 13.7 %all_to_all.28 = bf16[4,8,8,2048]{3,2,1,0:T(8,128)(2,1)S(1)} all-to-all(bf16[4,8,8,2048]{3,2,1,0:T(8,128)(2,1)S(1)} %broadcast_in_dim.99), channel_id=1, replica_groups=mesh['x'=4,'y'=8,'c'=2,'zh'=4,'zl'=2] {'x'}, dimensions={0} | all-to-all | bytes 2097152 | tf_op jit(solution)/shard_map/all_to_all | solution.py:102
  107.4 6.6 %collective-permute-start.4 = (bf16[256,2048]{1,0:T(8,128)(2,1)S(1)}, bf16[256,2048]{1,0:T(8,128)(2,1)S(1)}, u32[]{:S(2)}, u32[]{:S(2)}) collective-permute-start(bf16[256,2048]{1,0:T(8,128)(2,1)S(1)} %bitcast.26), channel_id=1, source_target_pairs={{0,8},{8,0},{1,9},{9,1},{2,10},{10,2},{3,11},{11,3},{4,12},{12,4},... | collective-permute-start | bytes 3145736 | tf_op jit(solution)/shard_map/ppermute | solution.py:248
  114.1 0.1 copy.20.target_ref
  114.2 0.8 shard_map.105.refs_0_
  115.0 1.4 %collective-permute-done.4.rows_ref = bf16[256,2048]{1,0:T(8,128)(2,1)S(1)} collective-permute-done((bf16[256,2048]{1,0:T(8,128)(2,1)S(1)}, bf16[256,2048]{1,0:T(8,128)(2,1)S(1)}, u32[]{:S(2)}, u32[]{:S(2)}) %collective-permute-start.4) | collective-permute-done | bytes 1048608 | tf_op jit(solution)/shard_map/ppermute | solution.py:248
  116.3 1.6 %shard_map.106 = bf16[128,4096]{1,0:T(8,128)(2,1)} custom-call(s32[128,1]{1,0:T(8,128)S(1)} %copy.20.target_ref, s32[1,256]{1,0:T(1,128)S(1)} %get-tuple-element.18.key_ref, bf16[256,2048]{1,0:T(8,128)(2,1)S(1)} %collective-permute-done.4.rows_ref, bf16[128,4096]{1,0:T(8,128)(2,1)S(1)} %shard_map.105.refs_0_), custom_call_target="tpu_custom_call" | custom-call | flops 268435456 | bytes 2097152 | tf_op jit(solution)/shard_map/pallas_call | solution.py:180
  (24 shorter events, 0.3 us)
Async XLA Ops:
  0.6 14.3 %copy-start.3 = (bf16[512,512]{1,0:T(8,128)(2,1)S(1)}, bf16[512,512]{1,0:T(8,128)(2,1)}, u32[]{:S(2)}) copy-start(bf16[512,512]{1,0:T(8,128)(2,1)} %param.7) | copy-start | bytes 1572868
  2.5 23.0 %all-to-all-start = ((bf16[4,512,128]{2,1,0:T(8,128)(2,1)}), bf16[4,512,128]{2,1,0:T(8,128)(2,1)S(1)}, u32[]{:S(2)}, u32[]{:S(2)}) async-start(bf16[4,512,128]{2,1,0:T(8,128)(2,1)} %broadcast_in_dim.92), calls=%async_computation | async-start | bytes 1048576 | tf_op jit(solution)/shard_map/all_to_all | solution.py:102
  14.9 19.9 %collective-permute-start.3 = (bf16[512,256]{1,0:T(8,128)(2,1)S(1)}, bf16[512,256]{1,0:T(8,128)(2,1)S(1)}, u32[]{:S(2)}, u32[]{:S(2)}) collective-permute-start(bf16[512,256]{1,0:T(8,128)(2,1)S(1)} %get-tuple-element.28), channel_id=1, source_target_pairs={{0,9},{1,10},{2,11},{3,12},{4,13},{5,14},{6,15},{7,8},{8,7},{9,0},... | collective-permute-start | bytes 786440 | tf_op jit(solution)/shard_map/ppermute | solution.py:216
  21.6 13.3 %collective-permute-start.1 = (bf16[512,256]{1,0:T(8,128)(2,1)S(1)}, bf16[512,256]{1,0:T(8,128)(2,1)S(1)}, u32[]{:S(2)}, u32[]{:S(2)}) collective-permute-start(bf16[512,256]{1,0:T(8,128)(2,1)S(1)} %get-tuple-element.28), channel_id=1, source_target_pairs={{0,8},{8,0},{1,9},{9,1},{2,10},{10,2},{3,11},{11,3},{4,12},{12,4},... | collective-permute-start | bytes 786440 | tf_op jit(solution)/shard_map/ppermute | solution.py:216
  23.5 11.4 %collective-permute-start.2 = (bf16[512,256]{1,0:T(8,128)(2,1)S(1)}, bf16[512,256]{1,0:T(8,128)(2,1)S(1)}, u32[]{:S(2)}, u32[]{:S(2)}) collective-permute-start(bf16[512,256]{1,0:T(8,128)(2,1)S(1)} %get-tuple-element.29.act_ref), channel_id=1, source_target_pairs={{0,7},{1,0},{2,1},{3,2},{4,3},{5,4},{6,5},{7,6},{8,9},{9,10},{10,1... | collective-permute-start | bytes 786440 | tf_op jit(solution)/shard_map/ppermute | solution.py:215
  25.4 9.5 %collective-permute-start = (bf16[4,512,128]{2,1,0:T(8,128)(2,1)S(1)}, bf16[4,512,128]{2,1,0:T(8,128)(2,1)S(1)}, u32[]{:S(2)}, u32[]{:S(2)}) collective-permute-start(bf16[4,512,128]{2,1,0:T(8,128)(2,1)S(1)} %all-to-all-done.cot_ref.here_ref), channel_id=1, source_target_pairs={{0,8},{8,0},{1,9},{9,1},{2,10},{10,2},{3,11},{11,3},{4,12},{12,4},... | collective-permute-start | bytes 1572872 | tf_op jit(solution)/shard_map/ppermute | solution.py:217
  56.5 21.6 %copy-start = (f32[1,1,4,4096]{3,2,1,0:T(4,128)S(1)}, f32[1,1,4,4096]{3,2,1,0:T(4,128)}, u32[]{:S(2)}) copy-start(f32[1,1,4,4096]{3,2,1,0:T(4,128)} %param.11) | copy-start | bytes 196612
  56.5 21.6 %copy-start.1 = (f32[1,1,4,4096]{3,2,1,0:T(4,128)S(1)}, f32[1,1,4,4096]{3,2,1,0:T(4,128)}, u32[]{:S(2)}) copy-start(f32[1,1,4,4096]{3,2,1,0:T(4,128)} %param.13) | copy-start | bytes 196612
  56.5 21.6 %copy-start.2 = (f32[1,1,2]{2,1,0:T(1,128)S(1)}, f32[1,1,2]{2,1,0:T(1,128)}, u32[]{:S(2)}) copy-start(f32[1,1,2]{2,1,0:T(1,128)} %param.12) | copy-start | bytes 28
  107.4 8.9 %collective-permute-start.4 = (bf16[256,2048]{1,0:T(8,128)(2,1)S(1)}, bf16[256,2048]{1,0:T(8,128)(2,1)S(1)}, u32[]{:S(2)}, u32[]{:S(2)}) collective-permute-start(bf16[256,2048]{1,0:T(8,128)(2,1)S(1)} %bitcast.26), channel_id=1, source_target_pairs={{0,8},{8,0},{1,9},{9,1},{2,10},{10,2},{3,11},{11,3},{4,12},{12,4},... | collective-permute-start | bytes 3145736 | tf_op jit(solution)/shard_map/ppermute | solution.py:248

commit v8 on v7

--- a/solution.py
+++ b/solution.py
@@ -110,6 +110,28 @@
     return pl.CostEstimate(flops=flops, bytes_accessed=moved, transcendentals=0)
 
 
+def copies_kernel(block_ref, out_ref, sems):
+    copies = [
+        pltpu.make_async_copy(block_ref, out_ref.at[i], sems.at[i]) for i in range(out_ref.shape[0])
+    ]
+    for copy in copies:
+        copy.start()
+    for copy in copies:
+        copy.wait()
+
+
+def copies_in_hbm(block, count):
+    whole = pl.BlockSpec(memory_space=pl.ANY)
+    return pl.pallas_call(
+        copies_kernel,
+        in_specs=[whole],
+        out_specs=whole,
+        out_shape=jax.ShapeDtypeStruct((count,) + block.shape, block.dtype),
+        scratch_shapes=[pltpu.SemaphoreType.DMA((count,))],
+        cost_estimate=cost(0, 2**20),
+    )(block)
+
+
 def first_kernel(cot_ref, act_ref, out_ref):
     for head in range(cot_ref.shape[0]):
         out_ref[head] = lax.dot_general(
@@ -198,7 +220,7 @@
     owner_here = chip * nc + core
     half = activations.shape[1] // 2
 
-    cot_here = copies_to_all(cotangent, "zh")
+    cot_here = lax.all_to_all(copies_in_hbm(cotangent, pairs), "zh", 0, 0, tiled=True)
     def of_side(table):
         return lax.dynamic_index_in_dim(table.reshape(pairs, PAIR, -1), side, 1, keepdims=False)
 

time: 118 us -> 134 us (1.14)
  Pallas kernels: 6.04 us -> 23.1 us
  local copies, waits for them, and re-layouts: 3.07 us -> 1.25 us
    pallas_call x0 -> x1, Pallas kernels: none -> 17 us  [copies_in_hbm(): pl.pallas_call(copies_kernel, in_specs=[whole], out_specs=whole, out_shap...]
    broadcast_in_dim x3 -> x2, local copies, waits for them, and re-layouts: 1.95 us -> 0.13 us  [copies_to_all(): jnp.broadcast_to(block[None], (count,) + block.shape)]
  transfers between devices with their start and end apart: 6 -> 6, of which waited for: 2 -> 2; matrix products, arithmetic and copies ran while one was open for 2% -> 1% of each run, Pallas kernels for 1% -> 1%
where the time goes in v8:
time: 134 us; the launch traced here: 133 us
  blocking collectives  68.1 us (51%)
  starting transfers between devices  33.3 us (25%)
  Pallas kernels  23.1 us (17%)
  waiting for transfers between devices  4.89 us (4%)
  other arithmetic  1.67 us (1%)
    all_to_all x2, blocking collectives, copies_to_all(): lax.all_to_all(jnp.broadcast_to(block[None], (count,) + block.shape), axi...  27.7 us
    all_to_all x1, blocking collectives, body(): lax.all_to_all(jnp.swapaxes(send, 0, 1), ('y', 'zh'), 0, 0, tiled=True)  21.1 us
    all_to_all x1, blocking collectives, body(): got = lax.all_to_all(send, ('x', 'c'), 0, 0, tiled=True)  19.3 us
    pallas_call x1, Pallas kernels, copies_in_hbm(): pl.pallas_call(copies_kernel, in_specs=[whole], out_specs=whole, out_shap...  17 us
    all_to_all x1, starting transfers between devices, body(): lax.all_to_all(copies_in_hbm(cotangent, pairs), 'zh', 0, 0, tiled=True)  10.9 us
    ppermute x1, starting transfers between devices, body(): low_other = lax.ppermute(low, 'c', SWAP)  6.64 us
    ppermute x1, starting transfers between devices, body(): lax.ppermute(give, ('c', 'zh', 'zl'), cross)  6.61 us
    ppermute x1, starting transfers between devices, body(): cot_other = lax.ppermute(cot_here, 'c', SWAP)  5.32 us
  transfers between devices with their start and end apart: 6, of which 2 were waited for; matrix products, arithmetic and copies ran while one was open for 1% of the time, Pallas kernels for 1%

profile of v8, /device:TPU:1, one launch (start us, length us, event | category | flops | bytes accessed | tf_op | source)
XLA Modules:
  0.0 133.2 jit_solution(16860624523982116691)
XLA Ops:
  0.6 17.0 %shard_map.102 = bf16[4,512,128]{2,1,0:T(8,128)(2,1)} custom-call(bf16[512,128]{1,0:T(8,128)(2,1)} %block_ref.1), custom_call_target="tpu_custom_call" | custom-call | bytes 1048576 | tf_op jit(solution)/shard_map/pallas_call | solution.py:125
  17.7 10.9 %all-to-all-start = ((bf16[4,512,128]{2,1,0:T(8,128)(2,1)}), bf16[4,512,128]{2,1,0:T(8,128)(2,1)S(1)}, u32[]{:S(2)}, u32[]{:S(2)}) async-start(bf16[4,512,128]{2,1,0:T(8,128)(2,1)} %shard_map.102), calls=%async_computation | async-start | bytes 1048576 | tf_op jit(solution)/shard_map/all_to_all | solution.py:223
  28.5 0.7 constant_dynamic-slice_fusion.4
  29.3 0.1 convert_reduce_fusion.3
  29.4 0.3 convert_reduce_fusion.2
  29.7 0.2 select_reduce_fusion
  29.8 0.2 convert_reduce_fusion.1
  30.2 6.6 %collective-permute-start.3 = (bf16[512,256]{1,0:T(8,128)(2,1)S(1)}, bf16[512,256]{1,0:T(8,128)(2,1)S(1)}, u32[]{:S(2)}, u32[]{:S(2)}) collective-permute-start(bf16[512,256]{1,0:T(8,128)(2,1)S(1)} %get-tuple-element.28), channel_id=1, source_target_pairs={{0,9},{1,10},{2,11},{3,12},{4,13},{5,14},{6,15},{7,8},{8,7},{9,0},... | collective-permute-start | bytes 786440 | tf_op jit(solution)/shard_map/ppermute | solution.py:238
  36.8 1.9 %collective-permute-start.1 = (bf16[512,256]{1,0:T(8,128)(2,1)S(1)}, bf16[512,256]{1,0:T(8,128)(2,1)S(1)}, u32[]{:S(2)}, u32[]{:S(2)}) collective-permute-start(bf16[512,256]{1,0:T(8,128)(2,1)S(1)} %get-tuple-element.28), channel_id=1, source_target_pairs={{0,8},{8,0},{1,9},{9,1},{2,10},{10,2},{3,11},{11,3},{4,12},{12,4},... | collective-permute-start | bytes 786440 | tf_op jit(solution)/shard_map/ppermute | solution.py:238
  38.7 1.9 %collective-permute-start.2 = (bf16[512,256]{1,0:T(8,128)(2,1)S(1)}, bf16[512,256]{1,0:T(8,128)(2,1)S(1)}, u32[]{:S(2)}, u32[]{:S(2)}) collective-permute-start(bf16[512,256]{1,0:T(8,128)(2,1)S(1)} %get-tuple-element.29.act_ref), channel_id=1, source_target_pairs={{0,7},{1,0},{2,1},{3,2},{4,3},{5,4},{6,5},{7,6},{8,9},{9,10},{10,1... | collective-permute-start | bytes 786440 | tf_op jit(solution)/shard_map/ppermute | solution.py:237
  40.7 5.3 %collective-permute-start = (bf16[4,512,128]{2,1,0:T(8,128)(2,1)S(1)}, bf16[4,512,128]{2,1,0:T(8,128)(2,1)S(1)}, u32[]{:S(2)}, u32[]{:S(2)}) collective-permute-start(bf16[4,512,128]{2,1,0:T(8,128)(2,1)S(1)} %all-to-all-done.cot_ref.here_ref), channel_id=1, source_target_pairs={{0,8},{8,0},{1,9},{9,1},{2,10},{10,2},{3,11},{11,3},{4,12},{12,4},... | collective-permute-start | bytes 1572872 | tf_op jit(solution)/shard_map/ppermute | solution.py:239
  46.1 0.2 select_reduce_fusion.2.rank_ref
  46.2 0.3 shard_map.103.first_ref
  46.6 3.5 %collective-permute-done.3.far_ref = bf16[512,256]{1,0:T(8,128)(2,1)S(1)} collective-permute-done((bf16[512,256]{1,0:T(8,128)(2,1)S(1)}, bf16[512,256]{1,0:T(8,128)(2,1)S(1)}, u32[]{:S(2)}, u32[]{:S(2)}) %collective-permute-start.3) | collective-permute-done | bytes 262176 | tf_op jit(solution)/shard_map/ppermute | solution.py:238
  50.1 1.9 %shard_map.104 = f32[8,8,4,8,256]{4,3,2,1,0:T(8,128)S(1)} custom-call(s32[4,1,128]{2,1,0:T(1,128)S(1)} %bitcast.30, f32[4,128,256]{2,1,0:T(8,128)S(1)} %shard_map.103.first_ref, bf16[4,512,128]{2,1,0:T(8,128)(2,1)S(1)} %all-to-all-done.cot_ref.here_ref, bf16[4,512,128]{2,1,0:T(8,128)(2,1)S(1)} %collective-permute-done.other_ref, ...), custom_call_target="tpu_custom_call" | custom-call | flops 671088640 | bytes 4194304 | tf_op jit(solution)/shard_map/pallas_call | solution.py:179
  52.0 0.3 convert_element_type.36
  52.3 19.3 %all_to_all.25 = f16[8,32,8,256]{3,2,1,0:T(8,128)(2,1)S(1)} all-to-all(f16[8,32,8,256]{3,2,1,0:T(8,128)(2,1)S(1)} %bitcast.32), channel_id=1, replica_groups=mesh['x'=4,'y'=8,'c'=2,'zh'=4,'zl'=2] {'x','c'}, dimensions={0} | all-to-all | bytes 2097152 | tf_op jit(solution)/shard_map/all_to_all | solution.py:258
  71.5 0.1 convert_reduce_fusion
  71.7 0.0 copy-start.1
  71.8 21.1 %all_to_all.26 = f16[32,2,8,256]{3,2,1,0:T(8,128)(2,1)S(1)} all-to-all(f16[32,2,8,256]{3,2,1,0:T(8,128)(2,1)S(1)} %copy.18), channel_id=1, replica_groups=mesh['x'=4,'y'=8,'c'=2,'zh'=4,'zl'=2] {'y','zh'}, dimensions={0} | all-to-all | bytes 524288 | tf_op jit(solution)/shard_map/all_to_all | solution.py:261
  93.0 0.1 convert_element_type.46
  93.0 0.1 reshape.203
  93.2 0.1 reduce_sum.69
  93.4 1.5 %shard_map.105 = (f32[4,4096]{1,0:T(4,128)}, f32[1,2]{1,0:T(1,128)}, f32[4,4096]{1,0:T(4,128)}, f32[8,2048]{1,0:T(8,128)S(1)}) custom-call(s32[1]{0:T(128)} %bitcast.9.side_ref, s32[4]{0:T(128)S(1)} %select_reduce_fusion.2.rank_ref, f32[4,2,2,4,256]{4,3,2,1,0:T(4,128)S(1)} %broadcast_multiply_fusion.sums_ref, f32[4,4096]{1,0:T(4,128)S(1)} %bitcast.28, ...), custom_call_target="tpu_custom_call" | custom-call | tf_op jit(solution)/shard_map/pallas_call | solution.py:83
  94.9 13.9 %all_to_all.27 = bf16[8,8,2048]{2,1,0:T(8,128)(2,1)S(1)} all-to-all(bf16[8,8,2048]{2,1,0:T(8,128)(2,1)S(1)} %broadcast_in_dim.91), channel_id=1, replica_groups=mesh['x'=4,'y'=8,'c'=2,'zh'=4,'zl'=2] {'y'}, dimensions={0} | all-to-all | bytes 524288 | tf_op jit(solution)/shard_map/all_to_all | solution.py:102
  108.8 0.1 broadcast_in_dim.92
  108.9 13.7 %all_to_all.28 = bf16[4,8,8,2048]{3,2,1,0:T(8,128)(2,1)S(1)} all-to-all(bf16[4,8,8,2048]{3,2,1,0:T(8,128)(2,1)S(1)} %broadcast_in_dim.92), channel_id=1, replica_groups=mesh['x'=4,'y'=8,'c'=2,'zh'=4,'zl'=2] {'x'}, dimensions={0} | all-to-all | bytes 2097152 | tf_op jit(solution)/shard_map/all_to_all | solution.py:102
  122.6 6.6 %collective-permute-start.4 = (bf16[256,2048]{1,0:T(8,128)(2,1)S(1)}, bf16[256,2048]{1,0:T(8,128)(2,1)S(1)}, u32[]{:S(2)}, u32[]{:S(2)}) collective-permute-start(bf16[256,2048]{1,0:T(8,128)(2,1)S(1)} %bitcast.26), channel_id=1, source_target_pairs={{0,8},{8,0},{1,9},{9,1},{2,10},{10,2},{3,11},{11,3},{4,12},{12,4},... | collective-permute-start | bytes 3145736 | tf_op jit(solution)/shard_map/ppermute | solution.py:270
  129.3 0.1 copy.20.target_ref
  129.4 0.8 shard_map.106.refs_0_
  130.2 1.4 %collective-permute-done.4.rows_ref = bf16[256,2048]{1,0:T(8,128)(2,1)S(1)} collective-permute-done((bf16[256,2048]{1,0:T(8,128)(2,1)S(1)}, bf16[256,2048]{1,0:T(8,128)(2,1)S(1)}, u32[]{:S(2)}, u32[]{:S(2)}) %collective-permute-start.4) | collective-permute-done | bytes 1048608 | tf_op jit(solution)/shard_map/ppermute | solution.py:270
  131.5 1.6 %shard_map.107 = bf16[128,4096]{1,0:T(8,128)(2,1)} custom-call(s32[128,1]{1,0:T(8,128)S(1)} %copy.20.target_ref, s32[1,256]{1,0:T(1,128)S(1)} %get-tuple-element.18.key_ref, bf16[256,2048]{1,0:T(8,128)(2,1)S(1)} %collective-permute-done.4.rows_ref, bf16[128,4096]{1,0:T(8,128)(2,1)S(1)} %shard_map.106.refs_0_), custom_call_target="tpu_custom_call" | custom-call | flops 268435456 | bytes 2097152 | tf_op jit(solution)/shard_map/pallas_call | solution.py:202
  (24 shorter events, 0.3 us)
Async XLA Ops:
  0.6 29.5 %copy-start.3 = (bf16[512,512]{1,0:T(8,128)(2,1)S(1)}, bf16[512,512]{1,0:T(8,128)(2,1)}, u32[]{:S(2)}) copy-start(bf16[512,512]{1,0:T(8,128)(2,1)} %param.7) | copy-start | bytes 1572868
  17.7 23.0 %all-to-all-start = ((bf16[4,512,128]{2,1,0:T(8,128)(2,1)}), bf16[4,512,128]{2,1,0:T(8,128)(2,1)S(1)}, u32[]{:S(2)}, u32[]{:S(2)}) async-start(bf16[4,512,128]{2,1,0:T(8,128)(2,1)} %shard_map.102), calls=%async_computation | async-start | bytes 1048576 | tf_op jit(solution)/shard_map/all_to_all | solution.py:223
  30.2 20.0 %collective-permute-start.3 = (bf16[512,256]{1,0:T(8,128)(2,1)S(1)}, bf16[512,256]{1,0:T(8,128)(2,1)S(1)}, u32[]{:S(2)}, u32[]{:S(2)}) collective-permute-start(bf16[512,256]{1,0:T(8,128)(2,1)S(1)} %get-tuple-element.28), channel_id=1, source_target_pairs={{0,9},{1,10},{2,11},{3,12},{4,13},{5,14},{6,15},{7,8},{8,7},{9,0},... | collective-permute-start | bytes 786440 | tf_op jit(solution)/shard_map/ppermute | solution.py:238
  36.8 13.3 %collective-permute-start.1 = (bf16[512,256]{1,0:T(8,128)(2,1)S(1)}, bf16[512,256]{1,0:T(8,128)(2,1)S(1)}, u32[]{:S(2)}, u32[]{:S(2)}) collective-permute-start(bf16[512,256]{1,0:T(8,128)(2,1)S(1)} %get-tuple-element.28), channel_id=1, source_target_pairs={{0,8},{8,0},{1,9},{9,1},{2,10},{10,2},{3,11},{11,3},{4,12},{12,4},... | collective-permute-start | bytes 786440 | tf_op jit(solution)/shard_map/ppermute | solution.py:238
  38.7 11.4 %collective-permute-start.2 = (bf16[512,256]{1,0:T(8,128)(2,1)S(1)}, bf16[512,256]{1,0:T(8,128)(2,1)S(1)}, u32[]{:S(2)}, u32[]{:S(2)}) collective-permute-start(bf16[512,256]{1,0:T(8,128)(2,1)S(1)} %get-tuple-element.29.act_ref), channel_id=1, source_target_pairs={{0,7},{1,0},{2,1},{3,2},{4,3},{5,4},{6,5},{7,6},{8,9},{9,10},{10,1... | collective-permute-start | bytes 786440 | tf_op jit(solution)/shard_map/ppermute | solution.py:237
  40.7 9.5 %collective-permute-start = (bf16[4,512,128]{2,1,0:T(8,128)(2,1)S(1)}, bf16[4,512,128]{2,1,0:T(8,128)(2,1)S(1)}, u32[]{:S(2)}, u32[]{:S(2)}) collective-permute-start(bf16[4,512,128]{2,1,0:T(8,128)(2,1)S(1)} %all-to-all-done.cot_ref.here_ref), channel_id=1, source_target_pairs={{0,8},{8,0},{1,9},{9,1},{2,10},{10,2},{3,11},{11,3},{4,12},{12,4},... | collective-permute-start | bytes 1572872 | tf_op jit(solution)/shard_map/ppermute | solution.py:239
  71.7 21.6 %copy-start = (f32[1,1,4,4096]{3,2,1,0:T(4,128)S(1)}, f32[1,1,4,4096]{3,2,1,0:T(4,128)}, u32[]{:S(2)}) copy-start(f32[1,1,4,4096]{3,2,1,0:T(4,128)} %param.11) | copy-start | bytes 196612
  71.7 21.6 %copy-start.1 = (f32[1,1,4,4096]{3,2,1,0:T(4,128)S(1)}, f32[1,1,4,4096]{3,2,1,0:T(4,128)}, u32[]{:S(2)}) copy-start(f32[1,1,4,4096]{3,2,1,0:T(4,128)} %param.13) | copy-start | bytes 196612
  71.7 21.6 %copy-start.2 = (f32[1,1,2]{2,1,0:T(1,128)S(1)}, f32[1,1,2]{2,1,0:T(1,128)}, u32[]{:S(2)}) copy-start(f32[1,1,2]{2,1,0:T(1,128)} %param.12) | copy-start | bytes 28
  122.6 8.9 %collective-permute-start.4 = (bf16[256,2048]{1,0:T(8,128)(2,1)S(1)}, bf16[256,2048]{1,0:T(8,128)(2,1)S(1)}, u32[]{:S(2)}, u32[]{:S(2)}) collective-permute-start(bf16[256,2048]{1,0:T(8,128)(2,1)S(1)} %bitcast.26), channel_id=1, source_target_pairs={{0,8},{8,0},{1,9},{9,1},{2,10},{10,2},{3,11},{11,3},{4,12},{12,4},... | collective-permute-start | bytes 3145736 | tf_op jit(solution)/shard_map/ppermute | solution.py:270

commit v9 on v8

--- a/solution.py
+++ b/solution.py
@@ -39,7 +39,7 @@
 
 
 def adam_kernel(side_ref, rank_ref, sums_ref, moment_ref, second_ref, master_ref, *outs):
-    moment_out, second_out, master_out, rows_out = outs
+    grad_out, scale_out, second_out, rows_out = outs
     even = side_ref[0] == 0
     capacity, width = moment_ref.shape
     half = sums_ref.shape[-1]
@@ -64,14 +64,14 @@
         slot_second = jnp.where(here, fresh, slot_second)
     filled = rank >= 0
     scale = 1.0 / (fix_one * (jnp.sqrt(slot_second / fix_two) + epsilon))
+    scale_out[...] = scale
     for part, grad in enumerate(grads):
         span = slice(part * half, (part + 1) * half)
         moment = jnp.where(filled, beta_one * moment_ref[:, span] + (1.0 - beta_one) * grad, 0.0)
         master = master_ref[:, span]
         master = master - learn_rate * (moment * scale + decay_rate * master)
         master = jnp.where(filled, master, 0.0)
-        moment_out[:, span] = moment
-        master_out[:, span] = master
+        grad_out[:, span] = grad
         piece, place = divmod(part * half, width // CUT)
         rows_out[piece * capacity : (piece + 1) * capacity, place : place + half] = master
 
@@ -86,8 +86,8 @@
         out_specs=[vmem] * 4,
         out_shape=[
             shape(capacity, width),
+            shape(capacity, 1),
             shape(1, 2),
-            shape(capacity, width),
             shape(capacity * CUT, width // CUT),
         ],
         compiler_params=pltpu.CompilerParams(vmem_limit_bytes=32 * 2**20),
@@ -121,11 +121,10 @@
 
 
 def copies_in_hbm(block, count):
-    whole = pl.BlockSpec(memory_space=pl.ANY)
     return pl.pallas_call(
         copies_kernel,
-        in_specs=[whole],
-        out_specs=whole,
+        in_specs=[pl.BlockSpec(memory_space=pltpu.VMEM)],
+        out_specs=pl.BlockSpec(memory_space=pl.ANY),
         out_shape=jax.ShapeDtypeStruct((count,) + block.shape, block.dtype),
         scratch_shapes=[pltpu.SemaphoreType.DMA((count,))],
         cost_estimate=cost(0, 2**20),
@@ -261,12 +260,18 @@
     got = lax.all_to_all(jnp.swapaxes(send, 0, 1), ("y", "zh"), 0, 0, tiled=True)
     got = got.reshape(ny, pairs, nc, 2, capacity, half)
     summed = jnp.sum(got.astype(jnp.float32), axis=0) * 2.0
-    moment_new, second_new, master_new, low = adam_rows(
-        side, rank, summed, first_moment[0, 0], block_second[0, 0], master_rows[0, 0]
-    )
+    moment, master = first_moment[0, 0], master_rows[0, 0]
+    grads, scale, second_new, low = adam_rows(side, rank, summed, moment, block_second[0, 0], master)
 
     low = copies_to_all(copies_to_all(low.astype(jnp.bfloat16), "y"), "x")
     low = low.reshape(-1, width // CUT)
+    low, grads, scale, second_new, target_here, rank = lax.optimization_barrier(
+        (low, grads, scale, second_new, target_here, rank)
+    )
+    filled = (rank >= 0)[:, None]
+    moment_new = jnp.where(filled, beta_one * moment + (1.0 - beta_one) * grads, 0.0)
+    master_new = master - learn_rate * (moment_new * scale + decay_rate * master)
+    master_new = jnp.where(filled, master_new, 0.0)
     low_other = lax.ppermute(low, "c", SWAP)
     placed = place_rows(target_here, key_here, low)
     new_weight = place_rows(target_here, key_other, low_other, placed)

time: 134 us -> 118 us (0.88)
  Pallas kernels: 23.1 us -> 7.52 us
    pallas_call x1, Pallas kernels: 17 us -> 1.78 us  [copies_in_hbm(): pl.pallas_call(copies_kernel, in_specs=[pl.BlockSpec(memory_space=pltpu.V...]
  transfers between devices with their start and end apart: 6 -> 6, of which waited for: 2 -> 2; matrix products, arithmetic and copies ran while one was open for 1% -> 2% of each run, Pallas kernels for 1% -> 1%
where the time goes in v9:
time: 118 us
  blocking collectives  68.1 us (58%)
  starting transfers between devices  33.3 us (28%)
  Pallas kernels  7.52 us (6%)
  waiting for transfers between devices  4.12 us (3%)
  other arithmetic  2.54 us (2%)
  local copies, waits for them, and re-layouts  1.25 us (1%)
    all_to_all x2, blocking collectives, copies_to_all(): lax.all_to_all(jnp.broadcast_to(block[None], (count,) + block.shape), axi...  27.7 us
    all_to_all x1, blocking collectives, body(): lax.all_to_all(jnp.swapaxes(send, 0, 1), ('y', 'zh'), 0, 0, tiled=True)  21.1 us
    all_to_all x1, blocking collectives, body(): got = lax.all_to_all(send, ('x', 'c'), 0, 0, tiled=True)  19.3 us
    all_to_all x1, starting transfers between devices, body(): lax.all_to_all(copies_in_hbm(cotangent, pairs), 'zh', 0, 0, tiled=True)  10.9 us
    ppermute x1, starting transfers between devices, body(): low_other = lax.ppermute(low, 'c', SWAP)  6.64 us
    ppermute x1, starting transfers between devices, body(): lax.ppermute(give, ('c', 'zh', 'zl'), cross)  6.61 us
    ppermute x1, starting transfers between devices, body(): cot_other = lax.ppermute(cot_here, 'c', SWAP)  5.32 us
    ppermute x1, waiting for transfers between devices, body(): lax.ppermute(give, ('c', 'zh', 'zl'), cross)  3.52 us
  transfers between devices with their start and end apart: 6, of which 2 were waited for; matrix products, arithmetic and copies ran while one was open for 2% of the time, Pallas kernels for 1%

profile of v9, /device:TPU:1, one launch (start us, length us, event | category | flops | bytes accessed | tf_op | source)
XLA Modules:
  0.0 117.7 jit_solution(18230799999694299343)
XLA Ops:
  0.6 1.8 %shard_map.102 = bf16[4,512,128]{2,1,0:T(8,128)(2,1)} custom-call(bf16[512,128]{1,0:T(8,128)(2,1)} %block_ref.1), custom_call_target="tpu_custom_call" | custom-call | bytes 1048576 | tf_op jit(solution)/shard_map/pallas_call | solution.py:124
  2.4 10.9 %all-to-all-start = ((bf16[4,512,128]{2,1,0:T(8,128)(2,1)}), bf16[4,512,128]{2,1,0:T(8,128)(2,1)S(1)}, u32[]{:S(2)}, u32[]{:S(2)}) async-start(bf16[4,512,128]{2,1,0:T(8,128)(2,1)} %shard_map.102), calls=%async_computation | async-start | bytes 1048576 | tf_op jit(solution)/shard_map/all_to_all | solution.py:222
  13.3 0.7 constant_dynamic-slice_fusion.4
  14.0 0.1 convert_reduce_fusion.3
  14.1 0.3 convert_reduce_fusion.2
  14.4 0.2 select_reduce_fusion
  14.6 0.2 convert_reduce_fusion.1
  14.9 6.6 %collective-permute-start.3 = (bf16[512,256]{1,0:T(8,128)(2,1)S(1)}, bf16[512,256]{1,0:T(8,128)(2,1)S(1)}, u32[]{:S(2)}, u32[]{:S(2)}) collective-permute-start(bf16[512,256]{1,0:T(8,128)(2,1)S(1)} %get-tuple-element.40), channel_id=1, source_target_pairs={{0,9},{1,10},{2,11},{3,12},{4,13},{5,14},{6,15},{7,8},{8,7},{9,0},... | collective-permute-start | bytes 786440 | tf_op jit(solution)/shard_map/ppermute | solution.py:237
  21.5 1.9 %collective-permute-start.1 = (bf16[512,256]{1,0:T(8,128)(2,1)S(1)}, bf16[512,256]{1,0:T(8,128)(2,1)S(1)}, u32[]{:S(2)}, u32[]{:S(2)}) collective-permute-start(bf16[512,256]{1,0:T(8,128)(2,1)S(1)} %get-tuple-element.40), channel_id=1, source_target_pairs={{0,8},{8,0},{1,9},{9,1},{2,10},{10,2},{3,11},{11,3},{4,12},{12,4},... | collective-permute-start | bytes 786440 | tf_op jit(solution)/shard_map/ppermute | solution.py:237
  23.5 1.9 %collective-permute-start.2 = (bf16[512,256]{1,0:T(8,128)(2,1)S(1)}, bf16[512,256]{1,0:T(8,128)(2,1)S(1)}, u32[]{:S(2)}, u32[]{:S(2)}) collective-permute-start(bf16[512,256]{1,0:T(8,128)(2,1)S(1)} %get-tuple-element.41.act_ref), channel_id=1, source_target_pairs={{0,7},{1,0},{2,1},{3,2},{4,3},{5,4},{6,5},{7,6},{8,9},{9,10},{10,1... | collective-permute-start | bytes 786440 | tf_op jit(solution)/shard_map/ppermute | solution.py:236
  25.4 5.3 %collective-permute-start = (bf16[4,512,128]{2,1,0:T(8,128)(2,1)S(1)}, bf16[4,512,128]{2,1,0:T(8,128)(2,1)S(1)}, u32[]{:S(2)}, u32[]{:S(2)}) collective-permute-start(bf16[4,512,128]{2,1,0:T(8,128)(2,1)S(1)} %all-to-all-done.cot_ref.here_ref), channel_id=1, source_target_pairs={{0,8},{8,0},{1,9},{9,1},{2,10},{10,2},{3,11},{11,3},{4,12},{12,4},... | collective-permute-start | bytes 1572872 | tf_op jit(solution)/shard_map/ppermute | solution.py:238
  30.8 0.2 select_reduce_fusion.2.rank_ref
  31.0 0.3 shard_map.103.first_ref
  31.4 3.5 %collective-permute-done.3.far_ref = bf16[512,256]{1,0:T(8,128)(2,1)S(1)} collective-permute-done((bf16[512,256]{1,0:T(8,128)(2,1)S(1)}, bf16[512,256]{1,0:T(8,128)(2,1)S(1)}, u32[]{:S(2)}, u32[]{:S(2)}) %collective-permute-start.3) | collective-permute-done | bytes 262176 | tf_op jit(solution)/shard_map/ppermute | solution.py:237
  34.9 1.8 %shard_map.104 = f32[8,8,4,8,256]{4,3,2,1,0:T(8,128)S(1)} custom-call(s32[4,1,128]{2,1,0:T(1,128)S(1)} %bitcast.38, f32[4,128,256]{2,1,0:T(8,128)S(1)} %shard_map.103.first_ref, bf16[4,512,128]{2,1,0:T(8,128)(2,1)S(1)} %all-to-all-done.cot_ref.here_ref, bf16[4,512,128]{2,1,0:T(8,128)(2,1)S(1)} %collective-permute-done.other_ref, ...), custom_call_target="tpu_custom_call" | custom-call | flops 671088640 | bytes 4194304 | tf_op jit(solution)/shard_map/pallas_call | solution.py:178
  36.7 0.3 convert_element_type.36
  37.0 19.3 %all_to_all.25 = f16[8,32,8,256]{3,2,1,0:T(8,128)(2,1)S(1)} all-to-all(f16[8,32,8,256]{3,2,1,0:T(8,128)(2,1)S(1)} %bitcast.40), channel_id=1, replica_groups=mesh['x'=4,'y'=8,'c'=2,'zh'=4,'zl'=2] {'x','c'}, dimensions={0} | all-to-all | bytes 2097152 | tf_op jit(solution)/shard_map/all_to_all | solution.py:257
  56.3 0.1 convert_reduce_fusion
  56.6 21.1 %all_to_all.26 = f16[32,2,8,256]{3,2,1,0:T(8,128)(2,1)S(1)} all-to-all(f16[32,2,8,256]{3,2,1,0:T(8,128)(2,1)S(1)} %copy.20), channel_id=1, replica_groups=mesh['x'=4,'y'=8,'c'=2,'zh'=4,'zl'=2] {'y','zh'}, dimensions={0} | all-to-all | bytes 524288 | tf_op jit(solution)/shard_map/all_to_all | solution.py:260
  77.8 0.1 reshape.204
  77.9 0.1 reduce_sum.69
  78.1 1.2 shard_map.105
  79.3 13.9 %all_to_all.27 = bf16[8,8,2048]{2,1,0:T(8,128)(2,1)S(1)} all-to-all(bf16[8,8,2048]{2,1,0:T(8,128)(2,1)S(1)} %broadcast_in_dim.108), channel_id=1, replica_groups=mesh['x'=4,'y'=8,'c'=2,'zh'=4,'zl'=2] {'y'}, dimensions={0} | all-to-all | bytes 524288 | tf_op jit(solution)/shard_map/all_to_all | solution.py:102
  93.2 0.1 broadcast_in_dim.109
  93.3 13.7 %all_to_all.28 = bf16[4,8,8,2048]{3,2,1,0:T(8,128)(2,1)S(1)} all-to-all(bf16[4,8,8,2048]{3,2,1,0:T(8,128)(2,1)S(1)} %broadcast_in_dim.109), channel_id=1, replica_groups=mesh['x'=4,'y'=8,'c'=2,'zh'=4,'zl'=2] {'x'}, dimensions={0} | all-to-all | bytes 2097152 | tf_op jit(solution)/shard_map/all_to_all | solution.py:102
  107.1 0.1 copy.22.target_ref
  107.2 6.6 %collective-permute-start.4 = (bf16[256,2048]{1,0:T(8,128)(2,1)S(1)}, bf16[256,2048]{1,0:T(8,128)(2,1)S(1)}, u32[]{:S(2)}, u32[]{:S(2)}) collective-permute-start(bf16[256,2048]{1,0:T(8,128)(2,1)S(1)} %bitcast.34), channel_id=1, source_target_pairs={{0,8},{8,0},{1,9},{9,1},{2,10},{10,2},{3,11},{11,3},{4,12},{12,4},... | collective-permute-start | bytes 3145736 | tf_op jit(solution)/shard_map/ppermute | solution.py:275
  113.8 0.1 reduce
  114.0 0.8 shard_map.106.refs_0_
  114.8 0.8 select_bitcast_fusion
  115.5 0.6 collective-permute-done.4.rows_ref
  116.1 1.6 %shard_map.107 = bf16[128,4096]{1,0:T(8,128)(2,1)} custom-call(s32[128,1]{1,0:T(8,128)S(1)} %copy.22.target_ref, s32[1,256]{1,0:T(1,128)S(1)} %get-tuple-element.31.key_ref, bf16[256,2048]{1,0:T(8,128)(2,1)S(1)} %collective-permute-done.4.rows_ref, bf16[128,4096]{1,0:T(8,128)(2,1)S(1)} %shard_map.106.refs_0_), custom_call_target="tpu_custom_call" | custom-call | flops 268435456 | bytes 2097152 | tf_op jit(solution)/shard_map/pallas_call | solution.py:201
  (27 shorter events, 0.3 us)
Async XLA Ops:
  0.6 14.2 %copy-start.3 = (bf16[512,512]{1,0:T(8,128)(2,1)S(1)}, bf16[512,512]{1,0:T(8,128)(2,1)}, u32[]{:S(2)}) copy-start(bf16[512,512]{1,0:T(8,128)(2,1)} %param.7) | copy-start | bytes 1572868
  2.4 23.0 %all-to-all-start = ((bf16[4,512,128]{2,1,0:T(8,128)(2,1)}), bf16[4,512,128]{2,1,0:T(8,128)(2,1)S(1)}, u32[]{:S(2)}, u32[]{:S(2)}) async-start(bf16[4,512,128]{2,1,0:T(8,128)(2,1)} %shard_map.102), calls=%async_computation | async-start | bytes 1048576 | tf_op jit(solution)/shard_map/all_to_all | solution.py:222
  14.9 20.0 %collective-permute-start.3 = (bf16[512,256]{1,0:T(8,128)(2,1)S(1)}, bf16[512,256]{1,0:T(8,128)(2,1)S(1)}, u32[]{:S(2)}, u32[]{:S(2)}) collective-permute-start(bf16[512,256]{1,0:T(8,128)(2,1)S(1)} %get-tuple-element.40), channel_id=1, source_target_pairs={{0,9},{1,10},{2,11},{3,12},{4,13},{5,14},{6,15},{7,8},{8,7},{9,0},... | collective-permute-start | bytes 786440 | tf_op jit(solution)/shard_map/ppermute | solution.py:237
  21.5 13.3 %collective-permute-start.1 = (bf16[512,256]{1,0:T(8,128)(2,1)S(1)}, bf16[512,256]{1,0:T(8,128)(2,1)S(1)}, u32[]{:S(2)}, u32[]{:S(2)}) collective-permute-start(bf16[512,256]{1,0:T(8,128)(2,1)S(1)} %get-tuple-element.40), channel_id=1, source_target_pairs={{0,8},{8,0},{1,9},{9,1},{2,10},{10,2},{3,11},{11,3},{4,12},{12,4},... | collective-permute-start | bytes 786440 | tf_op jit(solution)/shard_map/ppermute | solution.py:237
  23.5 11.4 %collective-permute-start.2 = (bf16[512,256]{1,0:T(8,128)(2,1)S(1)}, bf16[512,256]{1,0:T(8,128)(2,1)S(1)}, u32[]{:S(2)}, u32[]{:S(2)}) collective-permute-start(bf16[512,256]{1,0:T(8,128)(2,1)S(1)} %get-tuple-element.41.act_ref), channel_id=1, source_target_pairs={{0,7},{1,0},{2,1},{3,2},{4,3},{5,4},{6,5},{7,6},{8,9},{9,10},{10,1... | collective-permute-start | bytes 786440 | tf_op jit(solution)/shard_map/ppermute | solution.py:236
  25.4 9.5 %collective-permute-start = (bf16[4,512,128]{2,1,0:T(8,128)(2,1)S(1)}, bf16[4,512,128]{2,1,0:T(8,128)(2,1)S(1)}, u32[]{:S(2)}, u32[]{:S(2)}) collective-permute-start(bf16[4,512,128]{2,1,0:T(8,128)(2,1)S(1)} %all-to-all-done.cot_ref.here_ref), channel_id=1, source_target_pairs={{0,8},{8,0},{1,9},{9,1},{2,10},{10,2},{3,11},{11,3},{4,12},{12,4},... | collective-permute-start | bytes 1572872 | tf_op jit(solution)/shard_map/ppermute | solution.py:238
  56.4 21.6 %copy-start = (f32[1,1,4,4096]{3,2,1,0:T(4,128)S(1)}, f32[1,1,4,4096]{3,2,1,0:T(4,128)}, u32[]{:S(2)}) copy-start(f32[1,1,4,4096]{3,2,1,0:T(4,128)} %param.11) | copy-start | bytes 196612
  56.4 21.6 %copy-start.1 = (f32[1,1,4,4096]{3,2,1,0:T(4,128)S(1)}, f32[1,1,4,4096]{3,2,1,0:T(4,128)}, u32[]{:S(2)}) copy-start(f32[1,1,4,4096]{3,2,1,0:T(4,128)} %param.13) | copy-start | bytes 196612
  56.5 21.6 %copy-start.2 = (f32[1,1,2]{2,1,0:T(1,128)S(1)}, f32[1,1,2]{2,1,0:T(1,128)}, u32[]{:S(2)}) copy-start(f32[1,1,2]{2,1,0:T(1,128)} %param.12) | copy-start | bytes 28
  107.2 8.9 %collective-permute-start.4 = (bf16[256,2048]{1,0:T(8,128)(2,1)S(1)}, bf16[256,2048]{1,0:T(8,128)(2,1)S(1)}, u32[]{:S(2)}, u32[]{:S(2)}) collective-permute-start(bf16[256,2048]{1,0:T(8,128)(2,1)S(1)} %bitcast.34), channel_id=1, source_target_pairs={{0,8},{8,0},{1,9},{9,1},{2,10},{10,2},{3,11},{11,3},{4,12},{12,4},... | collective-permute-start | bytes 3145736 | tf_op jit(solution)/shard_map/ppermute | solution.py:275

commit v10 on v9

--- a/solution.py
+++ b/solution.py
@@ -186,7 +186,7 @@
 
 
 def place_kernel(target_ref, key_ref, rows_ref, *refs):
-    want = target_ref[...] * CUT + pl.program_id(0)
+    want = target_ref[...] * CUT + pl.program_id(1)
     pick = jnp.where(want == key_ref[...], 1.0, 0.0).astype(jnp.bfloat16)
     placed = jnp.dot(pick, rows_ref[...], preferred_element_type=jnp.float32)
     for ref in refs[:-1]:
@@ -196,13 +196,16 @@
 
 def place_rows(target, key, rows, *placed):
     count, piece = rows.shape
-    whole = lambda shape: pl.BlockSpec(shape, lambda j: (0, 0))
-    piece_spec = pl.BlockSpec((HD, piece), lambda j: (0, j))
+    whole = lambda shape: pl.BlockSpec(shape, lambda i, j: (0, 0))
+    parts = 2
+    part = piece // parts
+    part_spec = pl.BlockSpec((HD, part), lambda i, j: (0, j * parts + i))
+    rows_spec = pl.BlockSpec((count, part), lambda i, j: (0, i))
     return pl.pallas_call(
         place_kernel,
-        grid=(CUT,),
-        in_specs=[whole((HD, 1)), whole((1, count)), whole((count, piece))] + [piece_spec] * len(placed),
-        out_specs=piece_spec,
+        grid=(parts, CUT),
+        in_specs=[whole((HD, 1)), whole((1, count)), rows_spec] + [part_spec] * len(placed),
+        out_specs=part_spec,
         out_shape=jax.ShapeDtypeStruct((HD, CUT * piece), jnp.bfloat16),
         compiler_params=PARAMS,
         cost_estimate=cost(2 * CUT * HD * count * piece, 2 * 2**20),
@@ -226,15 +229,17 @@
     target, row_rank = jax.vmap(partial(block_tables, capacity=capacity))(
         of_side(block_start), of_side(block_owner)
     )
+    keep = lax.dynamic_slice_in_dim(activations, core * half, half, 1)
     target, activations = lax.optimization_barrier((target, activations))
-    keep = lax.dynamic_slice_in_dim(activations, core * half, half, 1)
     give = lax.dynamic_slice_in_dim(activations, (1 - core) * half, half, 1)
     depth = PAIR * pairs
     to_chip = lambda core_to, z: core_to * depth + (z + 2 * core_to - 1) % depth
     same = [(c * depth + z, to_chip(c, z)) for c in range(nc) for z in range(depth)]
     cross = [(c * depth + z, to_chip(1 - c, z)) for c in range(nc) for z in range(depth)]
     act_here = (keep, lax.ppermute(keep, ("c", "zh", "zl"), same))
-    act_other = (lax.ppermute(give, "c", SWAP), lax.ppermute(give, ("c", "zh", "zl"), cross))
+    far = lax.ppermute(give, ("c", "zh", "zl"), cross)
+    row_rank, give = lax.optimization_barrier((row_rank + 0 * target, give))
+    act_other = (lax.ppermute(give, "c", SWAP), far)
     cot_other = lax.ppermute(cot_here, "c", SWAP)
 
     target_here = lax.dynamic_index_in_dim(target, pair, 0, keepdims=False)

time: 118 us -> 122 us (1.034)
  starting transfers between devices: 33.3 us -> 36.6 us
  waiting for transfers between devices: 4.12 us -> 2.51 us
  Pallas kernels: 7.52 us -> 8.75 us
    ppermute x2, waiting for transfers between devices: 3.52 us -> 0.01 us  [the longest x1 0.01 us: body(): far = lax.ppermute(give, ('c', 'zh', 'zl'), cross)]
    ppermute x1, starting transfers between devices: 1.92 us -> 4.83 us  [body(): act_here = (keep, lax.ppermute(keep, ('c', 'zh', 'zl'), same))]
    ppermute x1, starting transfers between devices: 5.32 us -> 8.09 us  [body(): cot_other = lax.ppermute(cot_here, 'c', SWAP)]
    all_to_all x1, starting transfers between devices: 10.9 us -> 9.13 us  [body(): lax.all_to_all(copies_in_hbm(cotangent, pairs), 'zh', 0, 0, tiled=True)]
    all_to_all x1, waiting for transfers between devices: 0.01 us -> 1.53 us  [body(): lax.all_to_all(copies_in_hbm(cotangent, pairs), 'zh', 0, 0, tiled=True)]
    pallas_call x2, Pallas kernels: 2.39 us -> 3.69 us  [place_rows(): pl.pallas_call(place_kernel, grid=(parts, CUT), in_specs=[whole((HD, 1)),...]
  transfers between devices with their start and end apart: 6 -> 6, of which waited for: 2 -> 3; matrix products, arithmetic and copies ran while one was open for 2% -> 2% of each run, Pallas kernels for 1% -> 3%
where the time goes in v10:
time: 122 us
  blocking collectives  68.6 us (56%)
  starting transfers between devices  36.6 us (30%)
  Pallas kernels  8.75 us (7%)
  other arithmetic  2.56 us (2%)
  waiting for transfers between devices  2.51 us (2%)
  local copies, waits for them, and re-layouts  1.56 us (1%)
    all_to_all x2, blocking collectives, copies_to_all(): lax.all_to_all(jnp.broadcast_to(block[None], (count,) + block.shape), axi...  27.7 us
    all_to_all x1, blocking collectives, body(): lax.all_to_all(jnp.swapaxes(send, 0, 1), ('y', 'zh'), 0, 0, tiled=True)  21.4 us
    all_to_all x1, blocking collectives, body(): got = lax.all_to_all(send, ('x', 'c'), 0, 0, tiled=True)  19.5 us
    all_to_all x1, starting transfers between devices, body(): lax.all_to_all(copies_in_hbm(cotangent, pairs), 'zh', 0, 0, tiled=True)  9.13 us
    ppermute x1, starting transfers between devices, body(): cot_other = lax.ppermute(cot_here, 'c', SWAP)  8.09 us
    ppermute x1, starting transfers between devices, body(): low_other = lax.ppermute(low, 'c', SWAP)  6.65 us
    ppermute x1, starting transfers between devices, body(): far = lax.ppermute(give, ('c', 'zh', 'zl'), cross)  5.97 us
    ppermute x1, starting transfers between devices, body(): act_here = (keep, lax.ppermute(keep, ('c', 'zh', 'zl'), same))  4.83 us
  transfers between devices with their start and end apart: 6, of which 3 were waited for; matrix products, arithmetic and copies ran while one was open for 2% of the time, Pallas kernels for 3%

profile of v10, /device:TPU:1, one launch (start us, length us, event | category | flops | bytes accessed | tf_op | source)
XLA Modules:
  0.0 121.6 jit_solution(3714849117242458706)
XLA Ops:
  0.7 1.0 copy-done
  1.7 4.8 %collective-permute-start.2 = (bf16[512,256]{1,0:T(8,128)(2,1)S(1)}, bf16[512,256]{1,0:T(8,128)(2,1)S(1)}, u32[]{:S(2)}, u32[]{:S(2)}) collective-permute-start(bf16[512,256]{1,0:T(8,128)(2,1)S(1)} %constant_dynamic-slice_fusion.3.act_ref), channel_id=1, source_target_pairs={{0,7},{1,0},{2,1},{3,2},{4,3},{5,4},{6,5},{7,6},{8,9},{9,10},{10,1... | collective-permute-start | bytes 786440 | tf_op jit(solution)/shard_map/ppermute | solution.py:239
  6.5 1.7 %shard_map.102 = bf16[4,512,128]{2,1,0:T(8,128)(2,1)} custom-call(bf16[512,128]{1,0:T(8,128)(2,1)} %block_ref.1), custom_call_target="tpu_custom_call" | custom-call | bytes 1048576 | tf_op jit(solution)/shard_map/pallas_call | solution.py:124
  8.3 9.1 %all-to-all-start = ((bf16[4,512,128]{2,1,0:T(8,128)(2,1)}), bf16[4,512,128]{2,1,0:T(8,128)(2,1)S(1)}, u32[]{:S(2)}, u32[]{:S(2)}) async-start(bf16[4,512,128]{2,1,0:T(8,128)(2,1)} %shard_map.102), calls=%async_computation | async-start | bytes 1048576 | tf_op jit(solution)/shard_map/all_to_all | solution.py:225
  17.5 0.1 convert_reduce_fusion.3
  17.6 0.3 convert_reduce_fusion.2
  17.9 0.2 select_reduce_fusion
  18.0 0.2 convert_reduce_fusion.1
  18.3 6.0 %collective-permute-start.3 = (bf16[512,256]{1,0:T(8,128)(2,1)S(1)}, bf16[512,256]{1,0:T(8,128)(2,1)S(1)}, u32[]{:S(2)}, u32[]{:S(2)}) collective-permute-start(bf16[512,256]{1,0:T(8,128)(2,1)S(1)} %constant_dynamic-slice_fusion.2), channel_id=1, source_target_pairs={{0,9},{1,10},{2,11},{3,12},{4,13},{5,14},{6,15},{7,8},{8,7},{9,0},... | collective-permute-start | bytes 786440 | tf_op jit(solution)/shard_map/ppermute | solution.py:240
  24.3 1.9 %collective-permute-start.1 = (bf16[512,256]{1,0:T(8,128)(2,1)S(1)}, bf16[512,256]{1,0:T(8,128)(2,1)S(1)}, u32[]{:S(2)}, u32[]{:S(2)}) collective-permute-start(bf16[512,256]{1,0:T(8,128)(2,1)S(1)} %constant_dynamic-slice_fusion.2), channel_id=1, source_target_pairs={{0,8},{8,0},{1,9},{9,1},{2,10},{10,2},{3,11},{11,3},{4,12},{12,4},... | collective-permute-start | bytes 786440 | tf_op jit(solution)/shard_map/ppermute | solution.py:242
  26.2 1.5 %all-to-all-done.cot_ref.here_ref = bf16[4,512,128]{2,1,0:T(8,128)(2,1)S(1)} async-done(((bf16[4,512,128]{2,1,0:T(8,128)(2,1)}), bf16[4,512,128]{2,1,0:T(8,128)(2,1)S(1)}, u32[]{:S(2)}, u32[]{:S(2)}) %all-to-all-start) | async-done | bytes 524320 | tf_op jit(solution)/shard_map/all_to_all | solution.py:225
  27.8 8.1 %collective-permute-start = (bf16[4,512,128]{2,1,0:T(8,128)(2,1)S(1)}, bf16[4,512,128]{2,1,0:T(8,128)(2,1)S(1)}, u32[]{:S(2)}, u32[]{:S(2)}) collective-permute-start(bf16[4,512,128]{2,1,0:T(8,128)(2,1)S(1)} %all-to-all-done.cot_ref.here_ref), channel_id=1, source_target_pairs={{0,8},{8,0},{1,9},{9,1},{2,10},{10,2},{3,11},{11,3},{4,12},{12,4},... | collective-permute-start | bytes 1572872 | tf_op jit(solution)/shard_map/ppermute | solution.py:243
  35.9 0.2 select_reduce_fusion.2.rank_ref
  36.1 0.3 shard_map.103.first_ref
  36.5 0.9 collective-permute-done.other_ref
  37.4 1.8 %shard_map.104 = f32[8,8,4,8,256]{4,3,2,1,0:T(8,128)S(1)} custom-call(s32[4,1,128]{2,1,0:T(1,128)S(1)} %bitcast.38, f32[4,128,256]{2,1,0:T(8,128)S(1)} %shard_map.103.first_ref, bf16[4,512,128]{2,1,0:T(8,128)(2,1)S(1)} %all-to-all-done.cot_ref.here_ref, bf16[4,512,128]{2,1,0:T(8,128)(2,1)S(1)} %collective-permute-done.other_ref, ...), custom_call_target="tpu_custom_call" | custom-call | flops 671088640 | bytes 4194304 | tf_op jit(solution)/shard_map/pallas_call | solution.py:178
  39.2 0.3 convert_element_type.37
  39.5 19.5 %all_to_all.25 = f16[8,32,8,256]{3,2,1,0:T(8,128)(2,1)S(1)} all-to-all(f16[8,32,8,256]{3,2,1,0:T(8,128)(2,1)S(1)} %bitcast.40), channel_id=1, replica_groups=mesh['x'=4,'y'=8,'c'=2,'zh'=4,'zl'=2] {'x','c'}, dimensions={0} | all-to-all | bytes 2097152 | tf_op jit(solution)/shard_map/all_to_all | solution.py:262
  59.1 0.1 convert_reduce_fusion
  59.3 21.4 %all_to_all.26 = f16[32,2,8,256]{3,2,1,0:T(8,128)(2,1)S(1)} all-to-all(f16[32,2,8,256]{3,2,1,0:T(8,128)(2,1)S(1)} %copy.20), channel_id=1, replica_groups=mesh['x'=4,'y'=8,'c'=2,'zh'=4,'zl'=2] {'y','zh'}, dimensions={0} | all-to-all | bytes 524288 | tf_op jit(solution)/shard_map/all_to_all | solution.py:265
  80.8 0.1 reshape.204
  81.0 0.1 reduce_sum.69
  81.1 1.2 shard_map.105
  82.3 14.0 %all_to_all.27 = bf16[8,8,2048]{2,1,0:T(8,128)(2,1)S(1)} all-to-all(bf16[8,8,2048]{2,1,0:T(8,128)(2,1)S(1)} %broadcast_in_dim.108), channel_id=1, replica_groups=mesh['x'=4,'y'=8,'c'=2,'zh'=4,'zl'=2] {'y'}, dimensions={0} | all-to-all | bytes 524288 | tf_op jit(solution)/shard_map/all_to_all | solution.py:102
  96.3 0.1 broadcast_in_dim.109
  96.4 13.7 %all_to_all.28 = bf16[4,8,8,2048]{3,2,1,0:T(8,128)(2,1)S(1)} all-to-all(bf16[4,8,8,2048]{3,2,1,0:T(8,128)(2,1)S(1)} %broadcast_in_dim.109), channel_id=1, replica_groups=mesh['x'=4,'y'=8,'c'=2,'zh'=4,'zl'=2] {'x'}, dimensions={0} | all-to-all | bytes 2097152 | tf_op jit(solution)/shard_map/all_to_all | solution.py:102
  110.2 0.1 copy.22.target_ref
  110.3 6.6 %collective-permute-start.4 = (bf16[256,2048]{1,0:T(8,128)(2,1)S(1)}, bf16[256,2048]{1,0:T(8,128)(2,1)S(1)}, u32[]{:S(2)}, u32[]{:S(2)}) collective-permute-start(bf16[256,2048]{1,0:T(8,128)(2,1)S(1)} %bitcast.34), channel_id=1, source_target_pairs={{0,8},{8,0},{1,9},{9,1},{2,10},{10,2},{3,11},{11,3},{4,12},{12,4},... | collective-permute-start | bytes 3145736 | tf_op jit(solution)/shard_map/ppermute | solution.py:280
  116.9 0.1 reduce
  117.0 1.3 %shard_map.106.refs_0_ = bf16[128,4096]{1,0:T(8,128)(2,1)S(1)} custom-call(s32[128,1]{1,0:T(8,128)S(1)} %copy.22.target_ref, s32[1,256]{1,0:T(1,128)S(1)} %get-tuple-element.37.key_ref, bf16[256,2048]{1,0:T(8,128)(2,1)S(1)} %bitcast.35), custom_call_target="tpu_custom_call" | custom-call | flops 268435456 | bytes 2097152 | tf_op jit(solution)/shard_map/pallas_call | solution.py:204
  118.4 0.8 select_bitcast_fusion
  119.2 2.4 %shard_map.107 = bf16[128,4096]{1,0:T(8,128)(2,1)} custom-call(s32[128,1]{1,0:T(8,128)S(1)} %copy.22.target_ref, s32[1,256]{1,0:T(1,128)S(1)} %get-tuple-element.35.key_ref, bf16[256,2048]{1,0:T(8,128)(2,1)S(1)} %collective-permute-done.4.rows_ref, bf16[128,4096]{1,0:T(8,128)(2,1)S(1)} %shard_map.106.refs_0_), custom_call_target="tpu_custom_call" | custom-call | flops 268435456 | bytes 2097152 | tf_op jit(solution)/shard_map/pallas_call | solution.py:204
  (32 shorter events, 0.4 us)
Async XLA Ops:
  0.6 1.0 copy-start
  0.6 16.8 %copy-start.4 = (s32[8,80]{1,0:T(8,128)S(1)}, s32[8,80]{1,0:T(8,128)}, u32[]{:S(2)}) copy-start(s32[8,80]{1,0:T(8,128)} %param.10) | copy-start | bytes 7684
  0.7 16.8 %copy-start.5 = (s32[8,80]{1,0:T(8,128)S(1)}, s32[8,80]{1,0:T(8,128)}, u32[]{:S(2)}) copy-start(s32[8,80]{1,0:T(8,128)} %param.9) | copy-start | bytes 7684
  1.7 34.8 %collective-permute-start.2 = (bf16[512,256]{1,0:T(8,128)(2,1)S(1)}, bf16[512,256]{1,0:T(8,128)(2,1)S(1)}, u32[]{:S(2)}, u32[]{:S(2)}) collective-permute-start(bf16[512,256]{1,0:T(8,128)(2,1)S(1)} %constant_dynamic-slice_fusion.3.act_ref), channel_id=1, source_target_pairs={{0,7},{1,0},{2,1},{3,2},{4,3},{5,4},{6,5},{7,6},{8,9},{9,10},{10,1... | collective-permute-start | bytes 786440 | tf_op jit(solution)/shard_map/ppermute | solution.py:239
  8.3 19.5 %all-to-all-start = ((bf16[4,512,128]{2,1,0:T(8,128)(2,1)}), bf16[4,512,128]{2,1,0:T(8,128)(2,1)S(1)}, u32[]{:S(2)}, u32[]{:S(2)}) async-start(bf16[4,512,128]{2,1,0:T(8,128)(2,1)} %shard_map.102), calls=%async_computation | async-start | bytes 1048576 | tf_op jit(solution)/shard_map/all_to_all | solution.py:225
  18.3 18.2 %collective-permute-start.3 = (bf16[512,256]{1,0:T(8,128)(2,1)S(1)}, bf16[512,256]{1,0:T(8,128)(2,1)S(1)}, u32[]{:S(2)}, u32[]{:S(2)}) collective-permute-start(bf16[512,256]{1,0:T(8,128)(2,1)S(1)} %constant_dynamic-slice_fusion.2), channel_id=1, source_target_pairs={{0,9},{1,10},{2,11},{3,12},{4,13},{5,14},{6,15},{7,8},{8,7},{9,0},... | collective-permute-start | bytes 786440 | tf_op jit(solution)/shard_map/ppermute | solution.py:240
  24.3 12.2 %collective-permute-start.1 = (bf16[512,256]{1,0:T(8,128)(2,1)S(1)}, bf16[512,256]{1,0:T(8,128)(2,1)S(1)}, u32[]{:S(2)}, u32[]{:S(2)}) collective-permute-start(bf16[512,256]{1,0:T(8,128)(2,1)S(1)} %constant_dynamic-slice_fusion.2), channel_id=1, source_target_pairs={{0,8},{8,0},{1,9},{9,1},{2,10},{10,2},{3,11},{11,3},{4,12},{12,4},... | collective-permute-start | bytes 786440 | tf_op jit(solution)/shard_map/ppermute | solution.py:242
  27.8 9.6 %collective-permute-start = (bf16[4,512,128]{2,1,0:T(8,128)(2,1)S(1)}, bf16[4,512,128]{2,1,0:T(8,128)(2,1)S(1)}, u32[]{:S(2)}, u32[]{:S(2)}) collective-permute-start(bf16[4,512,128]{2,1,0:T(8,128)(2,1)S(1)} %all-to-all-done.cot_ref.here_ref), channel_id=1, source_target_pairs={{0,8},{8,0},{1,9},{9,1},{2,10},{10,2},{3,11},{11,3},{4,12},{12,4},... | collective-permute-start | bytes 1572872 | tf_op jit(solution)/shard_map/ppermute | solution.py:243
  59.2 21.9 %copy-start.1 = (f32[1,1,4,4096]{3,2,1,0:T(4,128)S(1)}, f32[1,1,4,4096]{3,2,1,0:T(4,128)}, u32[]{:S(2)}) copy-start(f32[1,1,4,4096]{3,2,1,0:T(4,128)} %param.11) | copy-start | bytes 196612
  59.2 21.9 %copy-start.2 = (f32[1,1,4,4096]{3,2,1,0:T(4,128)S(1)}, f32[1,1,4,4096]{3,2,1,0:T(4,128)}, u32[]{:S(2)}) copy-start(f32[1,1,4,4096]{3,2,1,0:T(4,128)} %param.13) | copy-start | bytes 196612
  59.2 21.9 %copy-start.3 = (f32[1,1,2]{2,1,0:T(1,128)S(1)}, f32[1,1,2]{2,1,0:T(1,128)}, u32[]{:S(2)}) copy-start(f32[1,1,2]{2,1,0:T(1,128)} %param.12) | copy-start | bytes 28
  110.3 8.9 %collective-permute-start.4 = (bf16[256,2048]{1,0:T(8,128)(2,1)S(1)}, bf16[256,2048]{1,0:T(8,128)(2,1)S(1)}, u32[]{:S(2)}, u32[]{:S(2)}) collective-permute-start(bf16[256,2048]{1,0:T(8,128)(2,1)S(1)} %bitcast.34), channel_id=1, source_target_pairs={{0,8},{8,0},{1,9},{9,1},{2,10},{10,2},{3,11},{11,3},{4,12},{12,4},... | collective-permute-start | bytes 3145736 | tf_op jit(solution)/shard_map/ppermute | solution.py:280

commit v11 on v9

--- a/solution.py
+++ b/solution.py
@@ -110,27 +110,6 @@
     return pl.CostEstimate(flops=flops, bytes_accessed=moved, transcendentals=0)
 
 
-def copies_kernel(block_ref, out_ref, sems):
-    copies = [
-        pltpu.make_async_copy(block_ref, out_ref.at[i], sems.at[i]) for i in range(out_ref.shape[0])
-    ]
-    for copy in copies:
-        copy.start()
-    for copy in copies:
-        copy.wait()
-
-
-def copies_in_hbm(block, count):
-    return pl.pallas_call(
-        copies_kernel,
-        in_specs=[pl.BlockSpec(memory_space=pltpu.VMEM)],
-        out_specs=pl.BlockSpec(memory_space=pl.ANY),
-        out_shape=jax.ShapeDtypeStruct((count,) + block.shape, block.dtype),
-        scratch_shapes=[pltpu.SemaphoreType.DMA((count,))],
-        cost_estimate=cost(0, 2**20),
-    )(block)
-
-
 def first_kernel(cot_ref, act_ref, out_ref):
     for head in range(cot_ref.shape[0]):
         out_ref[head] = lax.dot_general(
@@ -185,25 +164,48 @@
     )(target[:, None, :], first, cot_here, cot_other, act_other[0], act_here[1], act_other[1])
 
 
-def place_kernel(target_ref, key_ref, rows_ref, *refs):
-    want = target_ref[...] * CUT + pl.program_id(0)
-    pick = jnp.where(want == key_ref[...], 1.0, 0.0).astype(jnp.bfloat16)
-    placed = jnp.dot(pick, rows_ref[...], preferred_element_type=jnp.float32)
-    for ref in refs[:-1]:
-        placed += ref[...].astype(jnp.float32)
-    refs[-1][...] = placed.astype(jnp.bfloat16)
+def placed_part(target_ref, key_ref, rows_ref, cut, span):
+    pick = jnp.where(target_ref[...] * CUT + cut == key_ref[...], 1.0, 0.0).astype(jnp.bfloat16)
+    return jnp.dot(pick, rows_ref[:, span], preferred_element_type=jnp.float32)
+
+
+def place_kernel(target_ref, key_ref, rows_ref, out_ref):
+    piece = rows_ref.shape[1]
+    for cut in range(CUT):
+        part = placed_part(target_ref, key_ref, rows_ref, cut, slice(0, piece))
+        out_ref[:, cut * piece : (cut + 1) * piece] = part.astype(jnp.bfloat16)
+
+
+def merge_kernel(target_ref, key_ref, rows_ref, placed_ref, out_ref, parts_ref, sems):
+    count, _, part = parts_ref.shape
+    copies = []
+    for i in range(count):
+        place = i * part % rows_ref.shape[1]
+        rows = placed_part(
+            target_ref, key_ref, rows_ref, i * part // rows_ref.shape[1], slice(place, place + part)
+        )
+        span = slice(i * part, (i + 1) * part)
+        parts_ref[i] = (rows + placed_ref[:, span].astype(jnp.float32)).astype(jnp.bfloat16)
+        copies.append(pltpu.make_async_copy(parts_ref.at[i], out_ref.at[:, span], sems.at[i]))
+        copies[-1].start()
+    for copy in copies:
+        copy.wait()
 
 
 def place_rows(target, key, rows, *placed):
     count, piece = rows.shape
-    whole = lambda shape: pl.BlockSpec(shape, lambda j: (0, 0))
-    piece_spec = pl.BlockSpec((HD, piece), lambda j: (0, j))
+    width, parts = CUT * piece, 2 * CUT
+    vmem = pl.BlockSpec(memory_space=pltpu.VMEM)
+    scratch = [
+        pltpu.VMEM((parts, HD, width // parts), jnp.bfloat16),
+        pltpu.SemaphoreType.DMA((parts,)),
+    ]
     return pl.pallas_call(
-        place_kernel,
-        grid=(CUT,),
-        in_specs=[whole((HD, 1)), whole((1, count)), whole((count, piece))] + [piece_spec] * len(placed),
-        out_specs=piece_spec,
-        out_shape=jax.ShapeDtypeStruct((HD, CUT * piece), jnp.bfloat16),
+        merge_kernel if placed else place_kernel,
+        in_specs=[vmem] * (3 + len(placed)),
+        out_specs=pl.BlockSpec(memory_space=pl.ANY) if placed else vmem,
+        out_shape=jax.ShapeDtypeStruct((HD, width), jnp.bfloat16),
+        scratch_shapes=scratch if placed else [],
         compiler_params=PARAMS,
         cost_estimate=cost(2 * CUT * HD * count * piece, 2 * 2**20),
     )(target, key, rows, *placed)
@@ -219,7 +221,7 @@
     owner_here = chip * nc + core
     half = activations.shape[1] // 2
 
-    cot_here = lax.all_to_all(copies_in_hbm(cotangent, pairs), "zh", 0, 0, tiled=True)
+    cot_here = copies_to_all(cotangent, "zh")
     def of_side(table):
         return lax.dynamic_index_in_dim(table.reshape(pairs, PAIR, -1), side, 1, keepdims=False)
 

time: 118 us -> 118 us (level)
  Pallas kernels: 7.52 us -> 5.13 us
  local copies, waits for them, and re-layouts: 1.25 us -> 3.07 us
    pallas_call x3 -> x2, Pallas kernels: 4.17 us -> 1.78 us  [place_rows(): pl.pallas_call(merge_kernel if placed else place_kernel, in_specs=[vmem]...]
    broadcast_in_dim x2 -> x3, local copies, waits for them, and re-layouts: 0.13 us -> 1.95 us  [copies_to_all(): jnp.broadcast_to(block[None], (count,) + block.shape)]
where the time goes in v11:
time: 118 us; the launch traced here: 117 us
  blocking collectives  68.1 us (58%)
  starting transfers between devices  33.2 us (28%)
  Pallas kernels  5.13 us (4%)
  waiting for transfers between devices  4.42 us (4%)
  local copies, waits for them, and re-layouts  3.07 us (3%)
  other arithmetic  2.56 us (2%)
    all_to_all x2, blocking collectives, copies_to_all(): lax.all_to_all(jnp.broadcast_to(block[None], (count,) + block.shape), axi...  27.7 us
    all_to_all x1, blocking collectives, body(): lax.all_to_all(jnp.swapaxes(send, 0, 1), ('y', 'zh'), 0, 0, tiled=True)  21.1 us
    all_to_all x1, blocking collectives, body(): got = lax.all_to_all(send, ('x', 'c'), 0, 0, tiled=True)  19.3 us
    all_to_all x1, starting transfers between devices, copies_to_all(): lax.all_to_all(jnp.broadcast_to(block[None], (count,) + block.shape), axi...  10.8 us
    ppermute x1, starting transfers between devices, body(): low_other = lax.ppermute(low, 'c', SWAP)  6.63 us
    ppermute x1, starting transfers between devices, body(): lax.ppermute(give, ('c', 'zh', 'zl'), cross)  6.61 us
    ppermute x1, starting transfers between devices, body(): cot_other = lax.ppermute(cot_here, 'c', SWAP)  5.32 us
    ppermute x1, waiting for transfers between devices, body(): lax.ppermute(give, ('c', 'zh', 'zl'), cross)  3.52 us
  transfers between devices with their start and end apart: 6, of which 2 were waited for; matrix products, arithmetic and copies ran while one was open for 2% of the time, Pallas kernels for 1%

profile of v11, /device:TPU:1, one launch (start us, length us, event | category | flops | bytes accessed | tf_op | source)
XLA Modules:
  0.0 117.4 jit_solution(16015823980326660868)
XLA Ops:
  0.6 1.8 %broadcast_in_dim.110 = bf16[4,512,128]{2,1,0:T(8,128)(2,1)} broadcast(bf16[512,128]{1,0:T(8,128)(2,1)} %param.8), dimensions={1,2} | broadcast | bytes 655360 | tf_op jit(solution)/shard_map/broadcast_in_dim | solution.py:102
  2.5 10.8 %all-to-all-start = ((bf16[4,512,128]{2,1,0:T(8,128)(2,1)}), bf16[4,512,128]{2,1,0:T(8,128)(2,1)S(1)}, u32[]{:S(2)}, u32[]{:S(2)}) async-start(bf16[4,512,128]{2,1,0:T(8,128)(2,1)} %broadcast_in_dim.110), calls=%async_computation | async-start | bytes 1048576 | tf_op jit(solution)/shard_map/all_to_all | solution.py:102
  13.3 0.7 constant_dynamic-slice_fusion.4
  14.0 0.1 convert_reduce_fusion.3
  14.2 0.3 convert_reduce_fusion.2
  14.5 0.2 select_reduce_fusion
  14.6 0.2 convert_reduce_fusion.1
  14.9 6.6 %collective-permute-start.3 = (bf16[512,256]{1,0:T(8,128)(2,1)S(1)}, bf16[512,256]{1,0:T(8,128)(2,1)S(1)}, u32[]{:S(2)}, u32[]{:S(2)}) collective-permute-start(bf16[512,256]{1,0:T(8,128)(2,1)S(1)} %get-tuple-element.40), channel_id=1, source_target_pairs={{0,9},{1,10},{2,11},{3,12},{4,13},{5,14},{6,15},{7,8},{8,7},{9,0},... | collective-permute-start | bytes 786440 | tf_op jit(solution)/shard_map/ppermute | solution.py:239
  21.6 1.9 %collective-permute-start.1 = (bf16[512,256]{1,0:T(8,128)(2,1)S(1)}, bf16[512,256]{1,0:T(8,128)(2,1)S(1)}, u32[]{:S(2)}, u32[]{:S(2)}) collective-permute-start(bf16[512,256]{1,0:T(8,128)(2,1)S(1)} %get-tuple-element.40), channel_id=1, source_target_pairs={{0,8},{8,0},{1,9},{9,1},{2,10},{10,2},{3,11},{11,3},{4,12},{12,4},... | collective-permute-start | bytes 786440 | tf_op jit(solution)/shard_map/ppermute | solution.py:239
  23.5 1.9 %collective-permute-start.2 = (bf16[512,256]{1,0:T(8,128)(2,1)S(1)}, bf16[512,256]{1,0:T(8,128)(2,1)S(1)}, u32[]{:S(2)}, u32[]{:S(2)}) collective-permute-start(bf16[512,256]{1,0:T(8,128)(2,1)S(1)} %get-tuple-element.41.act_ref), channel_id=1, source_target_pairs={{0,7},{1,0},{2,1},{3,2},{4,3},{5,4},{6,5},{7,6},{8,9},{9,10},{10,1... | collective-permute-start | bytes 786440 | tf_op jit(solution)/shard_map/ppermute | solution.py:238
  25.4 5.3 %collective-permute-start = (bf16[4,512,128]{2,1,0:T(8,128)(2,1)S(1)}, bf16[4,512,128]{2,1,0:T(8,128)(2,1)S(1)}, u32[]{:S(2)}, u32[]{:S(2)}) collective-permute-start(bf16[4,512,128]{2,1,0:T(8,128)(2,1)S(1)} %all-to-all-done.cot_ref.here_ref), channel_id=1, source_target_pairs={{0,8},{8,0},{1,9},{9,1},{2,10},{10,2},{3,11},{11,3},{4,12},{12,4},... | collective-permute-start | bytes 1572872 | tf_op jit(solution)/shard_map/ppermute | solution.py:240
  30.8 0.2 select_reduce_fusion.2.rank_ref
  31.0 0.3 shard_map.102.first_ref
  31.4 3.5 %collective-permute-done.3.far_ref = bf16[512,256]{1,0:T(8,128)(2,1)S(1)} collective-permute-done((bf16[512,256]{1,0:T(8,128)(2,1)S(1)}, bf16[512,256]{1,0:T(8,128)(2,1)S(1)}, u32[]{:S(2)}, u32[]{:S(2)}) %collective-permute-start.3) | collective-permute-done | bytes 262176 | tf_op jit(solution)/shard_map/ppermute | solution.py:239
  34.9 1.8 %shard_map.103 = f32[8,8,4,8,256]{4,3,2,1,0:T(8,128)S(1)} custom-call(s32[4,1,128]{2,1,0:T(1,128)S(1)} %bitcast.38, f32[4,128,256]{2,1,0:T(8,128)S(1)} %shard_map.102.first_ref, bf16[4,512,128]{2,1,0:T(8,128)(2,1)S(1)} %all-to-all-done.cot_ref.here_ref, bf16[4,512,128]{2,1,0:T(8,128)(2,1)S(1)} %collective-permute-done.other_ref, ...), custom_call_target="tpu_custom_call" | custom-call | flops 671088640 | bytes 4194304 | tf_op jit(solution)/shard_map/pallas_call | solution.py:157
  36.8 0.3 convert_element_type.36
  37.0 19.3 %all_to_all.25 = f16[8,32,8,256]{3,2,1,0:T(8,128)(2,1)S(1)} all-to-all(f16[8,32,8,256]{3,2,1,0:T(8,128)(2,1)S(1)} %bitcast.40), channel_id=1, replica_groups=mesh['x'=4,'y'=8,'c'=2,'zh'=4,'zl'=2] {'x','c'}, dimensions={0} | all-to-all | bytes 2097152 | tf_op jit(solution)/shard_map/all_to_all | solution.py:259
  56.3 0.1 convert_reduce_fusion
  56.6 21.1 %all_to_all.26 = f16[32,2,8,256]{3,2,1,0:T(8,128)(2,1)S(1)} all-to-all(f16[32,2,8,256]{3,2,1,0:T(8,128)(2,1)S(1)} %copy.20), channel_id=1, replica_groups=mesh['x'=4,'y'=8,'c'=2,'zh'=4,'zl'=2] {'y','zh'}, dimensions={0} | all-to-all | bytes 524288 | tf_op jit(solution)/shard_map/all_to_all | solution.py:262
  77.8 0.1 reshape.205
  78.0 0.1 reduce_sum.69
  78.1 1.2 shard_map.104
  79.3 13.9 %all_to_all.27 = bf16[8,8,2048]{2,1,0:T(8,128)(2,1)S(1)} all-to-all(bf16[8,8,2048]{2,1,0:T(8,128)(2,1)S(1)} %broadcast_in_dim.115), channel_id=1, replica_groups=mesh['x'=4,'y'=8,'c'=2,'zh'=4,'zl'=2] {'y'}, dimensions={0} | all-to-all | bytes 524288 | tf_op jit(solution)/shard_map/all_to_all | solution.py:102
  93.3 0.1 broadcast_in_dim.116
  93.4 13.7 %all_to_all.28 = bf16[4,8,8,2048]{3,2,1,0:T(8,128)(2,1)S(1)} all-to-all(bf16[4,8,8,2048]{3,2,1,0:T(8,128)(2,1)S(1)} %broadcast_in_dim.116), channel_id=1, replica_groups=mesh['x'=4,'y'=8,'c'=2,'zh'=4,'zl'=2] {'x'}, dimensions={0} | all-to-all | bytes 2097152 | tf_op jit(solution)/shard_map/all_to_all | solution.py:102
  107.1 0.1 copy.22.target_ref
  107.2 6.6 %collective-permute-start.4 = (bf16[256,2048]{1,0:T(8,128)(2,1)S(1)}, bf16[256,2048]{1,0:T(8,128)(2,1)S(1)}, u32[]{:S(2)}, u32[]{:S(2)}) collective-permute-start(bf16[256,2048]{1,0:T(8,128)(2,1)S(1)} %bitcast.34), channel_id=1, source_target_pairs={{0,8},{8,0},{1,9},{9,1},{2,10},{10,2},{3,11},{11,3},{4,12},{12,4},... | collective-permute-start | bytes 3145736 | tf_op jit(solution)/shard_map/ppermute | solution.py:277
  113.9 0.1 reduce
  114.0 0.5 shard_map.105.placed_ref
  114.5 0.8 select_bitcast_fusion
  115.2 0.9 collective-permute-done.4.rows_ref
  116.1 1.3 %shard_map.106 = bf16[128,4096]{1,0:T(8,128)(2,1)} custom-call(s32[128,1]{1,0:T(8,128)S(1)} %copy.22.target_ref, s32[1,256]{1,0:T(1,128)S(1)} %get-tuple-element.31.key_ref, bf16[256,2048]{1,0:T(8,128)(2,1)S(1)} %collective-permute-done.4.rows_ref, bf16[128,4096]{1,0:T(8,128)(2,1)S(1)} %shard_map.105.placed_ref), custom_call_target="tpu_custom_call" | custom-call | flops 268435456 | bytes 2097152 | tf_op jit(solution)/shard_map/pallas_call | solution.py:203
  (27 shorter events, 0.3 us)
Async XLA Ops:
  0.6 14.3 %copy-start.3 = (bf16[512,512]{1,0:T(8,128)(2,1)S(1)}, bf16[512,512]{1,0:T(8,128)(2,1)}, u32[]{:S(2)}) copy-start(bf16[512,512]{1,0:T(8,128)(2,1)} %param.7) | copy-start | bytes 1572868
  2.5 23.0 %all-to-all-start = ((bf16[4,512,128]{2,1,0:T(8,128)(2,1)}), bf16[4,512,128]{2,1,0:T(8,128)(2,1)S(1)}, u32[]{:S(2)}, u32[]{:S(2)}) async-start(bf16[4,512,128]{2,1,0:T(8,128)(2,1)} %broadcast_in_dim.110), calls=%async_computation | async-start | bytes 1048576 | tf_op jit(solution)/shard_map/all_to_all | solution.py:102
  14.9 19.9 %collective-permute-start.3 = (bf16[512,256]{1,0:T(8,128)(2,1)S(1)}, bf16[512,256]{1,0:T(8,128)(2,1)S(1)}, u32[]{:S(2)}, u32[]{:S(2)}) collective-permute-start(bf16[512,256]{1,0:T(8,128)(2,1)S(1)} %get-tuple-element.40), channel_id=1, source_target_pairs={{0,9},{1,10},{2,11},{3,12},{4,13},{5,14},{6,15},{7,8},{8,7},{9,0},... | collective-permute-start | bytes 786440 | tf_op jit(solution)/shard_map/ppermute | solution.py:239
  21.6 13.3 %collective-permute-start.1 = (bf16[512,256]{1,0:T(8,128)(2,1)S(1)}, bf16[512,256]{1,0:T(8,128)(2,1)S(1)}, u32[]{:S(2)}, u32[]{:S(2)}) collective-permute-start(bf16[512,256]{1,0:T(8,128)(2,1)S(1)} %get-tuple-element.40), channel_id=1, source_target_pairs={{0,8},{8,0},{1,9},{9,1},{2,10},{10,2},{3,11},{11,3},{4,12},{12,4},... | collective-permute-start | bytes 786440 | tf_op jit(solution)/shard_map/ppermute | solution.py:239
  23.5 11.4 %collective-permute-start.2 = (bf16[512,256]{1,0:T(8,128)(2,1)S(1)}, bf16[512,256]{1,0:T(8,128)(2,1)S(1)}, u32[]{:S(2)}, u32[]{:S(2)}) collective-permute-start(bf16[512,256]{1,0:T(8,128)(2,1)S(1)} %get-tuple-element.41.act_ref), channel_id=1, source_target_pairs={{0,7},{1,0},{2,1},{3,2},{4,3},{5,4},{6,5},{7,6},{8,9},{9,10},{10,1... | collective-permute-start | bytes 786440 | tf_op jit(solution)/shard_map/ppermute | solution.py:238
  25.4 9.5 %collective-permute-start = (bf16[4,512,128]{2,1,0:T(8,128)(2,1)S(1)}, bf16[4,512,128]{2,1,0:T(8,128)(2,1)S(1)}, u32[]{:S(2)}, u32[]{:S(2)}) collective-permute-start(bf16[4,512,128]{2,1,0:T(8,128)(2,1)S(1)} %all-to-all-done.cot_ref.here_ref), channel_id=1, source_target_pairs={{0,8},{8,0},{1,9},{9,1},{2,10},{10,2},{3,11},{11,3},{4,12},{12,4},... | collective-permute-start | bytes 1572872 | tf_op jit(solution)/shard_map/ppermute | solution.py:240
  56.5 21.6 %copy-start = (f32[1,1,4,4096]{3,2,1,0:T(4,128)S(1)}, f32[1,1,4,4096]{3,2,1,0:T(4,128)}, u32[]{:S(2)}) copy-start(f32[1,1,4,4096]{3,2,1,0:T(4,128)} %param.11) | copy-start | bytes 196612
  56.5 21.6 %copy-start.1 = (f32[1,1,4,4096]{3,2,1,0:T(4,128)S(1)}, f32[1,1,4,4096]{3,2,1,0:T(4,128)}, u32[]{:S(2)}) copy-start(f32[1,1,4,4096]{3,2,1,0:T(4,128)} %param.13) | copy-start | bytes 196612
  56.5 21.6 %copy-start.2 = (f32[1,1,2]{2,1,0:T(1,128)S(1)}, f32[1,1,2]{2,1,0:T(1,128)}, u32[]{:S(2)}) copy-start(f32[1,1,2]{2,1,0:T(1,128)} %param.12) | copy-start | bytes 28
  107.2 8.9 %collective-permute-start.4 = (bf16[256,2048]{1,0:T(8,128)(2,1)S(1)}, bf16[256,2048]{1,0:T(8,128)(2,1)S(1)}, u32[]{:S(2)}, u32[]{:S(2)}) collective-permute-start(bf16[256,2048]{1,0:T(8,128)(2,1)S(1)} %bitcast.34), channel_id=1, source_target_pairs={{0,8},{8,0},{1,9},{9,1},{2,10},{10,2},{3,11},{11,3},{4,12},{12,4},... | collective-permute-start | bytes 3145736 | tf_op jit(solution)/shard_map/ppermute | solution.py:277

commit v12 on v11

--- a/solution.py
+++ b/solution.py
@@ -236,7 +236,9 @@
     same = [(c * depth + z, to_chip(c, z)) for c in range(nc) for z in range(depth)]
     cross = [(c * depth + z, to_chip(1 - c, z)) for c in range(nc) for z in range(depth)]
     act_here = (keep, lax.ppermute(keep, ("c", "zh", "zl"), same))
-    act_other = (lax.ppermute(give, "c", SWAP), lax.ppermute(give, ("c", "zh", "zl"), cross))
+    far = lax.ppermute(give, ("c", "zh", "zl"), cross)
+    cot_here, give = lax.optimization_barrier((cot_here, give))
+    act_other = (lax.ppermute(give, "c", SWAP), far)
     cot_other = lax.ppermute(cot_here, "c", SWAP)
 
     target_here = lax.dynamic_index_in_dim(target, pair, 0, keepdims=False)

time: 118 us -> 119 us (level)
  starting transfers between devices: 33.2 us -> 37.7 us
  blocking collectives: 68.1 us -> 65.7 us
    ppermute x1, starting transfers between devices: 5.32 us -> 9.3 us  [body(): cot_other = lax.ppermute(cot_here, 'c', SWAP)]
    ppermute x2, waiting for transfers between devices: 3.52 us -> 0.91 us  [the longest x1 0.9 us: body(): act_other = (lax.ppermute(give, 'c', SWAP), far)]
    all_to_all x1, blocking collectives: 21.1 us -> 18.6 us  [body(): lax.all_to_all(jnp.swapaxes(send, 0, 1), ('y', 'zh'), 0, 0, tiled=True)]
    all_to_all x1, waiting for transfers between devices: 0.01 us -> 1.66 us  [copies_to_all(): lax.all_to_all(jnp.broadcast_to(block[None], (count,) + block.shape), axi...]
  transfers between devices with their start and end apart: 6 -> 6, of which waited for: 2 -> 3; matrix products, arithmetic and copies ran while one was open for 2% -> 2% of each run, Pallas kernels for 1% -> 1%
where the time goes in v12:
time: 119 us
  blocking collectives  65.7 us (55%)
  starting transfers between devices  37.7 us (32%)
  Pallas kernels  5.14 us (4%)
  waiting for transfers between devices  3.46 us (3%)
  local copies, waits for them, and re-layouts  3.07 us (3%)
  other arithmetic  2.56 us (2%)
    all_to_all x2, blocking collectives, copies_to_all(): lax.all_to_all(jnp.broadcast_to(block[None], (count,) + block.shape), axi...  27.8 us
    all_to_all x1, blocking collectives, body(): got = lax.all_to_all(send, ('x', 'c'), 0, 0, tiled=True)  19.3 us
    all_to_all x1, blocking collectives, body(): lax.all_to_all(jnp.swapaxes(send, 0, 1), ('y', 'zh'), 0, 0, tiled=True)  18.6 us
    all_to_all x1, starting transfers between devices, copies_to_all(): lax.all_to_all(jnp.broadcast_to(block[None], (count,) + block.shape), axi...  10.8 us
    ppermute x1, starting transfers between devices, body(): cot_other = lax.ppermute(cot_here, 'c', SWAP)  9.3 us
    ppermute x1, starting transfers between devices, body(): low_other = lax.ppermute(low, 'c', SWAP)  6.55 us
    ppermute x1, starting transfers between devices, body(): far = lax.ppermute(give, ('c', 'zh', 'zl'), cross)  5.97 us
    ppermute x1, starting transfers between devices, body(): act_here = (keep, lax.ppermute(keep, ('c', 'zh', 'zl'), same))  3.1 us
  transfers between devices with their start and end apart: 6, of which 3 were waited for; matrix products, arithmetic and copies ran while one was open for 2% of the time, Pallas kernels for 1%

profile of v12, /device:TPU:1, one launch (start us, length us, event | category | flops | bytes accessed | tf_op | source)
XLA Modules:
  0.0 118.6 jit_solution(6846867374984853525)
XLA Ops:
  0.6 1.8 %broadcast_in_dim.110 = bf16[4,512,128]{2,1,0:T(8,128)(2,1)} broadcast(bf16[512,128]{1,0:T(8,128)(2,1)} %param.8), dimensions={1,2} | broadcast | bytes 655360 | tf_op jit(solution)/shard_map/broadcast_in_dim | solution.py:102
  2.5 10.8 %all-to-all-start = ((bf16[4,512,128]{2,1,0:T(8,128)(2,1)}), bf16[4,512,128]{2,1,0:T(8,128)(2,1)S(1)}, u32[]{:S(2)}, u32[]{:S(2)}) async-start(bf16[4,512,128]{2,1,0:T(8,128)(2,1)} %broadcast_in_dim.110), calls=%async_computation | async-start | bytes 1048576 | tf_op jit(solution)/shard_map/all_to_all | solution.py:102
  13.3 0.7 constant_dynamic-slice_fusion.4
  14.0 0.1 convert_reduce_fusion.3
  14.2 0.3 convert_reduce_fusion.2
  14.5 0.2 select_reduce_fusion
  14.6 0.2 convert_reduce_fusion.1
  14.9 3.1 %collective-permute-start.2 = (bf16[512,256]{1,0:T(8,128)(2,1)S(1)}, bf16[512,256]{1,0:T(8,128)(2,1)S(1)}, u32[]{:S(2)}, u32[]{:S(2)}) collective-permute-start(bf16[512,256]{1,0:T(8,128)(2,1)S(1)} %get-tuple-element.44.act_ref), channel_id=1, source_target_pairs={{0,7},{1,0},{2,1},{3,2},{4,3},{5,4},{6,5},{7,6},{8,9},{9,10},{10,1... | collective-permute-start | bytes 786440 | tf_op jit(solution)/shard_map/ppermute | solution.py:238
  18.1 6.0 %collective-permute-start.3 = (bf16[512,256]{1,0:T(8,128)(2,1)S(1)}, bf16[512,256]{1,0:T(8,128)(2,1)S(1)}, u32[]{:S(2)}, u32[]{:S(2)}) collective-permute-start(bf16[512,256]{1,0:T(8,128)(2,1)S(1)} %get-tuple-element.26), channel_id=1, source_target_pairs={{0,9},{1,10},{2,11},{3,12},{4,13},{5,14},{6,15},{7,8},{8,7},{9,0},... | collective-permute-start | bytes 786440 | tf_op jit(solution)/shard_map/ppermute | solution.py:239
  24.0 1.7 %all-to-all-done.cot_ref.here_ref = bf16[4,512,128]{2,1,0:T(8,128)(2,1)S(1)} async-done(((bf16[4,512,128]{2,1,0:T(8,128)(2,1)}), bf16[4,512,128]{2,1,0:T(8,128)(2,1)S(1)}, u32[]{:S(2)}, u32[]{:S(2)}) %all-to-all-start) | async-done | bytes 524320 | tf_op jit(solution)/shard_map/all_to_all | solution.py:102
  25.7 9.3 %collective-permute-start = (bf16[4,512,128]{2,1,0:T(8,128)(2,1)S(1)}, bf16[4,512,128]{2,1,0:T(8,128)(2,1)S(1)}, u32[]{:S(2)}, u32[]{:S(2)}) collective-permute-start(bf16[4,512,128]{2,1,0:T(8,128)(2,1)S(1)} %all-to-all-done.cot_ref.here_ref), channel_id=1, source_target_pairs={{0,8},{8,0},{1,9},{9,1},{2,10},{10,2},{3,11},{11,3},{4,12},{12,4},... | collective-permute-start | bytes 1572872 | tf_op jit(solution)/shard_map/ppermute | solution.py:242
  35.0 1.9 %collective-permute-start.1 = (bf16[512,256]{1,0:T(8,128)(2,1)S(1)}, bf16[512,256]{1,0:T(8,128)(2,1)S(1)}, u32[]{:S(2)}, u32[]{:S(2)}) collective-permute-start(bf16[512,256]{1,0:T(8,128)(2,1)S(1)} %get-tuple-element.26), channel_id=1, source_target_pairs={{0,8},{8,0},{1,9},{9,1},{2,10},{10,2},{3,11},{11,3},{4,12},{12,4},... | collective-permute-start | bytes 786440 | tf_op jit(solution)/shard_map/ppermute | solution.py:241
  37.0 0.2 select_reduce_fusion.2.rank_ref
  37.2 0.3 shard_map.102.first_ref
  37.6 0.9 collective-permute-done.1.own_ref
  38.5 1.9 %shard_map.103 = f32[8,8,4,8,256]{4,3,2,1,0:T(8,128)S(1)} custom-call(s32[4,1,128]{2,1,0:T(1,128)S(1)} %bitcast.38, f32[4,128,256]{2,1,0:T(8,128)S(1)} %shard_map.102.first_ref, bf16[4,512,128]{2,1,0:T(8,128)(2,1)S(1)} %all-to-all-done.cot_ref.here_ref, bf16[4,512,128]{2,1,0:T(8,128)(2,1)S(1)} %collective-permute-done.other_ref, ...), custom_call_target="tpu_custom_call" | custom-call | flops 671088640 | bytes 4194304 | tf_op jit(solution)/shard_map/pallas_call | solution.py:157
  40.3 0.3 convert_element_type.36
  40.6 19.3 %all_to_all.25 = f16[8,32,8,256]{3,2,1,0:T(8,128)(2,1)S(1)} all-to-all(f16[8,32,8,256]{3,2,1,0:T(8,128)(2,1)S(1)} %bitcast.40), channel_id=1, replica_groups=mesh['x'=4,'y'=8,'c'=2,'zh'=4,'zl'=2] {'x','c'}, dimensions={0} | all-to-all | bytes 2097152 | tf_op jit(solution)/shard_map/all_to_all | solution.py:261
  59.9 0.1 convert_reduce_fusion
  60.2 18.6 %all_to_all.26 = f16[32,2,8,256]{3,2,1,0:T(8,128)(2,1)S(1)} all-to-all(f16[32,2,8,256]{3,2,1,0:T(8,128)(2,1)S(1)} %copy.20), channel_id=1, replica_groups=mesh['x'=4,'y'=8,'c'=2,'zh'=4,'zl'=2] {'y','zh'}, dimensions={0} | all-to-all | bytes 524288 | tf_op jit(solution)/shard_map/all_to_all | solution.py:264
  78.9 0.1 reshape.205
  79.2 1.2 shard_map.104
  80.4 14.0 %all_to_all.27 = bf16[8,8,2048]{2,1,0:T(8,128)(2,1)S(1)} all-to-all(bf16[8,8,2048]{2,1,0:T(8,128)(2,1)S(1)} %broadcast_in_dim.115), channel_id=1, replica_groups=mesh['x'=4,'y'=8,'c'=2,'zh'=4,'zl'=2] {'y'}, dimensions={0} | all-to-all | bytes 524288 | tf_op jit(solution)/shard_map/all_to_all | solution.py:102
  94.4 0.1 broadcast_in_dim.116
  94.5 13.8 %all_to_all.28 = bf16[4,8,8,2048]{3,2,1,0:T(8,128)(2,1)S(1)} all-to-all(bf16[4,8,8,2048]{3,2,1,0:T(8,128)(2,1)S(1)} %broadcast_in_dim.116), channel_id=1, replica_groups=mesh['x'=4,'y'=8,'c'=2,'zh'=4,'zl'=2] {'x'}, dimensions={0} | all-to-all | bytes 2097152 | tf_op jit(solution)/shard_map/all_to_all | solution.py:102
  108.3 0.1 copy.22.target_ref
  108.4 6.6 %collective-permute-start.4 = (bf16[256,2048]{1,0:T(8,128)(2,1)S(1)}, bf16[256,2048]{1,0:T(8,128)(2,1)S(1)}, u32[]{:S(2)}, u32[]{:S(2)}) collective-permute-start(bf16[256,2048]{1,0:T(8,128)(2,1)S(1)} %bitcast.34), channel_id=1, source_target_pairs={{0,8},{8,0},{1,9},{9,1},{2,10},{10,2},{3,11},{11,3},{4,12},{12,4},... | collective-permute-start | bytes 3145736 | tf_op jit(solution)/shard_map/ppermute | solution.py:279
  115.0 0.1 reduce
  115.1 0.5 shard_map.105.placed_ref
  115.6 0.8 select_bitcast_fusion
  116.4 0.9 collective-permute-done.4.rows_ref
  117.3 1.3 %shard_map.106 = bf16[128,4096]{1,0:T(8,128)(2,1)} custom-call(s32[128,1]{1,0:T(8,128)S(1)} %copy.22.target_ref, s32[1,256]{1,0:T(1,128)S(1)} %get-tuple-element.35.key_ref, bf16[256,2048]{1,0:T(8,128)(2,1)S(1)} %collective-permute-done.4.rows_ref, bf16[128,4096]{1,0:T(8,128)(2,1)S(1)} %shard_map.105.placed_ref), custom_call_target="tpu_custom_call" | custom-call | flops 268435456 | bytes 2097152 | tf_op jit(solution)/shard_map/pallas_call | solution.py:203
  (27 shorter events, 0.4 us)
Async XLA Ops:
  0.6 14.3 %copy-start.3 = (bf16[512,512]{1,0:T(8,128)(2,1)S(1)}, bf16[512,512]{1,0:T(8,128)(2,1)}, u32[]{:S(2)}) copy-start(bf16[512,512]{1,0:T(8,128)(2,1)} %param.7) | copy-start | bytes 1572868
  2.5 23.2 %all-to-all-start = ((bf16[4,512,128]{2,1,0:T(8,128)(2,1)}), bf16[4,512,128]{2,1,0:T(8,128)(2,1)S(1)}, u32[]{:S(2)}, u32[]{:S(2)}) async-start(bf16[4,512,128]{2,1,0:T(8,128)(2,1)} %broadcast_in_dim.110), calls=%async_computation | async-start | bytes 1048576 | tf_op jit(solution)/shard_map/all_to_all | solution.py:102
  14.9 22.6 %collective-permute-start.2 = (bf16[512,256]{1,0:T(8,128)(2,1)S(1)}, bf16[512,256]{1,0:T(8,128)(2,1)S(1)}, u32[]{:S(2)}, u32[]{:S(2)}) collective-permute-start(bf16[512,256]{1,0:T(8,128)(2,1)S(1)} %get-tuple-element.44.act_ref), channel_id=1, source_target_pairs={{0,7},{1,0},{2,1},{3,2},{4,3},{5,4},{6,5},{7,6},{8,9},{9,10},{10,1... | collective-permute-start | bytes 786440 | tf_op jit(solution)/shard_map/ppermute | solution.py:238
  18.1 19.5 %collective-permute-start.3 = (bf16[512,256]{1,0:T(8,128)(2,1)S(1)}, bf16[512,256]{1,0:T(8,128)(2,1)S(1)}, u32[]{:S(2)}, u32[]{:S(2)}) collective-permute-start(bf16[512,256]{1,0:T(8,128)(2,1)S(1)} %get-tuple-element.26), channel_id=1, source_target_pairs={{0,9},{1,10},{2,11},{3,12},{4,13},{5,14},{6,15},{7,8},{8,7},{9,0},... | collective-permute-start | bytes 786440 | tf_op jit(solution)/shard_map/ppermute | solution.py:239
  25.7 12.8 %collective-permute-start = (bf16[4,512,128]{2,1,0:T(8,128)(2,1)S(1)}, bf16[4,512,128]{2,1,0:T(8,128)(2,1)S(1)}, u32[]{:S(2)}, u32[]{:S(2)}) collective-permute-start(bf16[4,512,128]{2,1,0:T(8,128)(2,1)S(1)} %all-to-all-done.cot_ref.here_ref), channel_id=1, source_target_pairs={{0,8},{8,0},{1,9},{9,1},{2,10},{10,2},{3,11},{11,3},{4,12},{12,4},... | collective-permute-start | bytes 1572872 | tf_op jit(solution)/shard_map/ppermute | solution.py:242
  35.0 3.4 %collective-permute-start.1 = (bf16[512,256]{1,0:T(8,128)(2,1)S(1)}, bf16[512,256]{1,0:T(8,128)(2,1)S(1)}, u32[]{:S(2)}, u32[]{:S(2)}) collective-permute-start(bf16[512,256]{1,0:T(8,128)(2,1)S(1)} %get-tuple-element.26), channel_id=1, source_target_pairs={{0,8},{8,0},{1,9},{9,1},{2,10},{10,2},{3,11},{11,3},{4,12},{12,4},... | collective-permute-start | bytes 786440 | tf_op jit(solution)/shard_map/ppermute | solution.py:241
  60.1 19.1 %copy-start = (f32[1,1,4,4096]{3,2,1,0:T(4,128)S(1)}, f32[1,1,4,4096]{3,2,1,0:T(4,128)}, u32[]{:S(2)}) copy-start(f32[1,1,4,4096]{3,2,1,0:T(4,128)} %param.11) | copy-start | bytes 196612
  60.1 19.1 %copy-start.1 = (f32[1,1,4,4096]{3,2,1,0:T(4,128)S(1)}, f32[1,1,4,4096]{3,2,1,0:T(4,128)}, u32[]{:S(2)}) copy-start(f32[1,1,4,4096]{3,2,1,0:T(4,128)} %param.13) | copy-start | bytes 196612
  60.1 19.1 %copy-start.2 = (f32[1,1,2]{2,1,0:T(1,128)S(1)}, f32[1,1,2]{2,1,0:T(1,128)}, u32[]{:S(2)}) copy-start(f32[1,1,2]{2,1,0:T(1,128)} %param.12) | copy-start | bytes 28
  108.4 8.8 %collective-permute-start.4 = (bf16[256,2048]{1,0:T(8,128)(2,1)S(1)}, bf16[256,2048]{1,0:T(8,128)(2,1)S(1)}, u32[]{:S(2)}, u32[]{:S(2)}) collective-permute-start(bf16[256,2048]{1,0:T(8,128)(2,1)S(1)} %bitcast.34), channel_id=1, source_target_pairs={{0,8},{8,0},{1,9},{9,1},{2,10},{10,2},{3,11},{11,3},{4,12},{12,4},... | collective-permute-start | bytes 3145736 | tf_op jit(solution)/shard_map/ppermute | solution.py:279

commit v13 on v11

--- a/solution.py
+++ b/solution.py
@@ -117,7 +117,7 @@
         )
 
 
-def padded_kernel(target_ref, first_ref, here_ref, other_ref, own_ref, near_ref, far_ref, out_ref):
+def padded_kernel(target_ref, first_ref, here_ref, other_ref, near_ref, far_ref, own_ref, out_ref):
     lines, spots, heads, rows, half = out_ref.shape
     count, cores, capacity = lines * spots * rows, GRID[2], rows // 2
     row = lax.broadcasted_iota(jnp.int32, (count, HD), 0)
@@ -161,7 +161,7 @@
         out_shape=jax.ShapeDtypeStruct((lines, spots, heads, 2 * capacity, half), jnp.float32),
         compiler_params=PARAMS,
         cost_estimate=cost(10 * heads * tokens * HD * half, 4 * 2**20),
-    )(target[:, None, :], first, cot_here, cot_other, act_other[0], act_here[1], act_other[1])
+    )(target[:, None, :], first, cot_here, cot_other, act_here[1], act_other[1], act_other[0])
 
 
 def placed_part(target_ref, key_ref, rows_ref, cut, span):

time: 118 us -> 118 us (level)
  no operation moved by 1% of the time
where the time goes in v13:
time: 118 us; the launch traced here: 117 us
  blocking collectives  68.1 us (58%)
  starting transfers between devices  33.3 us (28%)
  Pallas kernels  5.12 us (4%)
  waiting for transfers between devices  4.41 us (4%)
  local copies, waits for them, and re-layouts  3.07 us (3%)
  other arithmetic  2.56 us (2%)
    all_to_all x2, blocking collectives, copies_to_all(): lax.all_to_all(jnp.broadcast_to(block[None], (count,) + block.shape), axi...  27.7 us
    all_to_all x1, blocking collectives, body(): lax.all_to_all(jnp.swapaxes(send, 0, 1), ('y', 'zh'), 0, 0, tiled=True)  21.1 us
    all_to_all x1, blocking collectives, body(): got = lax.all_to_all(send, ('x', 'c'), 0, 0, tiled=True)  19.3 us
    all_to_all x1, starting transfers between devices, copies_to_all(): lax.all_to_all(jnp.broadcast_to(block[None], (count,) + block.shape), axi...  10.8 us
    ppermute x1, starting transfers between devices, body(): low_other = lax.ppermute(low, 'c', SWAP)  6.63 us
    ppermute x1, starting transfers between devices, body(): lax.ppermute(give, ('c', 'zh', 'zl'), cross)  5.67 us
    ppermute x1, starting transfers between devices, body(): cot_other = lax.ppermute(cot_here, 'c', SWAP)  5.32 us
    ppermute x1, waiting for transfers between devices, body(): lax.ppermute(give, ('c', 'zh', 'zl'), cross)  3.51 us
  transfers between devices with their start and end apart: 6, of which 2 were waited for; matrix products, arithmetic and copies ran while one was open for 2% of the time, Pallas kernels for 1%

profile of v13, /device:TPU:1, one launch (start us, length us, event | category | flops | bytes accessed | tf_op | source)
XLA Modules:
  0.0 117.4 jit_solution(13103033470029487873)
XLA Ops:
  0.6 1.8 %broadcast_in_dim.110 = bf16[4,512,128]{2,1,0:T(8,128)(2,1)} broadcast(bf16[512,128]{1,0:T(8,128)(2,1)} %param.8), dimensions={1,2} | broadcast | bytes 655360 | tf_op jit(solution)/shard_map/broadcast_in_dim | solution.py:102
  2.5 10.8 %all-to-all-start = ((bf16[4,512,128]{2,1,0:T(8,128)(2,1)}), bf16[4,512,128]{2,1,0:T(8,128)(2,1)S(1)}, u32[]{:S(2)}, u32[]{:S(2)}) async-start(bf16[4,512,128]{2,1,0:T(8,128)(2,1)} %broadcast_in_dim.110), calls=%async_computation | async-start | bytes 1048576 | tf_op jit(solution)/shard_map/all_to_all | solution.py:102
  13.3 0.7 constant_dynamic-slice_fusion.4
  14.0 0.1 convert_reduce_fusion.3
  14.2 0.3 convert_reduce_fusion.2
  14.5 0.2 select_reduce_fusion
  14.6 0.2 convert_reduce_fusion.1
  14.9 2.9 %collective-permute-start.3 = (bf16[512,256]{1,0:T(8,128)(2,1)S(1)}, bf16[512,256]{1,0:T(8,128)(2,1)S(1)}, u32[]{:S(2)}, u32[]{:S(2)}) collective-permute-start(bf16[512,256]{1,0:T(8,128)(2,1)S(1)} %get-tuple-element.40), channel_id=1, source_target_pairs={{0,8},{8,0},{1,9},{9,1},{2,10},{10,2},{3,11},{11,3},{4,12},{12,4},... | collective-permute-start | bytes 786440 | tf_op jit(solution)/shard_map/ppermute | solution.py:239
  17.8 5.7 %collective-permute-start.2 = (bf16[512,256]{1,0:T(8,128)(2,1)S(1)}, bf16[512,256]{1,0:T(8,128)(2,1)S(1)}, u32[]{:S(2)}, u32[]{:S(2)}) collective-permute-start(bf16[512,256]{1,0:T(8,128)(2,1)S(1)} %get-tuple-element.40), channel_id=1, source_target_pairs={{0,9},{1,10},{2,11},{3,12},{4,13},{5,14},{6,15},{7,8},{8,7},{9,0},... | collective-permute-start | bytes 786440 | tf_op jit(solution)/shard_map/ppermute | solution.py:239
  23.5 1.9 %collective-permute-start.1 = (bf16[512,256]{1,0:T(8,128)(2,1)S(1)}, bf16[512,256]{1,0:T(8,128)(2,1)S(1)}, u32[]{:S(2)}, u32[]{:S(2)}) collective-permute-start(bf16[512,256]{1,0:T(8,128)(2,1)S(1)} %get-tuple-element.41.act_ref), channel_id=1, source_target_pairs={{0,7},{1,0},{2,1},{3,2},{4,3},{5,4},{6,5},{7,6},{8,9},{9,10},{10,1... | collective-permute-start | bytes 786440 | tf_op jit(solution)/shard_map/ppermute | solution.py:238
  25.4 5.3 %collective-permute-start = (bf16[4,512,128]{2,1,0:T(8,128)(2,1)S(1)}, bf16[4,512,128]{2,1,0:T(8,128)(2,1)S(1)}, u32[]{:S(2)}, u32[]{:S(2)}) collective-permute-start(bf16[4,512,128]{2,1,0:T(8,128)(2,1)S(1)} %all-to-all-done.cot_ref.here_ref), channel_id=1, source_target_pairs={{0,8},{8,0},{1,9},{9,1},{2,10},{10,2},{3,11},{11,3},{4,12},{12,4},... | collective-permute-start | bytes 1572872 | tf_op jit(solution)/shard_map/ppermute | solution.py:240
  30.8 0.2 select_reduce_fusion.2.rank_ref
  31.0 0.3 shard_map.102.first_ref
  31.4 3.5 %collective-permute-done.2.far_ref = bf16[512,256]{1,0:T(8,128)(2,1)S(1)} collective-permute-done((bf16[512,256]{1,0:T(8,128)(2,1)S(1)}, bf16[512,256]{1,0:T(8,128)(2,1)S(1)}, u32[]{:S(2)}, u32[]{:S(2)}) %collective-permute-start.2) | collective-permute-done | bytes 262176 | tf_op jit(solution)/shard_map/ppermute | solution.py:239
  34.9 1.8 %shard_map.103 = f32[8,8,4,8,256]{4,3,2,1,0:T(8,128)S(1)} custom-call(s32[4,1,128]{2,1,0:T(1,128)S(1)} %bitcast.38, f32[4,128,256]{2,1,0:T(8,128)S(1)} %shard_map.102.first_ref, bf16[4,512,128]{2,1,0:T(8,128)(2,1)S(1)} %all-to-all-done.cot_ref.here_ref, bf16[4,512,128]{2,1,0:T(8,128)(2,1)S(1)} %collective-permute-done.other_ref, ...), custom_call_target="tpu_custom_call" | custom-call | flops 671088640 | bytes 4194304 | tf_op jit(solution)/shard_map/pallas_call | solution.py:157
  36.7 0.3 convert_element_type.36
  37.0 19.3 %all_to_all.25 = f16[8,32,8,256]{3,2,1,0:T(8,128)(2,1)S(1)} all-to-all(f16[8,32,8,256]{3,2,1,0:T(8,128)(2,1)S(1)} %bitcast.40), channel_id=1, replica_groups=mesh['x'=4,'y'=8,'c'=2,'zh'=4,'zl'=2] {'x','c'}, dimensions={0} | all-to-all | bytes 2097152 | tf_op jit(solution)/shard_map/all_to_all | solution.py:259
  56.3 0.1 convert_reduce_fusion
  56.6 21.1 %all_to_all.26 = f16[32,2,8,256]{3,2,1,0:T(8,128)(2,1)S(1)} all-to-all(f16[32,2,8,256]{3,2,1,0:T(8,128)(2,1)S(1)} %copy.20), channel_id=1, replica_groups=mesh['x'=4,'y'=8,'c'=2,'zh'=4,'zl'=2] {'y','zh'}, dimensions={0} | all-to-all | bytes 524288 | tf_op jit(solution)/shard_map/all_to_all | solution.py:262
  77.8 0.1 reshape.205
  78.0 0.1 reduce_sum.69
  78.1 1.2 shard_map.104
  79.3 13.9 %all_to_all.27 = bf16[8,8,2048]{2,1,0:T(8,128)(2,1)S(1)} all-to-all(bf16[8,8,2048]{2,1,0:T(8,128)(2,1)S(1)} %broadcast_in_dim.115), channel_id=1, replica_groups=mesh['x'=4,'y'=8,'c'=2,'zh'=4,'zl'=2] {'y'}, dimensions={0} | all-to-all | bytes 524288 | tf_op jit(solution)/shard_map/all_to_all | solution.py:102
  93.3 0.1 broadcast_in_dim.116
  93.4 13.7 %all_to_all.28 = bf16[4,8,8,2048]{3,2,1,0:T(8,128)(2,1)S(1)} all-to-all(bf16[4,8,8,2048]{3,2,1,0:T(8,128)(2,1)S(1)} %broadcast_in_dim.116), channel_id=1, replica_groups=mesh['x'=4,'y'=8,'c'=2,'zh'=4,'zl'=2] {'x'}, dimensions={0} | all-to-all | bytes 2097152 | tf_op jit(solution)/shard_map/all_to_all | solution.py:102
  107.1 0.1 copy.22.target_ref
  107.2 6.6 %collective-permute-start.4 = (bf16[256,2048]{1,0:T(8,128)(2,1)S(1)}, bf16[256,2048]{1,0:T(8,128)(2,1)S(1)}, u32[]{:S(2)}, u32[]{:S(2)}) collective-permute-start(bf16[256,2048]{1,0:T(8,128)(2,1)S(1)} %bitcast.34), channel_id=1, source_target_pairs={{0,8},{8,0},{1,9},{9,1},{2,10},{10,2},{3,11},{11,3},{4,12},{12,4},... | collective-permute-start | bytes 3145736 | tf_op jit(solution)/shard_map/ppermute | solution.py:277
  113.9 0.1 reduce
  114.0 0.5 shard_map.105.placed_ref
  114.5 0.8 select_bitcast_fusion
  115.2 0.9 collective-permute-done.4.rows_ref
  116.1 1.3 %shard_map.106 = bf16[128,4096]{1,0:T(8,128)(2,1)} custom-call(s32[128,1]{1,0:T(8,128)S(1)} %copy.22.target_ref, s32[1,256]{1,0:T(1,128)S(1)} %get-tuple-element.31.key_ref, bf16[256,2048]{1,0:T(8,128)(2,1)S(1)} %collective-permute-done.4.rows_ref, bf16[128,4096]{1,0:T(8,128)(2,1)S(1)} %shard_map.105.placed_ref), custom_call_target="tpu_custom_call" | custom-call | flops 268435456 | bytes 2097152 | tf_op jit(solution)/shard_map/pallas_call | solution.py:203
  (27 shorter events, 0.3 us)
Async XLA Ops:
  0.6 14.3 %copy-start.3 = (bf16[512,512]{1,0:T(8,128)(2,1)S(1)}, bf16[512,512]{1,0:T(8,128)(2,1)}, u32[]{:S(2)}) copy-start(bf16[512,512]{1,0:T(8,128)(2,1)} %param.7) | copy-start | bytes 1572868
  2.5 23.0 %all-to-all-start = ((bf16[4,512,128]{2,1,0:T(8,128)(2,1)}), bf16[4,512,128]{2,1,0:T(8,128)(2,1)S(1)}, u32[]{:S(2)}, u32[]{:S(2)}) async-start(bf16[4,512,128]{2,1,0:T(8,128)(2,1)} %broadcast_in_dim.110), calls=%async_computation | async-start | bytes 1048576 | tf_op jit(solution)/shard_map/all_to_all | solution.py:102
  14.9 16.4 %collective-permute-start.3 = (bf16[512,256]{1,0:T(8,128)(2,1)S(1)}, bf16[512,256]{1,0:T(8,128)(2,1)S(1)}, u32[]{:S(2)}, u32[]{:S(2)}) collective-permute-start(bf16[512,256]{1,0:T(8,128)(2,1)S(1)} %get-tuple-element.40), channel_id=1, source_target_pairs={{0,8},{8,0},{1,9},{9,1},{2,10},{10,2},{3,11},{11,3},{4,12},{12,4},... | collective-permute-start | bytes 786440 | tf_op jit(solution)/shard_map/ppermute | solution.py:239
  17.8 17.1 %collective-permute-start.2 = (bf16[512,256]{1,0:T(8,128)(2,1)S(1)}, bf16[512,256]{1,0:T(8,128)(2,1)S(1)}, u32[]{:S(2)}, u32[]{:S(2)}) collective-permute-start(bf16[512,256]{1,0:T(8,128)(2,1)S(1)} %get-tuple-element.40), channel_id=1, source_target_pairs={{0,9},{1,10},{2,11},{3,12},{4,13},{5,14},{6,15},{7,8},{8,7},{9,0},... | collective-permute-start | bytes 786440 | tf_op jit(solution)/shard_map/ppermute | solution.py:239
  23.5 11.4 %collective-permute-start.1 = (bf16[512,256]{1,0:T(8,128)(2,1)S(1)}, bf16[512,256]{1,0:T(8,128)(2,1)S(1)}, u32[]{:S(2)}, u32[]{:S(2)}) collective-permute-start(bf16[512,256]{1,0:T(8,128)(2,1)S(1)} %get-tuple-element.41.act_ref), channel_id=1, source_target_pairs={{0,7},{1,0},{2,1},{3,2},{4,3},{5,4},{6,5},{7,6},{8,9},{9,10},{10,1... | collective-permute-start | bytes 786440 | tf_op jit(solution)/shard_map/ppermute | solution.py:238
  25.4 9.5 %collective-permute-start = (bf16[4,512,128]{2,1,0:T(8,128)(2,1)S(1)}, bf16[4,512,128]{2,1,0:T(8,128)(2,1)S(1)}, u32[]{:S(2)}, u32[]{:S(2)}) collective-permute-start(bf16[4,512,128]{2,1,0:T(8,128)(2,1)S(1)} %all-to-all-done.cot_ref.here_ref), channel_id=1, source_target_pairs={{0,8},{8,0},{1,9},{9,1},{2,10},{10,2},{3,11},{11,3},{4,12},{12,4},... | collective-permute-start | bytes 1572872 | tf_op jit(solution)/shard_map/ppermute | solution.py:240
  56.5 21.6 %copy-start = (f32[1,1,4,4096]{3,2,1,0:T(4,128)S(1)}, f32[1,1,4,4096]{3,2,1,0:T(4,128)}, u32[]{:S(2)}) copy-start(f32[1,1,4,4096]{3,2,1,0:T(4,128)} %param.11) | copy-start | bytes 196612
  56.5 21.6 %copy-start.1 = (f32[1,1,4,4096]{3,2,1,0:T(4,128)S(1)}, f32[1,1,4,4096]{3,2,1,0:T(4,128)}, u32[]{:S(2)}) copy-start(f32[1,1,4,4096]{3,2,1,0:T(4,128)} %param.13) | copy-start | bytes 196612
  56.5 21.6 %copy-start.2 = (f32[1,1,2]{2,1,0:T(1,128)S(1)}, f32[1,1,2]{2,1,0:T(1,128)}, u32[]{:S(2)}) copy-start(f32[1,1,2]{2,1,0:T(1,128)} %param.12) | copy-start | bytes 28
  107.2 8.9 %collective-permute-start.4 = (bf16[256,2048]{1,0:T(8,128)(2,1)S(1)}, bf16[256,2048]{1,0:T(8,128)(2,1)S(1)}, u32[]{:S(2)}, u32[]{:S(2)}) collective-permute-start(bf16[256,2048]{1,0:T(8,128)(2,1)S(1)} %bitcast.34), channel_id=1, source_target_pairs={{0,8},{8,0},{1,9},{9,1},{2,10},{10,2},{3,11},{11,3},{4,12},{12,4},... | collective-permute-start | bytes 3145736 | tf_op jit(solution)/shard_map/ppermute | solution.py:277

commit v14 on v11

--- a/solution.py
+++ b/solution.py
@@ -194,7 +194,7 @@
 
 def place_rows(target, key, rows, *placed):
     count, piece = rows.shape
-    width, parts = CUT * piece, 2 * CUT
+    width, parts = CUT * piece, 4 * CUT
     vmem = pl.BlockSpec(memory_space=pltpu.VMEM)
     scratch = [
         pltpu.VMEM((parts, HD, width // parts), jnp.bfloat16),

time: 118 us -> 118 us (level)
  no operation moved by 1% of the time
where the time goes in v14:
time: 118 us; the launch traced here: 117 us
  blocking collectives  68.1 us (58%)
  starting transfers between devices  33.2 us (28%)
  Pallas kernels  5.13 us (4%)
  waiting for transfers between devices  4.42 us (4%)
  local copies, waits for them, and re-layouts  3.07 us (3%)
  other arithmetic  2.56 us (2%)
    all_to_all x2, blocking collectives, copies_to_all(): lax.all_to_all(jnp.broadcast_to(block[None], (count,) + block.shape), axi...  27.7 us
    all_to_all x1, blocking collectives, body(): lax.all_to_all(jnp.swapaxes(send, 0, 1), ('y', 'zh'), 0, 0, tiled=True)  21.1 us
    all_to_all x1, blocking collectives, body(): got = lax.all_to_all(send, ('x', 'c'), 0, 0, tiled=True)  19.3 us
    all_to_all x1, starting transfers between devices, copies_to_all(): lax.all_to_all(jnp.broadcast_to(block[None], (count,) + block.shape), axi...  10.8 us
    ppermute x1, starting transfers between devices, body(): low_other = lax.ppermute(low, 'c', SWAP)  6.63 us
    ppermute x1, starting transfers between devices, body(): lax.ppermute(give, ('c', 'zh', 'zl'), cross)  6.61 us
    ppermute x1, starting transfers between devices, body(): cot_other = lax.ppermute(cot_here, 'c', SWAP)  5.32 us
    ppermute x1, waiting for transfers between devices, body(): lax.ppermute(give, ('c', 'zh', 'zl'), cross)  3.52 us
  transfers between devices with their start and end apart: 6, of which 2 were waited for; matrix products, arithmetic and copies ran while one was open for 2% of the time, Pallas kernels for 1%

profile of v14, /device:TPU:1, one launch (start us, length us, event | category | flops | bytes accessed | tf_op | source)
XLA Modules:
  0.0 117.4 jit_solution(17776323030956575970)
XLA Ops:
  0.6 1.8 %broadcast_in_dim.110 = bf16[4,512,128]{2,1,0:T(8,128)(2,1)} broadcast(bf16[512,128]{1,0:T(8,128)(2,1)} %param.8), dimensions={1,2} | broadcast | bytes 655360 | tf_op jit(solution)/shard_map/broadcast_in_dim | solution.py:102
  2.5 10.8 %all-to-all-start = ((bf16[4,512,128]{2,1,0:T(8,128)(2,1)}), bf16[4,512,128]{2,1,0:T(8,128)(2,1)S(1)}, u32[]{:S(2)}, u32[]{:S(2)}) async-start(bf16[4,512,128]{2,1,0:T(8,128)(2,1)} %broadcast_in_dim.110), calls=%async_computation | async-start | bytes 1048576 | tf_op jit(solution)/shard_map/all_to_all | solution.py:102
  13.3 0.7 constant_dynamic-slice_fusion.4
  14.0 0.1 convert_reduce_fusion.3
  14.2 0.3 convert_reduce_fusion.2
  14.5 0.2 select_reduce_fusion
  14.6 0.2 convert_reduce_fusion.1
  14.9 6.6 %collective-permute-start.3 = (bf16[512,256]{1,0:T(8,128)(2,1)S(1)}, bf16[512,256]{1,0:T(8,128)(2,1)S(1)}, u32[]{:S(2)}, u32[]{:S(2)}) collective-permute-start(bf16[512,256]{1,0:T(8,128)(2,1)S(1)} %get-tuple-element.40), channel_id=1, source_target_pairs={{0,9},{1,10},{2,11},{3,12},{4,13},{5,14},{6,15},{7,8},{8,7},{9,0},... | collective-permute-start | bytes 786440 | tf_op jit(solution)/shard_map/ppermute | solution.py:239
  21.6 1.9 %collective-permute-start.1 = (bf16[512,256]{1,0:T(8,128)(2,1)S(1)}, bf16[512,256]{1,0:T(8,128)(2,1)S(1)}, u32[]{:S(2)}, u32[]{:S(2)}) collective-permute-start(bf16[512,256]{1,0:T(8,128)(2,1)S(1)} %get-tuple-element.40), channel_id=1, source_target_pairs={{0,8},{8,0},{1,9},{9,1},{2,10},{10,2},{3,11},{11,3},{4,12},{12,4},... | collective-permute-start | bytes 786440 | tf_op jit(solution)/shard_map/ppermute | solution.py:239
  23.5 1.9 %collective-permute-start.2 = (bf16[512,256]{1,0:T(8,128)(2,1)S(1)}, bf16[512,256]{1,0:T(8,128)(2,1)S(1)}, u32[]{:S(2)}, u32[]{:S(2)}) collective-permute-start(bf16[512,256]{1,0:T(8,128)(2,1)S(1)} %get-tuple-element.41.act_ref), channel_id=1, source_target_pairs={{0,7},{1,0},{2,1},{3,2},{4,3},{5,4},{6,5},{7,6},{8,9},{9,10},{10,1... | collective-permute-start | bytes 786440 | tf_op jit(solution)/shard_map/ppermute | solution.py:238
  25.4 5.3 %collective-permute-start = (bf16[4,512,128]{2,1,0:T(8,128)(2,1)S(1)}, bf16[4,512,128]{2,1,0:T(8,128)(2,1)S(1)}, u32[]{:S(2)}, u32[]{:S(2)}) collective-permute-start(bf16[4,512,128]{2,1,0:T(8,128)(2,1)S(1)} %all-to-all-done.cot_ref.here_ref), channel_id=1, source_target_pairs={{0,8},{8,0},{1,9},{9,1},{2,10},{10,2},{3,11},{11,3},{4,12},{12,4},... | collective-permute-start | bytes 1572872 | tf_op jit(solution)/shard_map/ppermute | solution.py:240
  30.8 0.2 select_reduce_fusion.2.rank_ref
  31.0 0.3 shard_map.102.first_ref
  31.4 3.5 %collective-permute-done.3.far_ref = bf16[512,256]{1,0:T(8,128)(2,1)S(1)} collective-permute-done((bf16[512,256]{1,0:T(8,128)(2,1)S(1)}, bf16[512,256]{1,0:T(8,128)(2,1)S(1)}, u32[]{:S(2)}, u32[]{:S(2)}) %collective-permute-start.3) | collective-permute-done | bytes 262176 | tf_op jit(solution)/shard_map/ppermute | solution.py:239
  34.9 1.8 %shard_map.103 = f32[8,8,4,8,256]{4,3,2,1,0:T(8,128)S(1)} custom-call(s32[4,1,128]{2,1,0:T(1,128)S(1)} %bitcast.38, f32[4,128,256]{2,1,0:T(8,128)S(1)} %shard_map.102.first_ref, bf16[4,512,128]{2,1,0:T(8,128)(2,1)S(1)} %all-to-all-done.cot_ref.here_ref, bf16[4,512,128]{2,1,0:T(8,128)(2,1)S(1)} %collective-permute-done.other_ref, ...), custom_call_target="tpu_custom_call" | custom-call | flops 671088640 | bytes 4194304 | tf_op jit(solution)/shard_map/pallas_call | solution.py:157
  36.8 0.3 convert_element_type.36
  37.0 19.3 %all_to_all.25 = f16[8,32,8,256]{3,2,1,0:T(8,128)(2,1)S(1)} all-to-all(f16[8,32,8,256]{3,2,1,0:T(8,128)(2,1)S(1)} %bitcast.40), channel_id=1, replica_groups=mesh['x'=4,'y'=8,'c'=2,'zh'=4,'zl'=2] {'x','c'}, dimensions={0} | all-to-all | bytes 2097152 | tf_op jit(solution)/shard_map/all_to_all | solution.py:259
  56.3 0.1 convert_reduce_fusion
  56.6 21.1 %all_to_all.26 = f16[32,2,8,256]{3,2,1,0:T(8,128)(2,1)S(1)} all-to-all(f16[32,2,8,256]{3,2,1,0:T(8,128)(2,1)S(1)} %copy.20), channel_id=1, replica_groups=mesh['x'=4,'y'=8,'c'=2,'zh'=4,'zl'=2] {'y','zh'}, dimensions={0} | all-to-all | bytes 524288 | tf_op jit(solution)/shard_map/all_to_all | solution.py:262
  77.8 0.1 reshape.205
  78.0 0.1 reduce_sum.69
  78.1 1.2 shard_map.104
  79.3 13.9 %all_to_all.27 = bf16[8,8,2048]{2,1,0:T(8,128)(2,1)S(1)} all-to-all(bf16[8,8,2048]{2,1,0:T(8,128)(2,1)S(1)} %broadcast_in_dim.115), channel_id=1, replica_groups=mesh['x'=4,'y'=8,'c'=2,'zh'=4,'zl'=2] {'y'}, dimensions={0} | all-to-all | bytes 524288 | tf_op jit(solution)/shard_map/all_to_all | solution.py:102
  93.3 0.1 broadcast_in_dim.116
  93.4 13.7 %all_to_all.28 = bf16[4,8,8,2048]{3,2,1,0:T(8,128)(2,1)S(1)} all-to-all(bf16[4,8,8,2048]{3,2,1,0:T(8,128)(2,1)S(1)} %broadcast_in_dim.116), channel_id=1, replica_groups=mesh['x'=4,'y'=8,'c'=2,'zh'=4,'zl'=2] {'x'}, dimensions={0} | all-to-all | bytes 2097152 | tf_op jit(solution)/shard_map/all_to_all | solution.py:102
  107.1 0.1 copy.22.target_ref
  107.2 6.6 %collective-permute-start.4 = (bf16[256,2048]{1,0:T(8,128)(2,1)S(1)}, bf16[256,2048]{1,0:T(8,128)(2,1)S(1)}, u32[]{:S(2)}, u32[]{:S(2)}) collective-permute-start(bf16[256,2048]{1,0:T(8,128)(2,1)S(1)} %bitcast.34), channel_id=1, source_target_pairs={{0,8},{8,0},{1,9},{9,1},{2,10},{10,2},{3,11},{11,3},{4,12},{12,4},... | collective-permute-start | bytes 3145736 | tf_op jit(solution)/shard_map/ppermute | solution.py:277
  113.9 0.1 reduce
  114.0 0.5 shard_map.105.placed_ref
  114.5 0.8 select_bitcast_fusion
  115.2 0.9 collective-permute-done.4.rows_ref
  116.1 1.3 %shard_map.106 = bf16[128,4096]{1,0:T(8,128)(2,1)} custom-call(s32[128,1]{1,0:T(8,128)S(1)} %copy.22.target_ref, s32[1,256]{1,0:T(1,128)S(1)} %get-tuple-element.31.key_ref, bf16[256,2048]{1,0:T(8,128)(2,1)S(1)} %collective-permute-done.4.rows_ref, bf16[128,4096]{1,0:T(8,128)(2,1)S(1)} %shard_map.105.placed_ref), custom_call_target="tpu_custom_call" | custom-call | flops 268435456 | bytes 2097152 | tf_op jit(solution)/shard_map/pallas_call | solution.py:203
  (27 shorter events, 0.3 us)
Async XLA Ops:
  0.6 14.3 %copy-start.3 = (bf16[512,512]{1,0:T(8,128)(2,1)S(1)}, bf16[512,512]{1,0:T(8,128)(2,1)}, u32[]{:S(2)}) copy-start(bf16[512,512]{1,0:T(8,128)(2,1)} %param.7) | copy-start | bytes 1572868
  2.5 23.0 %all-to-all-start = ((bf16[4,512,128]{2,1,0:T(8,128)(2,1)}), bf16[4,512,128]{2,1,0:T(8,128)(2,1)S(1)}, u32[]{:S(2)}, u32[]{:S(2)}) async-start(bf16[4,512,128]{2,1,0:T(8,128)(2,1)} %broadcast_in_dim.110), calls=%async_computation | async-start | bytes 1048576 | tf_op jit(solution)/shard_map/all_to_all | solution.py:102
  14.9 19.9 %collective-permute-start.3 = (bf16[512,256]{1,0:T(8,128)(2,1)S(1)}, bf16[512,256]{1,0:T(8,128)(2,1)S(1)}, u32[]{:S(2)}, u32[]{:S(2)}) collective-permute-start(bf16[512,256]{1,0:T(8,128)(2,1)S(1)} %get-tuple-element.40), channel_id=1, source_target_pairs={{0,9},{1,10},{2,11},{3,12},{4,13},{5,14},{6,15},{7,8},{8,7},{9,0},... | collective-permute-start | bytes 786440 | tf_op jit(solution)/shard_map/ppermute | solution.py:239
  21.6 13.3 %collective-permute-start.1 = (bf16[512,256]{1,0:T(8,128)(2,1)S(1)}, bf16[512,256]{1,0:T(8,128)(2,1)S(1)}, u32[]{:S(2)}, u32[]{:S(2)}) collective-permute-start(bf16[512,256]{1,0:T(8,128)(2,1)S(1)} %get-tuple-element.40), channel_id=1, source_target_pairs={{0,8},{8,0},{1,9},{9,1},{2,10},{10,2},{3,11},{11,3},{4,12},{12,4},... | collective-permute-start | bytes 786440 | tf_op jit(solution)/shard_map/ppermute | solution.py:239
  23.5 11.4 %collective-permute-start.2 = (bf16[512,256]{1,0:T(8,128)(2,1)S(1)}, bf16[512,256]{1,0:T(8,128)(2,1)S(1)}, u32[]{:S(2)}, u32[]{:S(2)}) collective-permute-start(bf16[512,256]{1,0:T(8,128)(2,1)S(1)} %get-tuple-element.41.act_ref), channel_id=1, source_target_pairs={{0,7},{1,0},{2,1},{3,2},{4,3},{5,4},{6,5},{7,6},{8,9},{9,10},{10,1... | collective-permute-start | bytes 786440 | tf_op jit(solution)/shard_map/ppermute | solution.py:238
  25.4 9.5 %collective-permute-start = (bf16[4,512,128]{2,1,0:T(8,128)(2,1)S(1)}, bf16[4,512,128]{2,1,0:T(8,128)(2,1)S(1)}, u32[]{:S(2)}, u32[]{:S(2)}) collective-permute-start(bf16[4,512,128]{2,1,0:T(8,128)(2,1)S(1)} %all-to-all-done.cot_ref.here_ref), channel_id=1, source_target_pairs={{0,8},{8,0},{1,9},{9,1},{2,10},{10,2},{3,11},{11,3},{4,12},{12,4},... | collective-permute-start | bytes 1572872 | tf_op jit(solution)/shard_map/ppermute | solution.py:240
  56.5 21.6 %copy-start = (f32[1,1,4,4096]{3,2,1,0:T(4,128)S(1)}, f32[1,1,4,4096]{3,2,1,0:T(4,128)}, u32[]{:S(2)}) copy-start(f32[1,1,4,4096]{3,2,1,0:T(4,128)} %param.11) | copy-start | bytes 196612
  56.5 21.6 %copy-start.1 = (f32[1,1,4,4096]{3,2,1,0:T(4,128)S(1)}, f32[1,1,4,4096]{3,2,1,0:T(4,128)}, u32[]{:S(2)}) copy-start(f32[1,1,4,4096]{3,2,1,0:T(4,128)} %param.13) | copy-start | bytes 196612
  56.5 21.6 %copy-start.2 = (f32[1,1,2]{2,1,0:T(1,128)S(1)}, f32[1,1,2]{2,1,0:T(1,128)}, u32[]{:S(2)}) copy-start(f32[1,1,2]{2,1,0:T(1,128)} %param.12) | copy-start | bytes 28
  107.2 8.9 %collective-permute-start.4 = (bf16[256,2048]{1,0:T(8,128)(2,1)S(1)}, bf16[256,2048]{1,0:T(8,128)(2,1)S(1)}, u32[]{:S(2)}, u32[]{:S(2)}) collective-permute-start(bf16[256,2048]{1,0:T(8,128)(2,1)S(1)} %bitcast.34), channel_id=1, source_target_pairs={{0,8},{8,0},{1,9},{9,1},{2,10},{10,2},{3,11},{11,3},{4,12},{12,4},... | collective-permute-start | bytes 3145736 | tf_op jit(solution)/shard_map/ppermute | solution.py:277
